TPU v7x, 32 devices: a whole 2x2x4 slice. The times are simulated.
32 devices in a mesh: prefix: 8 (over z, core), branch: 4 (over y, x).
Axes of the slice: x: 2, y: 2, z: 4, core: 2. Of those that a mesh axis runs over, the one named last changes fastest.
Arguments:
- hidden: bfloat16 [3, 32, 8192], P(None, 'branch', 'prefix'), may hold values from -4 to 4
- attn_gain: float32 [8192], P('prefix'), may hold values from 0.1 to 1.9
- ffn_gain: float32 [8192], P('prefix'), may hold values from 0.1 to 1.9
- w_qkv: bfloat16 [8192, 10240], P('prefix', 'branch'), may hold values from -0.0625 to 0.0625
- w_out: bfloat16 [8192, 8192], P('branch', 'prefix'), may hold values from -0.0625 to 0.0625
- w_gate_up: bfloat16 [2, 8192, 28672], P(None, 'prefix', 'branch'), may hold values from -0.0625 to 0.0625
- w_down: bfloat16 [28672, 8192], P('branch', 'prefix'), may hold values from -0.03125 to 0.03125
- tree_kv: bfloat16 [8, 2, 512, 1024], P('prefix'), may hold values from -64 to 64
- suffix_kv: bfloat16 [32, 2, 512, 1024], P('branch', None, 'prefix'), may hold values from -64 to 64
- parent: int32 [8], replicated, may hold values from -1 to 6, as said below
- block_map: int32 [8], replicated, may hold values from 0 to 7, each once
- leaf: int32 [32], P('branch'), may hold values from 0 to 7
- suffix_len: int32 [32], P('branch'), may hold values from 1 to 512, as said below
Outputs:
- out: bfloat16 [3, 32, 8192], P(None, 'branch', 'prefix')
- new_kv: bfloat16 [32, 2, 3, 1024], P('branch')
Inputs may be any that keep to these rules, and one draw needn't show every extreme that they name: Block 0 is the root with parent -1; every other block n has a parent below n; the last block's parent is block 6. `suffix_len`: some branch has exactly 512 used positions and some exactly 1.
All inputs are finite; a program needn't handle non-finite values.
Results may differ from a plain program's by a relative error of at most 0.01225.
The roundings to bfloat16 on the way count: a program that leaves them out, or rounds other values in their place, can miss the bound.
Values may be sent and summed in bfloat16 or wider, within the bound.
No kernel may reach another device: no remote copies, remote signals or barrier semaphores. Data moves between devices by JAX's collectives and lax.ppermute only.
A program may use at most 128 MiB of HBM per device.

v0:
```python
import jax
import jax.numpy as jnp
from jax import lax
from jax.sharding import PartitionSpec as P

HEADS = 64
KVH = 8
HD = 128
BLK = 512


EPS = 1e-05
ROPE_BASE = 500000.0
FLOOR = -1e30


def combined_all(part, axis, combine):
    gathered = jax.tree.map(lambda a: lax.all_gather(a, axis), part)

    def take(source):
        return jax.tree.map(lambda a: lax.dynamic_index_in_dim(a, source, 0, False), gathered)

    return lax.fori_loop(
        1, lax.axis_size(axis), lambda source, state: combine(state, take(source)), take(0)
    )


def rotate(values, position):
    half_dim = values.shape[-1] // 2
    frequency = ROPE_BASE ** (-(jnp.arange(half_dim, dtype=jnp.float32) * 2.0 / values.shape[-1]))
    angles = position.astype(jnp.float32)[..., None] * frequency
    cosine = jnp.cos(angles)
    sine_part = jnp.sin(angles)
    first_half = values[..., :half_dim]
    second_half = values[..., half_dim:]
    return jnp.concatenate(
        [
            first_half * cosine - second_half * sine_part,
            second_half * cosine + first_half * sine_part,
        ],
        axis=-1,
    )


def path_members(leaf, parent):
    node_ids = jnp.arange(parent.shape[0], dtype=jnp.int32)

    def climb_step(index, carry):
        current, member = carry
        hits = node_ids[None, :] == current[:, None]
        member = jnp.maximum(member, hits.astype(jnp.int32))
        upward = jnp.sum(jnp.where(hits, parent[None, :], 0), axis=1)
        current = jnp.where(current >= 0, upward, -1)
        return (current, member)

    start = (leaf, jnp.zeros((leaf.shape[0], parent.shape[0]), jnp.int32))
    return lax.fori_loop(0, parent.shape[0], climb_step, start)[1]


def partial_softmax(scores, allowed, values, form):
    masked = jnp.where(allowed, scores, FLOOR)
    highest = jnp.max(masked, axis=-1)
    weights = jnp.where(allowed, jnp.exp(masked - highest[..., None]), 0.0)
    return (
        highest,
        jnp.sum(weights, axis=-1),
        jnp.einsum(form, weights, values.astype(jnp.float32)),
    )


def combine(first_part, second_part):
    highest = jnp.maximum(first_part[0], second_part[0])
    first_scale = jnp.exp(first_part[0] - highest)
    second_scale = jnp.exp(second_part[0] - highest)
    totals = first_part[1] * first_scale + second_part[1] * second_scale
    weighted = first_part[2] * first_scale[..., None] + second_part[2] * second_scale[..., None]
    return (highest, totals, weighted)


def body(
    hidden,
    attn_gain,
    ffn_gain,
    w_qkv,
    w_out,
    w_gate_up,
    w_down,
    tree_kv,
    suffix_kv,
    parent,
    block_map,
    leaf,
    suffix_len,
):
    step_count, rows_dev, width_dev = hidden.shape
    prefix_count = lax.axis_size("prefix")
    width = width_dev * prefix_count
    every_row = lax.all_gather(hidden, "branch", axis=1, tiled=True)
    row_count = every_row.shape[1]
    row_float = every_row.astype(jnp.float32)
    squares = lax.psum(jnp.sum(row_float * row_float, axis=2), "prefix")
    normed = (row_float * lax.rsqrt(squares / width + EPS)[..., None] * attn_gain).astype(
        jnp.bfloat16
    )
    partial_sums = jnp.einsum("srd,dc->src", normed, w_qkv, preferred_element_type=jnp.float32)
    summed = lax.psum(partial_sums, "prefix").astype(jnp.bfloat16)
    projected = lax.all_to_all(summed, "branch", split_axis=1, concat_axis=2, tiled=True)
    q_width = HEADS * HD
    kv_width = KVH * HD
    queries = (
        projected[..., :q_width]
        .reshape(step_count, rows_dev, KVH, HEADS // KVH, HD)
        .astype(jnp.float32)
    )
    new_keys = (
        projected[..., q_width : q_width + kv_width]
        .reshape(step_count, rows_dev, KVH, HD)
        .astype(jnp.float32)
    )
    new_values = projected[..., q_width + kv_width :].reshape(step_count, rows_dev, KVH, HD)
    member = path_members(leaf, parent)
    path_depth = jnp.sum(member, axis=1)
    position = (
        BLK * path_depth[None, :]
        + suffix_len[None, :]
        + jnp.arange(step_count, dtype=jnp.int32)[:, None]
    )
    query_rot = rotate(queries, position[:, :, None, None]).astype(jnp.bfloat16)
    key_rot = rotate(new_keys, position[:, :, None]).astype(jnp.bfloat16)
    new_kv = jnp.stack(
        [
            key_rot.reshape(step_count, rows_dev, kv_width),
            new_values.reshape(step_count, rows_dev, kv_width),
        ],
        axis=0,
    ).transpose(2, 0, 1, 3)
    blocks_here = tree_kv.shape[0]
    slot_ids = lax.axis_index("prefix") * blocks_here + jnp.arange(blocks_here, dtype=jnp.int32)
    owned_slots = (block_map[:, None] == slot_ids[None, :]).astype(jnp.int32)
    slot_member = jnp.max(member[:, :, None] * owned_slots[None, :, :], axis=1) > 0
    tree_allowed = jnp.repeat(slot_member, tree_kv.shape[2], axis=1)
    tree_keys = tree_kv[:, 0].reshape(-1, KVH, HD)
    tree_values = tree_kv[:, 1].reshape(-1, KVH, HD)
    score_scale = HD ** (-0.5)
    tree_scores = (
        jnp.einsum("srkgh,nkh->srkgn", query_rot, tree_keys, preferred_element_type=jnp.float32)
        * score_scale
    )
    tree_part = partial_softmax(
        tree_scores, tree_allowed[None, :, None, None, :], tree_values, "srkgn,nkh->srkgh"
    )
    suffix_here = suffix_kv.shape[2]
    suffix_ids = lax.axis_index("prefix") * suffix_here + jnp.arange(suffix_here, dtype=jnp.int32)
    suffix_allowed = suffix_ids[None, :] < suffix_len[:, None]
    suffix_keys = suffix_kv[:, 0].reshape(rows_dev, suffix_here, KVH, HD)
    suffix_values = suffix_kv[:, 1].reshape(rows_dev, suffix_here, KVH, HD)
    suffix_scores = (
        jnp.einsum("srkgh,rnkh->srkgn", query_rot, suffix_keys, preferred_element_type=jnp.float32)
        * score_scale
    )
    suffix_part = partial_softmax(
        suffix_scores, suffix_allowed[None, :, None, None, :], suffix_values, "srkgn,rnkh->srkgh"
    )
    local_part = combine(tree_part, suffix_part)
    joined_part = combined_all(local_part, "prefix", combine)
    causal = jnp.arange(step_count)[None, :] <= jnp.arange(step_count)[:, None]
    new_scores = (
        jnp.einsum("srkgh,urkh->srkgu", query_rot, key_rot, preferred_element_type=jnp.float32)
        * score_scale
    )
    new_part = partial_softmax(
        new_scores, causal[:, None, None, None, :], new_values, "srkgu,urkh->srkgh"
    )
    final_part = combine(joined_part, new_part)
    attended = (
        (final_part[2] / final_part[1][..., None])
        .reshape(step_count, rows_dev, q_width)
        .astype(jnp.bfloat16)
    )
    head_rows = lax.all_to_all(attended, "branch", split_axis=2, concat_axis=1, tiled=True)
    mixed_part = jnp.einsum("srf,fd->srd", head_rows, w_out, preferred_element_type=jnp.float32)
    mixed_out = lax.psum(mixed_part, "branch")
    residual = (row_float + mixed_out).astype(jnp.bfloat16)
    res_float = residual.astype(jnp.float32)
    squares_two = lax.psum(jnp.sum(res_float * res_float, axis=2), "prefix")
    normed2 = (res_float * lax.rsqrt(squares_two / width + EPS)[..., None] * ffn_gain).astype(
        jnp.bfloat16
    )
    flat_rows = normed2.reshape(step_count * row_count, width_dev)
    gate_whole = lax.psum(
        jnp.einsum("rd,gdf->rgf", flat_rows, w_gate_up, preferred_element_type=jnp.float32),
        "prefix",
    )
    activation = (jax.nn.silu(gate_whole[:, 0]) * gate_whole[:, 1]).astype(jnp.bfloat16)
    act_steps = activation.reshape(step_count, row_count, activation.shape[-1])
    down_part = lax.psum_scatter(
        jnp.einsum("srf,fd->rsd", act_steps, w_down, preferred_element_type=jnp.float32),
        "branch",
        scatter_dimension=0,
        tiled=True,
    )
    own_rows = lax.dynamic_slice_in_dim(res_float, lax.axis_index("branch") * rows_dev, rows_dev, 1)
    result_rows = (own_rows + down_part.transpose(1, 0, 2)).astype(jnp.bfloat16)
    return (result_rows, new_kv)


def solution(mesh):
    placed = (
        P(None, "branch", "prefix"),
        P("prefix"),
        P("prefix"),
        P("prefix", "branch"),
        P("branch", "prefix"),
        P(None, "prefix", "branch"),
        P("branch", "prefix"),
        P("prefix", None, None, None),
        P("branch", None, "prefix", None),
        P(),
        P(),
        P("branch"),
        P("branch"),
    )
    return jax.shard_map(
        body,
        mesh=mesh,
        in_specs=placed,
        out_specs=(P(None, "branch", "prefix"), P("branch", None, None, None)),
        check_vma=False,
    )
```

profile of v0, /device:TPU:0, one launch (start us, length us, event | category | flops | bytes accessed | tf_op | source)
XLA Modules:
  0.0 476.6 jit_solution(1984361198519370911)
XLA Ops:
  7.2 10.4 %all_gather.17 = bf16[3,32,1024]{2,1,0:T(8,128)(2,1)S(1)} all-gather(bf16[3,8,1024]{2,1,0:T(8,128)(2,1)} %param.17), channel_id=1, replica_groups=mesh['prefix'=8,'branch'=4] {'branch'}, dimensions={1}, use_global_device_ids=true | all-gather | bytes 245760 | tf_op jit(solution)/shard_map/all_gather | solution.py:98
  17.7 14.9 %psum.35 = f32[3,32]{1,0:T(4,128)S(1)} all-reduce(f32[3,32]{1,0:T(4,128)S(1)} %fusion.50), channel_id=1, replica_groups=mesh['prefix'=8,'branch'=4] {'prefix'}, use_global_device_ids=true, to_apply=%region_5.6 | all-reduce | flops 96 | bytes 768 | tf_op jit(solution)/shard_map/psum | solution.py:101
  32.6 3.5 fusion.12
  36.2 36.6 %all-reduce.7 = bf16[3,32,2560]{2,1,0:T(8,128)(2,1)S(1)} all-reduce(f32[3,32,2560]{2,1,0:T(8,128)S(1)} %fusion.12), channel_id=1, replica_groups=mesh['prefix'=8,'branch'=4] {'prefix'}, use_global_device_ids=true, to_apply=%region_6.7 | all-reduce | flops 245760 | bytes 1474560 | tf_op jit(solution)/shard_map/psum | solution.py:106
  72.8 1.2 copy.126
  74.1 4.2 all-to-all-start
  78.4 1.6 while.33
  78.4 0.2 fusion.106
  78.6 0.2 fusion.106
  79.4 0.2 fusion.106
  80.3 1.7 fusion.90
  82.0 1.8 fusion.89
  83.8 0.3 copy.191
  84.1 1.1 bitcast_bitcast_fusion
  85.2 0.6 broadcast_compare_fusion.1
  85.8 1.3 copy.186
  87.2 1.3 copy.185
  88.5 0.3 copy.190
  88.8 1.6 copy.253
  90.4 0.4 all_to_all.29
  91.0 0.3 fusion.91
  91.3 0.2 subtract_convert_fusion
  91.5 0.2 pad_maximum_fusion
  91.8 0.8 fusion.93
  92.6 1.2 fusion.87
  93.8 0.7 bitcast_reduce_fusion
  94.6 1.1 fusion.38
  95.8 1.3 fusion.35
  97.3 0.8 copy.147
  98.1 1.5 slice_bitcast_fusion.2
  99.5 0.6 copy.255
  100.2 1.8 fusion.20
  102.3 18.6 %all_gather.18 = f32[8,3,8,8,8]{4,3,2,1,0:T(8,128)S(1)} all-gather(f32[1,3,8,8,8]{4,3,2,1,0:T(8,128)S(1)} %copy.135), channel_id=1, replica_groups=mesh['prefix'=8,'branch'=4] {'prefix'}, dimensions={0}, use_global_device_ids=true | all-gather | bytes 55296 | tf_op jit(solution)/shard_map/all_gather | solution.py:18
  120.9 19.1 %all_gather.19 = f32[8,3,8,8,8]{4,3,2,1,0:T(8,128)S(1)} all-gather(f32[1,3,8,8,8]{4,3,2,1,0:T(8,128)S(1)} %copy.137), channel_id=1, replica_groups=mesh['prefix'=8,'branch'=4] {'prefix'}, dimensions={0}, use_global_device_ids=true | all-gather | bytes 55296 | tf_op jit(solution)/shard_map/all_gather | solution.py:18
  140.3 1.4 fusion.94
  141.8 0.4 fusion.57
  142.2 0.3 copy-done.11
  142.5 28.5 %all-gather.3.cloned.1.call-done = f32[24,8,8,8,128]{4,3,1,0,2:T(8,128)} async-done(((f32[3,8,8,8,128]{4,3,1,0,2:T(8,128)}), f32[24,8,8,8,128]{4,3,1,0,2:T(8,128)}) %all-gather.3.cloned.1.call-update) | async-done | bytes 6291472 | tf_op jit(solution)/shard_map/all_gather | solution.py:18
  171.0 1.2 slice.59
  172.3 12.5 %while.32 = (s32[]{:T(128)}, f32[3,8,8,8]{3,2,1,0:T(8,128)S(1)}, f32[3,8,8,8]{3,2,1,0:T(8,128)S(1)}, f32[3,8,8,8,128]{4,3,2,1,0:T(8,128)S(1)}, f32[8,3,8,8,8]{4,...) while((s32[]{:T(128)}, f32[3,8,8,8]{3,2,1,0:T(8,128)S(1)}, ...), condition=%wide.region_13.14_spmd, body=%wide.region_12.13_spmd.sunk | while | flops 599045 | bytes 2420879 | solution.py:23
  172.5 1.7 fusion.105
  174.2 1.7 fusion.105
  176.0 1.7 fusion.105
  177.8 1.7 fusion.105
  179.6 1.7 fusion.105
  181.4 1.7 fusion.105
  183.2 1.7 fusion.105
  185.2 1.2 fusion.41
  186.4 6.4 %copy.180 = bf16[3,8,8,8,128]{1,0,4,3,2:T(4,128)(2,1)} copy(bf16[3,8,8,8,128]{4,3,0,2,1:T(8,128)(2,1)S(1)} %fusion.41) | data formatting | bytes 786432 | tf_op jit(solution)/shard_map/convert_element_type | solution.py:178
  192.8 9.3 %reshape.262 = bf16[4,2,24576]{2,1,0:T(2,128)(2,1)S(1)} reshape(bf16[8192,3,8]{2,1,0:T(4,128)(2,1)} %bitcast.197) | data formatting | bytes 786432
  202.1 11.0 %all_to_all.36 = bf16[4,2,24576]{2,1,0:T(2,128)(2,1)S(1)} all-to-all(bf16[4,2,24576]{2,1,0:T(2,128)(2,1)S(1)} %reshape.262), channel_id=1, replica_groups=mesh['prefix'=8,'branch'=4] {'branch'}, dimensions={0} | all-to-all | bytes 786432 | tf_op jit(solution)/shard_map/all_to_all | solution.py:180
  213.1 9.3 %reshape.263 = bf16[8192,3,8]{2,1,0:T(4,128)(2,1)} reshape(bf16[4,2,24576]{2,1,0:T(2,128)(2,1)S(1)} %all_to_all.36) | data formatting | bytes 786432
  222.4 10.4 %copy.161 = bf16[3,8,4,2048]{3,1,2,0:T(8,128)(2,1)S(1)} copy(bf16[3,8,4,2048]{1,0,3,2:T(4,128)(2,1)} %bitcast.198) | data formatting | bytes 786432 | tf_op jit(solution)/shard_map/all_to_all | solution.py:180
  232.8 3.8 fusion.14
  236.7 42.8 %all-reduce.4.cloned.1.call-done = f32[3,32,1024]{2,1,0:T(8,128)} async-done(((f32[3,32,1024]{2,1,0:T(8,128)}), f32[3,32,1024]{2,1,0:T(8,128)}) %all-reduce.4.cloned.1.call-update) | async-done | bytes 393232 | tf_op jit(solution)/shard_map/psum | solution.py:182
  279.5 1.1 multiply_reduce_fusion
  280.6 16.1 %psum.38 = f32[3,32]{1,0:T(4,128)S(1)} all-reduce(f32[3,32]{1,0:T(4,128)S(1)} %get-tuple-element.299), channel_id=1, replica_groups=mesh['prefix'=8,'branch'=4] {'prefix'}, use_global_device_ids=true, to_apply=%region_18.19 | all-reduce | flops 96 | bytes 768 | tf_op jit(solution)/shard_map/psum | solution.py:185
  296.9 16.6 %fusion.95 = f32[96,2,7168]{2,0,1:T(8,128)} fusion(bf16[96,1024,1]{1,0,2:T(8,128)(2,1)S(1)} %bitcast.210, bf16[2,1024,7168]{2,1,0:T(8,128)(2,1)} %param.22), kind=kOutput, calls=%fused_computation.151 | convolution fusion | flops 2818572288 | bytes 35061760 | tf_op jit(solution)/shard_map/rd,gdf->rgf/dot_general | solution.py:191
  313.5 118.5 %all-reduce.6.cloned.1.call-done = f32[96,2,7168]{2,0,1:T(8,128)} async-done(((f32[96,2,7168]{2,0,1:T(8,128)}), f32[96,2,7168]{2,0,1:T(8,128)}) %all-reduce.6.cloned.1.call-update) | async-done | bytes 5505040 | tf_op jit(solution)/shard_map/psum | solution.py:190
  432.0 3.1 fusion.88
  435.2 8.6 %fusion.44 = f32[32,3,1024]{2,0,1:T(8,128)} fusion(bf16[7168,1024]{1,0:T(8,128)(2,1)} %param.23, f32[3,32,7168]{2,1,0:T(8,128)S(1)} %bitcast.207, f32[3,32,7168]{2,1,0:T(8,128)S(1)} %bitcast.206), kind=kOutput, calls=%fused_computation.54 | convolution fusion | flops 1413414912 | bytes 20578304 | tf_op jit(solution)/shard_map/srf,fd->rsd/dot_general | solution.py:197
  444.0 0.7 copy.163
  444.7 23.8 %reduce-scatter.2.cloned.1.call-done = f32[8,3,1024]{2,0,1:T(8,128)} async-done(((f32[32,3,1024]{2,0,1:T(8,128)}), f32[8,3,1024]{2,0,1:T(8,128)}) %reduce-scatter.2.cloned.1.call-update) | async-done | bytes 98320 | tf_op jit(solution)/shard_map/reduce_scatter | solution.py:196
  468.5 1.5 fusion.71
  (114 shorter events, 4.0 us)
Async XLA Ops:
  17.6 18.6 %copy-start.2 = (bf16[3,32,1024]{2,1,0:T(8,128)(2,1)}, bf16[3,32,1024]{2,1,0:T(8,128)(2,1)S(1)}, u32[]{:S(2)}) copy-start(bf16[3,32,1024]{2,1,0:T(8,128)(2,1)S(1)} %all_gather.17) | copy-start | bytes 589828
  36.1 42.2 %copy-start.24 = (s32[8]{0:T(128)S(1)}, s32[8]{0:T(128)}, u32[]{:S(2)}) copy-start(s32[8]{0:T(128)} %param.27) | copy-start | bytes 100
  36.2 42.2 %copy-start.18 = (s32[8]{0:T(128)S(1)}, s32[8]{0:T(128)}, u32[]{:S(2)}) copy-start(s32[8]{0:T(128)} %param.26) | copy-start | bytes 100
  36.2 42.2 %copy-start.19 = (s32[8]{0:T(128)S(1)}, s32[8]{0:T(128)}, u32[]{:S(2)}) copy-start(s32[8]{0:T(128)} %param.28) | copy-start | bytes 100
  36.2 43.9 %copy-start.23 = (s32[8]{0:T(128)S(1)}, s32[8]{0:T(128)}, u32[]{:S(2)}) copy-start(s32[8]{0:T(128)} %param.29) | copy-start | bytes 100
  74.1 14.8 %all-to-all-start = ((bf16[3,32,2560]{2,0,1:T(4,128)(2,1)}), bf16[3,32,2560]{2,0,1:T(4,128)(2,1)}, u32[]{:S(2)}, u32[]{:S(2)}) async-start(bf16[3,32,2560]{2,0,1:T(4,128)(2,1)} %copy.126), calls=%async_computation | async-start | bytes 1310720 | tf_op jit(solution)/shard_map/all_to_all | solution.py:107
  78.2 92.8 %all-gather.3.cloned.1.call-start = ((), (), s32[]{:S(2)}) async-start(), calls=%async_computation.6 | async-start | bytes 7077888 | tf_op jit(solution)/shard_map/all_gather | solution.py:18
  85.2 6.0 %copy-start.16 = (f32[3,8,64]{2,1,0:T(8,128)}, f32[3,8,64]{2,1,0:T(8,128)S(1)}, u32[]{:S(2)}) copy-start(f32[3,8,64]{2,1,0:T(8,128)S(1)} %get-tuple-element.329) | copy-start | bytes 18436
  90.8 0.8 copy-start.6
  91.3 2.5 copy-start.1
  91.3 2.5 copy-start.20
  92.6 2.0 copy-start.4
  92.6 2.0 copy-start.9
  94.5 1.2 copy-start.7
  94.6 1.2 copy-start
  95.7 4.5 copy-start.21
  97.2 182.3 %all-reduce.4.cloned.1.call-start = ((), (), s32[]{:S(2)}) async-start(), calls=%async_computation.3 | async-start | bytes 786432 | tf_op jit(solution)/shard_map/psum | solution.py:182
  97.3 4.8 %copy-start.5 = (f32[3,8,8,8]{3,0,2,1:T(4,128)S(1)}, f32[3,8,8,8]{3,0,2,1:T(4,128)}, u32[]{:S(2)}) copy-start(f32[3,8,8,8]{3,0,2,1:T(4,128)} %copy-done.4) | copy-start | bytes 18436
  97.3 4.8 %copy-start.8 = (f32[3,8,8,8]{3,1,0,2:T(8,128)S(1)}, f32[3,8,8,8]{3,1,0,2:T(8,128)}, u32[]{:S(2)}) copy-start(f32[3,8,8,8]{3,1,0,2:T(8,128)} %copy-done.7) | copy-start | bytes 18436
  97.3 4.8 %copy-start.10 = (f32[3,8,8,8]{3,0,2,1:T(4,128)S(1)}, f32[3,8,8,8]{3,0,2,1:T(4,128)}, u32[]{:S(2)}) copy-start(f32[3,8,8,8]{3,0,2,1:T(4,128)} %get-tuple-element.304) | copy-start | bytes 18436
  140.3 1.4 copy-start.13
  141.7 0.7 copy-start.11
  172.3 12.8 %copy-start.12 = (f32[3,8,8,8,3]{3,4,0,2,1:T(4,128)S(1)}, f32[3,8,8,8,3]{3,4,0,2,1:T(4,128)}, u32[]{:S(2)}) copy-start(f32[3,8,8,8,3]{3,4,0,2,1:T(4,128)} %copy-done.11) | copy-start | bytes 55300
  172.3 12.8 %copy-start.17 = (bf16[3,8,8,128]{3,2,1,0:T(8,128)(2,1)S(1)}, bf16[3,8,8,128]{3,2,1,0:T(8,128)(2,1)}, u32[]{:S(2)}) copy-start(bf16[3,8,8,128]{3,2,1,0:T(8,128)(2,1)} %copy.255) | copy-start | bytes 147460
  232.8 46.7 %copy-start.3 = (bf16[3,32,1024]{2,1,0:T(8,128)(2,1)S(1)}, bf16[3,32,1024]{2,1,0:T(8,128)(2,1)}, u32[]{:S(2)}) copy-start(bf16[3,32,1024]{2,1,0:T(8,128)(2,1)} %copy-done.2) | copy-start | bytes 589828
  232.8 63.9 %copy-start.22 = (f32[1024]{0:T(1024)S(1)}, f32[1024]{0:T(1024)}, u32[]{:S(2)}) copy-start(f32[1024]{0:T(1024)} %param.19) | copy-start | bytes 12292
  236.6 195.4 %all-reduce.6.cloned.1.call-start = ((), (), s32[]{:S(2)}) async-start(), calls=%async_computation.4 | async-start | bytes 11010048 | tf_op jit(solution)/shard_map/psum | solution.py:190
  313.5 155.1 %reduce-scatter.2.cloned.1.call-start = ((), (), s32[]{:S(2)}) async-start(), calls=%async_computation.5 | async-start | bytes 491520 | tf_op jit(solution)/shard_map/reduce_scatter | solution.py:196
  435.2 8.7 %copy-start.14 = (bf16[3,8,8,128]{3,0,2,1:T(4,128)(2,1)S(1)}, bf16[3,8,8,128]{3,0,2,1:T(4,128)(2,1)}, u32[]{:S(2)}) copy-start(bf16[3,8,8,128]{3,0,2,1:T(4,128)(2,1)} %copy-done.13) | copy-start | bytes 147460
  435.2 8.7 %copy-start.15 = (bf16[1,3,8,1024]{3,2,1,0:T(8,128)(2,1)S(1)}, bf16[1,3,8,1024]{3,2,1,0:T(8,128)(2,1)}, u32[]{:S(2)}) copy-start(bf16[1,3,8,1024]{3,2,1,0:T(8,128)(2,1)} %get-tuple-element.318) | copy-start | bytes 147460
Sparse Core Ops, SparseCore 0:
  97.3 73.6 all-gather.2
  236.8 42.6 all-reduce.3
  313.6 118.4 all-reduce.5
  444.0 24.4 reduce-scatter.1
where the time goes:
time: 478 us; the launch traced here: 477 us
  waiting for transfers between devices  214 us (45%)
  blocking collectives  127 us (27%)
  local copies, waits for them, and re-layouts  54.2 us (11%)
  matrix products  39 us (8%)
  other arithmetic  23.7 us (5%)
  between operations  14.4 us (3%)
    psum x1, waiting for transfers between devices, body(): lax.psum(jnp.einsum('rd,gdf->rgf', flat_rows, w_gate_up, preferred_elemen...  119 us
    psum x1, waiting for transfers between devices, body(): mixed_out = lax.psum(mixed_part, 'branch')  42.8 us
    all_gather x2, blocking collectives, combined_all(): gathered = jax.tree.map(lambda a: lax.all_gather(a, axis), part)  37.7 us
    psum x1, blocking collectives, body(): summed = lax.psum(partial_sums, 'prefix').astype(jnp.bfloat16)  36.6 us
    all_gather x1, waiting for transfers between devices, combined_all(): gathered = jax.tree.map(lambda a: lax.all_gather(a, axis), part)  28.5 us
    unnamed x60, local copies, waits for them, and re-layouts  23.9 us
    reduce_scatter x1, waiting for transfers between devices, body(): lax.psum_scatter(jnp.einsum('srf,fd->rsd', act_steps, w_down, preferred_e...  23.8 us
    dot_general x1, matrix products, body(): jnp.einsum('rd,gdf->rgf', flat_rows, w_gate_up, preferred_element_type=jn...  16.6 us
  transfers between devices with their start and end apart: 5, of which 4 were waited for; matrix products, arithmetic and copies ran while one was open for 4% of the time, Pallas kernels for 0%

commit v1 on v0

v1 whole, which is shorter than its diff:
```python
import functools

import jax
import jax.numpy as jnp
from jax import lax
from jax.experimental import pallas as pl
from jax.experimental.pallas import tpu as pltpu
from jax.sharding import Mesh
from jax.sharding import PartitionSpec as P

HEADS = 64
KVH = 8
HD = 128
GROUP = HEADS // KVH
BLK = 512
CORES = 2
SUB = 8
LANE = 128

EPS = 1e-05
ROPE_BASE = 500000.0
FLOOR = -1e30
LOWEST = -1e29
F32 = jnp.float32
BF16 = jnp.bfloat16
EVERY = ("z", "core", "branch")


def ceil_div(a, b):
    return -(-a // b)


def whole(shape):
    return pl.BlockSpec(shape, lambda *_: (0,) * len(shape))


def params(mib):
    return pltpu.CompilerParams(vmem_limit_bytes=mib * 2**20)


def swap(x, axis, n, k):
    return lax.ppermute(x, axis, [(i, i ^ k) for i in range(n)])


def exchange(x, axes):
    return lax.all_to_all(x, axes, split_axis=0, concat_axis=0, tiled=True)


def spread(x, axes):
    n = lax.axis_size(axes)
    return exchange(jnp.broadcast_to(x[None], (n,) + x.shape), axes)


def stat_tile(rows):
    lane = lax.broadcasted_iota(jnp.int32, (SUB, LANE), 1)
    tile = jnp.zeros((SUB, LANE), F32)
    for s, x in enumerate(rows):
        tile = jnp.where(lane == s, jnp.sum(x * x, axis=1, keepdims=True), tile)
    return tile


def stats_kernel(hidden, stats):
    tile = stat_tile([hidden[s].astype(F32) for s in range(hidden.shape[0])])
    stats[...] = jnp.broadcast_to(tile[None], stats.shape)


def residual_kernel(hidden, parts, residual, stats):
    steps = hidden.shape[0]
    rows = []
    for s in range(steps):
        total = hidden[s].astype(F32)
        mixed = parts[0, s].astype(F32)
        for b in range(1, parts.shape[0]):
            mixed = mixed + parts[b, s].astype(F32)
        rounded = (total + mixed).astype(BF16)
        residual[s] = rounded
        rows.append(rounded.astype(F32))
    stats[...] = jnp.broadcast_to(stat_tile(rows)[None], stats.shape)


def normed_rows(parts, stats, gain, branch, width):
    out = []
    for k, part in enumerate(parts):
        b = branch ^ k
        total = stats[0, b]
        for p in range(1, stats.shape[0]):
            total = total + stats[p, b]
        scale = lax.rsqrt(total / width + EPS)
        for s in range(part.shape[0]):
            out.append(part[s].astype(F32) * scale[:, s : s + 1] * gain[...])
    return jnp.concatenate(out, axis=0).astype(BF16)


def qkv_kernel(width, heads_step, tiles, ids, *refs):
    *parts, stats, gain, w, out, lhs = refs
    step = pl.program_id(0)

    @pl.when(step == 0)
    def _():
        lhs[...] = normed_rows(parts, stats, gain, ids[2], width)

    acc = jnp.dot(lhs[...], w[...], preferred_element_type=F32)
    steps = parts[0].shape[0]
    for hh in range(heads_step):
        for s in range(steps):
            index = (step * heads_step + hh) * steps + s
            owner = index // tiles
            at = index % tiles
            side = (owner % CORES) ^ ids[1]
            for k in range(len(parts)):
                row = (k * steps + s) * SUB
                out[side, owner // CORES, ids[2] ^ k, at] = acc[
                    row : row + SUB, hh * HD : (hh + 1) * HD
                ]


def project_qkv(ids, parts, stats, gain, w, width, prefix):
    branches = len(parts)
    steps = parts[0].shape[0]
    depth, columns = w.shape
    heads = columns // HD
    heads_step = max(n for n in range(1, 6) if heads % n == 0)
    tiles = ceil_div(heads * steps, prefix)
    shape = (CORES, prefix // CORES, branches, tiles, SUB, HD)
    return pl.pallas_call(
        functools.partial(qkv_kernel, width, heads_step, tiles),
        grid_spec=pltpu.PrefetchScalarGridSpec(
            num_scalar_prefetch=1,
            grid=(heads // heads_step,),
            in_specs=[whole(p.shape) for p in parts]
            + [
                whole(stats.shape),
                whole(gain.shape),
                pl.BlockSpec((depth, heads_step * HD), lambda i, _: (0, i)),
            ],
            out_specs=whole(shape),
            scratch_shapes=[pltpu.VMEM((branches * steps * SUB, depth), BF16)],
        ),
        out_shape=jax.ShapeDtypeStruct(shape, F32),
        compiler_params=params(40),
        name="qkv",
    )(ids, *parts, stats, gain, w)


def gate_up_kernel(width, ids, *refs):
    *parts, stats, gain, w, out, lhs = refs

    @pl.when(pl.program_id(0) == 0)
    def _():
        lhs[...] = normed_rows(parts, stats, gain, ids[2], width)

    for half in range(2):
        out[0, 0, half] = jnp.dot(lhs[...], w[half], preferred_element_type=F32).astype(BF16)


def project_gate_up(ids, parts, stats, gain, w, width, prefix):
    branches = len(parts)
    rows = branches * parts[0].shape[0] * SUB
    _, depth, columns = w.shape
    unit = ceil_div(columns // LANE, prefix) * LANE
    shape = (CORES, prefix // CORES, 2, rows, unit)
    return pl.pallas_call(
        functools.partial(gate_up_kernel, width),
        grid_spec=pltpu.PrefetchScalarGridSpec(
            num_scalar_prefetch=1,
            grid=(columns // unit,),
            in_specs=[whole(p.shape) for p in parts]
            + [
                whole(stats.shape),
                whole(gain.shape),
                pl.BlockSpec((2, depth, unit), lambda i, _: (0, 0, i)),
            ],
            out_specs=pl.BlockSpec(
                (1, 1, 2, rows, unit),
                lambda i, ids: ((i % CORES) ^ ids[1], i // CORES, 0, 0, 0),
            ),
            scratch_shapes=[pltpu.VMEM((rows, depth), BF16)],
        ),
        out_shape=jax.ShapeDtypeStruct(shape, BF16),
        compiler_params=params(40),
        name="gate_up",
    )(ids, *parts, stats, gain, w)


def mix_kernel(steps, tiles, attended, w, out, lhs):
    branches = attended.shape[1]

    @pl.when(pl.program_id(0) == 0)
    def _():
        for j in range(lhs.shape[1] // HD):
            column = []
            for b in range(branches):
                for s in range(steps):
                    index = j * steps + s
                    column.append(attended[index // tiles, b, index % tiles].astype(F32))
            lhs[:, j * HD : (j + 1) * HD] = jnp.concatenate(column, axis=0).astype(BF16)

    acc = jnp.dot(lhs[...], w[...], preferred_element_type=F32)
    for b in range(branches):
        for s in range(steps):
            row = (b * steps + s) * SUB
            out[b, s] = acc[row : row + SUB].astype(BF16)


def mix_heads(attended, w, steps):
    _, branches, tiles = attended.shape[:3]
    depth, columns = w.shape
    unit = min(columns, 256)
    rows = branches * steps * SUB
    return pl.pallas_call(
        functools.partial(mix_kernel, steps, tiles),
        grid=(columns // unit,),
        in_specs=[whole(attended.shape), pl.BlockSpec((depth, unit), lambda i: (0, i))],
        out_specs=pl.BlockSpec((branches, steps, SUB, unit), lambda i: (0, 0, 0, i)),
        out_shape=jax.ShapeDtypeStruct((branches, steps, SUB, columns), BF16),
        scratch_shapes=[pltpu.VMEM((rows, depth), BF16)],
        compiler_params=params(40),
        name="mix",
    )(attended, w)


def down_kernel(steps, ids, own, other, w, out, acc):
    step = pl.program_id(0)
    mine = (step % CORES) == ids[1]

    @pl.when(step == 0)
    def _():
        acc[...] = jnp.zeros_like(acc)

    @pl.when(mine)
    def _():
        acc[...] += jnp.dot(own[0], w[...], preferred_element_type=F32)

    @pl.when(jnp.logical_not(mine))
    def _():
        acc[...] += jnp.dot(other[0], w[...], preferred_element_type=F32)

    @pl.when(step == pl.num_programs(0) - 1)
    def _():
        for b in range(out.shape[0]):
            for s in range(steps):
                row = ((ids[2] ^ b) * steps + s) * SUB
                out[b, s] = acc[pl.ds(pl.multiple_of(row, SUB), SUB), :].astype(BF16)


def project_down(ids, own, other, w, branches, steps):
    _, rows, unit = own.shape
    columns = w.shape[1]
    piece = pl.BlockSpec((1, rows, unit), lambda i, _: (i // CORES, 0, 0))
    shape = (branches, steps, SUB, columns)
    return pl.pallas_call(
        functools.partial(down_kernel, steps),
        grid_spec=pltpu.PrefetchScalarGridSpec(
            num_scalar_prefetch=1,
            grid=(w.shape[0] // unit,),
            in_specs=[piece, piece, pl.BlockSpec((unit, columns), lambda i, _: (i, 0))],
            out_specs=whole(shape),
            scratch_shapes=[pltpu.VMEM((rows, columns), F32)],
        ),
        out_shape=jax.ShapeDtypeStruct(shape, BF16),
        compiler_params=params(40),
        name="down",
    )(ids, own, other, w)


def prepare_kernel(steps, blocks_here, suffix_here, prefix, ids, parent, block_map, leaf, length, pos, bias):
    rows = leaf.shape[0]
    place = ids[0] * CORES + ids[1]
    sub = lax.broadcasted_iota(jnp.int32, (SUB, LANE), 0)
    base = jnp.zeros((SUB, LANE), jnp.int32)
    used = jnp.zeros((SUB, LANE), jnp.int32)
    owned = [jnp.zeros((SUB, LANE), jnp.int32) for _ in range(blocks_here)]
    for r in range(rows):
        current = leaf[r]
        depth = jnp.int32(0)
        hits = [jnp.int32(0)] * blocks_here
        for _ in range(parent.shape[0]):
            valid = current >= 0
            at = jnp.maximum(current, 0)
            slot = jnp.where(valid, block_map[at], -1)
            hits = [h + (slot == place * blocks_here + n).astype(jnp.int32) for n, h in enumerate(hits)]
            depth = depth + valid.astype(jnp.int32)
            current = jnp.where(valid, parent[at], -1)
        base = jnp.where(sub == r, BLK * depth + length[r], base)
        used = jnp.where(sub == r, length[r], used)
        owned = [jnp.where(sub == r, h, o) for h, o in zip(hits, owned)]
    tree = blocks_here * BLK
    keys = SUB * suffix_here
    sub_keys = lax.broadcasted_iota(jnp.int32, (SUB, keys), 0)
    key = lax.broadcasted_iota(jnp.int32, (SUB, keys), 1)
    suffix_ok = (key // suffix_here == sub_keys) & (
        place * suffix_here + key % suffix_here < used[:, :1]
    )
    suffix = jnp.where(suffix_ok, 0.0, FLOOR)
    lane = lax.broadcasted_iota(jnp.int32, (SUB, LANE), 1)
    for s in range(steps):
        pos[s] = (base + s).astype(F32)
        row = slice(s * SUB, (s + 1) * SUB)
        for n in range(blocks_here):
            bias[row, n * BLK : (n + 1) * BLK] = jnp.broadcast_to(
                jnp.where(owned[n][:, :1] > 0, 0.0, FLOOR), (SUB, BLK)
            )
        bias[row, tree : tree + keys] = suffix
        new_ok = (lane % SUB == sub) & (lane // SUB <= s) & (place == 0)
        bias[row, tree + keys : tree + keys + LANE] = jnp.where(new_ok, 0.0, FLOOR)


def prepare(ids, parent, block_map, leaf, length, steps, blocks_here, suffix_here, prefix):
    columns = blocks_here * BLK + SUB * suffix_here + LANE
    smem = pl.BlockSpec(memory_space=pltpu.SMEM)
    return pl.pallas_call(
        functools.partial(prepare_kernel, steps, blocks_here, suffix_here, prefix),
        in_specs=[smem] * 5,
        out_shape=[
            jax.ShapeDtypeStruct((steps, SUB, LANE), F32),
            jax.ShapeDtypeStruct((steps * SUB, columns), F32),
        ],
        name="prepare",
    )(ids, parent, block_map, leaf, length)


def attend_kernel(heads_in, tiles_in, heads_out, tiles_out, qkv, cosine, sine, bias, tree, suffix, out, new_kv, sums):
    k = pl.program_id(0)
    steps = cosine.shape[0]
    rows = steps * SUB
    lane = lax.broadcasted_iota(jnp.int32, (SUB, LANE), 1)

    @pl.when(k == 0)
    def _():
        sums[...] = jnp.zeros_like(sums)

    def tile(head, s):
        index = (head % heads_in) * steps + s
        return qkv[index // tiles_in, head // heads_in, index % tiles_in].astype(F32)

    def turned(x, s):
        return x * cosine[s] + pltpu.roll(x, HD // 2, 1) * sine[s]

    query = jnp.concatenate(
        [turned(tile(k * GROUP + g, s), s) for g in range(GROUP) for s in range(steps)], axis=0
    ).astype(BF16)
    keys = [turned(tile(HEADS + k, s), s) for s in range(steps)]
    values = [tile(HEADS + KVH + k, s) for s in range(steps)]
    for s in range(steps):
        new_kv[0, s] = keys[s].astype(BF16)
        new_kv[1, s] = values[s].astype(BF16)
    fill = [jnp.zeros((LANE - rows, HD), F32)]
    sources = [
        (tree[:, 0].reshape(-1, HD), tree[:, 1].reshape(-1, HD)),
        (suffix[:, 0].reshape(-1, HD), suffix[:, 1].reshape(-1, HD)),
        (
            jnp.concatenate(keys + fill, axis=0).astype(BF16),
            jnp.concatenate(values + fill, axis=0).astype(BF16),
        ),
    ]
    scores = []
    start = 0
    highest = jnp.full((GROUP, rows, 1), LOWEST, F32)
    for key, _ in sources:
        count = key.shape[0]
        product = lax.dot_general(
            query, key, (((1,), (1,)), ((), ())), preferred_element_type=F32
        ) * (HD**-0.5)
        product = product.reshape(GROUP, rows, count) + bias[:, start : start + count][None]
        highest = jnp.maximum(highest, jnp.max(product, axis=-1, keepdims=True))
        scores.append(product)
        start += count
    total = jnp.zeros((GROUP, rows, 1), F32)
    acc = jnp.zeros((GROUP * rows, HD), F32)
    for product, (_, value) in zip(scores, sources):
        weight = jnp.exp(product - highest)
        total = total + jnp.sum(weight, axis=-1, keepdims=True)
        acc = acc + jnp.dot(
            weight.reshape(GROUP * rows, -1).astype(BF16), value, preferred_element_type=F32
        )
    some = total > 0
    safe = jnp.where(some, total, 1.0)
    result = acc.reshape(GROUP, rows, HD) / safe
    log_sum = jnp.where(some, highest + jnp.log(safe), LOWEST)
    for g in range(GROUP):
        head = k * GROUP + g
        for s in range(steps):
            index = (head % heads_out) * steps + s
            owner, b, at = index // tiles_out, head // heads_out, index % tiles_out
            row = slice(s * SUB, (s + 1) * SUB)
            out[owner, b, at] = result[g, row].astype(BF16)
            sums[owner, b] = jnp.where(lane == at, log_sum[g, row], sums[owner, b])

    @pl.when(k == pl.num_programs(0) - 1)
    def _():
        for p in range(sums.shape[0]):
            for b in range(sums.shape[1]):
                value = sums[p, b]
                high = value.astype(BF16).astype(F32)
                rest = value - high
                middle = rest.astype(BF16).astype(F32)
                low = rest - middle
                packed = jnp.where(
                    lane < 32,
                    high,
                    jnp.where(lane < 64, pltpu.roll(middle, 32, 1), pltpu.roll(low, 64, 1)),
                )
                out[p, b, tiles_out] = packed.astype(BF16)


def attend(qkv, cosine, sine, bias, tree_kv, suffix_kv, heads_in, heads_out, prefix):
    _, branches, tiles_in = qkv.shape[:3]
    steps = cosine.shape[0]
    tiles_out = ceil_div(heads_out * steps, prefix)
    shape = (prefix, branches, tiles_out + 1, SUB, HD)

    def by_head(array):
        block = array.shape[:-1] + (HD,)
        return pl.BlockSpec(block, lambda k: (0,) * (len(block) - 1) + (k,))

    return pl.pallas_call(
        functools.partial(attend_kernel, heads_in, tiles_in, heads_out, tiles_out),
        grid=(KVH,),
        in_specs=[whole(a.shape) for a in (qkv, cosine, sine, bias)]
        + [by_head(tree_kv), by_head(suffix_kv)],
        out_specs=[
            whole(shape),
            pl.BlockSpec((2, steps, SUB, HD), lambda k: (0, 0, 0, k)),
        ],
        out_shape=[
            jax.ShapeDtypeStruct(shape, BF16),
            jax.ShapeDtypeStruct((2, steps, SUB, KVH * HD), BF16),
        ],
        scratch_shapes=[pltpu.VMEM((prefix, branches, SUB, LANE), F32)],
        compiler_params=params(40),
        name="attend",
    )(qkv, cosine, sine, bias, tree_kv, suffix_kv)


def join_kernel(parts, out):
    prefix, branches, count = parts.shape[:3]
    tiles = count - 1
    for b in range(branches):
        logs = []
        for p in range(prefix):
            packed = parts[p, b, tiles].astype(F32)
            logs.append(packed + pltpu.roll(packed, LANE - 32, 1) + pltpu.roll(packed, LANE - 64, 1))
        highest = functools.reduce(jnp.maximum, logs)
        weights = [jnp.exp(x - highest) for x in logs]
        total = functools.reduce(jnp.add, weights)
        weights = [w / total for w in weights]
        for t in range(tiles):
            acc = jnp.zeros((SUB, HD), F32)
            for p in range(prefix):
                acc = acc + parts[p, b, t].astype(F32) * weights[p][:, t : t + 1]
            out[b, t] = acc.astype(BF16)


def join(parts):
    _, branches, count = parts.shape[:3]
    return pl.pallas_call(
        join_kernel,
        out_shape=jax.ShapeDtypeStruct((branches, count - 1, SUB, HD), BF16),
        name="join",
    )(parts)


def body(
    hidden,
    attn_gain,
    ffn_gain,
    w_qkv,
    w_out,
    w_gate_up,
    w_down,
    tree_kv,
    suffix_kv,
    parent,
    block_map,
    leaf,
    suffix_len,
):
    steps, rows, width_dev = hidden.shape
    z_count = lax.axis_size("z")
    branches = lax.axis_size("branch")
    prefix = z_count * CORES
    width = width_dev * prefix
    devices = prefix * branches
    ids = jnp.stack([lax.axis_index("z"), lax.axis_index("core"), lax.axis_index("branch")]).astype(
        jnp.int32
    )

    pos, bias = prepare(
        ids, parent, block_map, leaf, suffix_len, steps, tree_kv.shape[0], suffix_kv.shape[2], prefix
    )
    half = HD // 2
    frequency = ROPE_BASE ** (-(jnp.arange(half, dtype=F32) * 2.0 / HD))
    angles = pos[..., :1] * frequency
    cos, sin = jnp.cos(angles), jnp.sin(angles)
    cosine = jnp.concatenate([cos, cos], axis=-1)
    sine = jnp.concatenate([-sin, sin], axis=-1)

    stats = pl.pallas_call(
        stats_kernel, out_shape=jax.ShapeDtypeStruct((devices, SUB, LANE), F32), name="stats"
    )(hidden)
    stats = exchange(stats, EVERY).reshape(prefix, branches, SUB, LANE)
    parts = [hidden] + [swap(hidden, "branch", branches, k) for k in range(1, branches)]
    part_sums = project_qkv(ids, parts, stats, attn_gain[None], w_qkv, width, prefix)
    chip_sums = part_sums[0] + lax.ppermute(part_sums[1], "core", [(0, 1), (1, 0)])
    tiles = chip_sums.shape[2]
    sent = exchange(chip_sums.reshape(z_count * branches, tiles, SUB, HD), ("z", "branch"))
    summed = jnp.sum(sent.reshape(z_count, branches, tiles, SUB, HD), axis=0).astype(BF16)
    qkv = spread(summed, ("z", "core"))

    heads_in = w_qkv.shape[1] // HD
    heads_out = w_out.shape[0] // HD
    softmax_parts, new_kv = attend(
        qkv, cosine, sine, bias, tree_kv, suffix_kv, heads_in, heads_out, prefix
    )
    new_kv = new_kv.transpose(2, 0, 1, 3)
    tiles_out = softmax_parts.shape[2]
    received = exchange(softmax_parts.reshape(devices, tiles_out, SUB, HD), EVERY)
    attended = join(received.reshape(prefix, branches, tiles_out, SUB, HD))
    attended = spread(attended, ("z", "core"))

    mixed = exchange(mix_heads(attended, w_out, steps), "branch")
    residual, stats = pl.pallas_call(
        residual_kernel,
        out_shape=[
            jax.ShapeDtypeStruct(hidden.shape, BF16),
            jax.ShapeDtypeStruct((devices, SUB, LANE), F32),
        ],
        name="residual",
    )(hidden, mixed)
    stats = exchange(stats, EVERY).reshape(prefix, branches, SUB, LANE)
    parts = [residual] + [swap(residual, "branch", branches, k) for k in range(1, branches)]
    part_sums = project_gate_up(ids, parts, stats, ffn_gain[None], w_gate_up, width, prefix)
    chip_sums = part_sums[0].astype(F32) + lax.ppermute(
        part_sums[1], "core", [(0, 1), (1, 0)]
    ).astype(F32)
    gathered = jnp.sum(exchange(chip_sums.astype(BF16), "z").astype(F32), axis=0)
    activation = (jax.nn.silu(gathered[0]) * gathered[1]).astype(BF16)
    own = spread(activation, "z")
    other = lax.ppermute(own, "core", [(0, 1), (1, 0)])
    down = exchange(project_down(ids, own, other, w_down, branches, steps), "branch")
    result = (residual.astype(F32) + jnp.sum(down.astype(F32), axis=0)).astype(BF16)
    return (result, new_kv)


def solution(mesh):
    prefix, branches = mesh.shape["prefix"], mesh.shape["branch"]
    split = Mesh(mesh.devices.reshape(prefix // CORES, CORES, branches), EVERY)
    along = ("z", "core")
    placed = (
        P(None, "branch", along),
        P(along),
        P(along),
        P(along, "branch"),
        P("branch", along),
        P(None, along, "branch"),
        P("branch", along),
        P(along, None, None, None),
        P("branch", None, along, None),
        P(),
        P(),
        P("branch"),
        P("branch"),
    )
    return jax.shard_map(
        body,
        mesh=split,
        in_specs=placed,
        out_specs=(P(None, "branch", along), P("branch", None, None, None)),
        check_vma=False,
    )
```

time: 478 us -> 238 us (0.50)
  waiting for transfers between devices: 214 us -> 34.1 us
  Pallas kernels: 0 us -> 44.8 us
  local copies, waits for them, and re-layouts: 54.2 us -> 13 us
  matrix products: 39 us -> 0 us
  other arithmetic: 23.7 us -> 1.66 us
  starting transfers between devices: 4.34 us -> 24 us
  between operations: 14.4 us -> 0.82 us
  blocking collectives: 127 us -> 118 us
    psum x2 -> x0, waiting for transfers between devices: 161 us -> none  [the longest x1 119 us: body(): lax.psum(jnp.einsum('rd,gdf->rgf', flat_rows, w_gate_up, preferred_elemen...]
    all_to_all x1 -> x6, blocking collectives: 11 us -> 118 us  [exchange(): return lax.all_to_all(x, axes, split_axis=0, concat_axis=0, tiled=True)]
    psum x3 -> x0, blocking collectives: 67.7 us -> none  [the longest x1 36.6 us: body(): summed = lax.psum(partial_sums, 'prefix').astype(jnp.bfloat16)]
    all_gather x3 -> x0, blocking collectives: 48.1 us -> none  [the longest x2 37.7 us: combined_all(): gathered = jax.tree.map(lambda a: lax.all_gather(a, axis), part)]
    pallas_call x0 -> x9, Pallas kernels: none -> 44.8 us  [the longest x1 13.6 us: project_gate_up(): pl.pallas_call(functools.partial(gate_up_kernel, width), grid_spec=pltpu....]
    dot_general x10 -> x0, matrix products: 39 us -> none  [the longest x1 16.6 us: body(): jnp.einsum('rd,gdf->rgf', flat_rows, w_gate_up, preferred_element_type=jn...]
    all_gather x1 -> x0, waiting for transfers between devices: 28.5 us -> none  [combined_all(): gathered = jax.tree.map(lambda a: lax.all_gather(a, axis), part)]
    reduce_scatter x1 -> x0, waiting for transfers between devices: 23.8 us -> none  [body(): lax.psum_scatter(jnp.einsum('srf,fd->rsd', act_steps, w_down, preferred_e...]
  transfers between devices with their start and end apart: 5 -> 13, of which waited for: 4 -> 13; matrix products, arithmetic and copies ran while one was open for 4% -> 1% of each run, Pallas kernels for 0% -> 1%
where the time goes in v1:
time: 238 us; the launch traced here: 236 us
  blocking collectives  118 us (50%)
  Pallas kernels  44.8 us (19%)
  waiting for transfers between devices  34.1 us (14%)
  starting transfers between devices  24 us (10%)
  local copies, waits for them, and re-layouts  13 us (5%)
    all_to_all x6, blocking collectives, exchange(): return lax.all_to_all(x, axes, split_axis=0, concat_axis=0, tiled=True)  118 us
    all_to_all x4, waiting for transfers between devices, exchange(): return lax.all_to_all(x, axes, split_axis=0, concat_axis=0, tiled=True)  18.8 us
    all_to_all x4, starting transfers between devices, exchange(): return lax.all_to_all(x, axes, split_axis=0, concat_axis=0, tiled=True)  16.7 us
    pallas_call x1, Pallas kernels, project_gate_up(): pl.pallas_call(functools.partial(gate_up_kernel, width), grid_spec=pltpu....  13.6 us
    unnamed x25, local copies, waits for them, and re-layouts  10.2 us
    pallas_call x1, Pallas kernels, project_down(): pl.pallas_call(functools.partial(down_kernel, steps), grid_spec=pltpu.Pre...  10.1 us
    pallas_call x1, Pallas kernels, attend(): pl.pallas_call(functools.partial(attend_kernel, heads_in, tiles_in, heads...  8.92 us
    ppermute x6, waiting for transfers between devices, swap(): return lax.ppermute(x, axis, [(i, i ^ k) for i in range(n)])  8.13 us
  transfers between devices with their start and end apart: 13, of which 13 were waited for; matrix products, arithmetic and copies ran while one was open for 1% of the time, Pallas kernels for 1%

profile of v1, /device:TPU:0, one launch (start us, length us, event | category | flops | bytes accessed | tf_op | source)
XLA Modules:
  0.0 236.4 jit_solution(13138266785622326068)
XLA Ops:
  0.6 1.5 stats.1
  2.2 7.3 %all-to-all-start = ((f32[32,8,128]{2,1,0:T(8,128)}), f32[32,8,128]{2,1,0:T(8,128)S(1)}, u32[]{:S(2)}, u32[]{:S(2)}) async-start(f32[32,8,128]{2,1,0:T(8,128)} %stats.1), calls=%async_computation | async-start | bytes 262144 | tf_op jit(solution)/shard_map/all_to_all | solution.py:46
  9.5 2.7 %collective-permute-start.2 = (bf16[3,8,1024]{2,1,0:T(8,128)(2,1)}, bf16[3,8,1024]{2,1,0:T(8,128)(2,1)S(1)}, u32[]{:S(2)}, u32[]{:S(2)}) collective-permute-start(bf16[3,8,1024]{2,1,0:T(8,128)(2,1)} %hidden.3), channel_id=1, source_target_pairs={{0,3},{1,2},{2,1},{3,0},{4,7},{5,6},{6,5},{7,4},{8,11},{9,10},{10,... | collective-permute-start | bytes 147464 | tf_op jit(solution)/shard_map/ppermute | solution.py:42
  12.2 0.6 collective-permute-start.1
  12.8 0.3 collective-permute-start
  13.0 0.1 pad_add_fusion.ids
  13.1 2.0 collective-permute-done.2.refs_3_
  15.1 1.5 collective-permute-done.1.refs_2_
  16.6 0.6 collective-permute-done.refs_1_
  17.2 0.7 all-to-all-done
  17.9 2.5 %copy-done = bf16[1024,2560]{1,0:T(8,128)(2,1)S(1)} copy-done((bf16[1024,2560]{1,0:T(8,128)(2,1)S(1)}, bf16[1024,2560]{1,0:T(8,128)(2,1)}, u32[]{:S(2)}) %copy-start) | copy-done | bytes 5242904
  20.4 0.8 copy-done.4
  21.2 0.7 copy-done.10
  21.9 3.1 %qkv.1 = f32[2,4,4,8,8,128]{5,4,3,2,1,0:T(8,128)S(1)} custom-call(s32[3]{0:T(128)S(1)} %pad_add_fusion.ids, bf16[3,8,1024]{2,1,0:T(8,128)(2,1)S(1)} %copy-done.4, bf16[3,8,1024]{2,1,0:T(8,128)(2,1)S(1)} %collective-permute-done.refs_1_, bf16[3,8,1024]{2,1,0:T(8,128)(2,1)S(1)} %collective-permute-done.1.refs_2_, ...), custom_call_target="tpu_custom_call" | custom-call | tf_op jit(solution)/shard_map/qkv/pallas_call | solution.py:125
  25.0 0.0 copy-start.2
  25.0 0.1 collective-permute-start.3
  25.1 1.9 collective-permute-done.3
  27.0 0.1 fusion.1
  27.1 20.0 %all_to_all.50 = f32[16,8,8,128]{3,2,1,0:T(8,128)S(1)} all-to-all(f32[16,8,8,128]{3,2,1,0:T(8,128)S(1)} %bitcast.33), channel_id=1, replica_groups=mesh['z'=4,'core'=2,'branch'=4] {'z','branch'}, dimensions={0} | all-to-all | bytes 1048576 | tf_op jit(solution)/shard_map/all_to_all | solution.py:46
  47.1 0.9 broadcast_in_dim.13
  48.1 3.5 %all-to-all-start.2 = ((bf16[8,4,8,8,128]{4,3,2,1,0:T(8,128)(2,1)}), bf16[8,4,8,8,128]{4,3,2,1,0:T(8,128)(2,1)S(1)}, u32[]{:S(2)}, u32[]{:S(2)}) async-start(bf16[8,4,8,8,128]{4,3,2,1,0:T(8,128)(2,1)} %broadcast_in_dim.13), calls=%async_computation.2 | async-start | bytes 1048576 | tf_op jit(solution)/shard_map/all_to_all | solution.py:46
  51.6 1.6 prepare.1
  53.2 0.8 slice_reduce_fusion
  54.0 0.1 fusion.4
  54.1 0.1 pad_maximum_fusion
  54.2 12.6 %all-to-all-done.2.qkv = bf16[8,4,8,8,128]{4,3,2,1,0:T(8,128)(2,1)S(1)} async-done(((bf16[8,4,8,8,128]{4,3,2,1,0:T(8,128)(2,1)}), bf16[8,4,8,8,128]{4,3,2,1,0:T(8,128)(2,1)S(1)}, u32[]{:S(2)}, u32[]{:S(2)}) %all-to-all-start.2) | async-done | bytes 524320 | tf_op jit(solution)/shard_map/all_to_all | solution.py:46
  66.8 1.6 copy-done.3
  68.4 0.9 copy-done.7
  69.3 8.9 %attend.1 = (bf16[8,4,7,8,128]{4,3,2,1,0:T(8,128)(2,1)S(1)}, bf16[2,3,8,1024]{3,2,1,0:T(8,128)(2,1)S(1)}) custom-call(bf16[8,4,8,8,128]{4,3,2,1,0:T(8,128)(2,1)S(1)} %all-to-all-done.2.qkv, f32[3,8,128]{2,1,0:T(8,128)S(1)} %get-tuple-element.21.cosine, f32[3,8,128]{2,1,0:T(8,128)S(1)} %get-tuple-element.22.sine, f32[24,1152]{1,0:T(8,128)S(1)} %copy-done.7, ...), custom_call_target="tpu_custom_call" | custom-call | tf_op jit(solution)/shard_map/attend/pallas_call | solution.py:416
  78.2 17.4 %all_to_all.51 = bf16[32,7,8,128]{3,2,1,0:T(8,128)(2,1)} all-to-all(bf16[32,7,8,128]{3,2,1,0:T(8,128)(2,1)S(1)} %bitcast.29), channel_id=1, replica_groups=mesh['z'=4,'core'=2,'branch'=4] {'z','core','branch'}, dimensions={0} | all-to-all | bytes 917504 | tf_op jit(solution)/shard_map/all_to_all | solution.py:46
  95.6 2.3 join.1
  97.9 0.8 broadcast_in_dim.14
  98.8 15.0 %all_to_all.52.attended = bf16[8,4,6,8,128]{4,3,2,1,0:T(8,128)(2,1)S(1)} all-to-all(bf16[8,4,6,8,128]{4,3,2,1,0:T(8,128)(2,1)S(1)} %broadcast_in_dim.14), channel_id=1, replica_groups=mesh['z'=4,'core'=2,'branch'=4] {'z','core'}, dimensions={0} | all-to-all | bytes 786432 | tf_op jit(solution)/shard_map/all_to_all | solution.py:46
  113.8 2.2 copy-done.1
  116.0 2.0 mix.1
  118.0 8.6 %all_to_all.53.parts = bf16[4,3,8,1024]{3,2,1,0:T(8,128)(2,1)} all-to-all(bf16[4,3,8,1024]{3,2,1,0:T(8,128)(2,1)S(1)} %mix.1), channel_id=1, replica_groups=mesh['z'=4,'core'=2,'branch'=4] {'branch'}, dimensions={0} | all-to-all | bytes 393216 | tf_op jit(solution)/shard_map/all_to_all | solution.py:46
  126.6 1.7 residual.1
  128.3 2.6 %all-to-all-start.6 = ((f32[32,8,128]{2,1,0:T(8,128)}), f32[32,8,128]{2,1,0:T(8,128)S(1)}, u32[]{:S(2)}, u32[]{:S(2)}) async-start(f32[32,8,128]{2,1,0:T(8,128)} %get-tuple-element.12), calls=%async_computation.6 | async-start | bytes 262144 | tf_op jit(solution)/shard_map/all_to_all | solution.py:46
  130.9 2.6 %collective-permute-start.6 = (bf16[3,8,1024]{2,1,0:T(8,128)(2,1)}, bf16[3,8,1024]{2,1,0:T(8,128)(2,1)S(1)}, u32[]{:S(2)}, u32[]{:S(2)}) collective-permute-start(bf16[3,8,1024]{2,1,0:T(8,128)(2,1)} %get-tuple-element.11.refs_0_), channel_id=1, source_target_pairs={{0,3},{1,2},{2,1},{3,0},{4,7},{5,6},{6,5},{7,4},{8,11},{9,10},{10,... | collective-permute-start | bytes 147464 | tf_op jit(solution)/shard_map/ppermute | solution.py:42
  133.5 0.5 collective-permute-start.5
  134.0 0.4 collective-permute-start.4
  134.4 2.1 collective-permute-done.6.refs_3_
  136.5 1.4 collective-permute-done.5.refs_2_
  137.9 0.5 collective-permute-done.4.refs_1_
  138.5 0.8 all-to-all-done.6
  139.3 0.0 copy-done.9
  139.3 0.8 copy-done.5
  140.1 13.6 %gate_up.1 = bf16[2,4,2,96,896]{4,3,2,1,0:T(8,128)(2,1)S(1)} custom-call(s32[3]{0:T(128)S(1)} %copy-done.9, bf16[3,8,1024]{2,1,0:T(8,128)(2,1)S(1)} %copy-done.5, bf16[3,8,1024]{2,1,0:T(8,128)(2,1)S(1)} %collective-permute-done.4.refs_1_, bf16[3,8,1024]{2,1,0:T(8,128)(2,1)S(1)} %collective-permute-done.5.refs_2_, ...), custom_call_target="tpu_custom_call" | custom-call | tf_op jit(solution)/shard_map/gate_up/pallas_call | solution.py:162
  153.7 0.1 slice_bitcast_fusion
  153.8 0.1 collective-permute-start.7
  153.9 3.1 %collective-permute-done.7 = bf16[4,2,96,896]{3,2,1,0:T(8,128)(2,1)S(1)} collective-permute-done((bf16[4,2,96,896]{3,2,1,0:T(8,128)(2,1)S(1)}, bf16[4,2,96,896]{3,2,1,0:T(8,128)(2,1)S(1)}, u32[]{:S(2)}, u32[]{:S(2)}) %collective-permute-start.7) | collective-permute-done | bytes 1376288 | tf_op jit(solution)/shard_map/ppermute | solution.py:533
  157.0 0.3 fusion
  157.3 36.6 %all_to_all.54 = bf16[4,2,96,896]{3,2,1,0:T(8,128)(2,1)S(1)} all-to-all(bf16[4,2,96,896]{3,2,1,0:T(8,128)(2,1)S(1)} %fusion), channel_id=1, replica_groups=mesh['z'=4,'core'=2,'branch'=4] {'z'}, dimensions={0} | all-to-all | bytes 2752512 | tf_op jit(solution)/shard_map/all_to_all | solution.py:46
  193.9 0.2 convert_reduce_fusion
  194.1 0.1 fusion.3
  194.2 0.1 broadcast_in_dim.32
  194.3 20.4 %all_to_all.55.own = bf16[4,96,896]{2,1,0:T(8,128)(2,1)S(1)} all-to-all(bf16[4,96,896]{2,1,0:T(8,128)(2,1)S(1)} %broadcast_in_dim.32), channel_id=1, replica_groups=mesh['z'=4,'core'=2,'branch'=4] {'z'}, dimensions={0} | all-to-all | bytes 1376256 | tf_op jit(solution)/shard_map/all_to_all | solution.py:46
  214.7 0.0 collective-permute-start.8
  214.7 2.1 collective-permute-done.8.other
  216.8 10.1 %down.1 = bf16[4,3,8,1024]{3,2,1,0:T(8,128)(2,1)} custom-call(s32[3]{0:T(128)S(1)} %copy-done.9, bf16[4,96,896]{2,1,0:T(8,128)(2,1)S(1)} %all_to_all.55.own, bf16[4,96,896]{2,1,0:T(8,128)(2,1)S(1)} %collective-permute-done.8.other, bf16[7168,1024]{1,0:T(8,128)(2,1)} %w.3), custom_call_target="tpu_custom_call" | custom-call | tf_op jit(solution)/shard_map/down/pallas_call | solution.py:251
  226.9 3.4 %all-to-all-start.9 = ((bf16[4,3,8,1024]{3,2,1,0:T(8,128)(2,1)}), bf16[4,3,8,1024]{3,2,1,0:T(8,128)(2,1)S(1)}, u32[]{:S(2)}, u32[]{:S(2)}) async-start(bf16[4,3,8,1024]{3,2,1,0:T(8,128)(2,1)} %down.1), calls=%async_computation.9 | async-start | bytes 393216 | tf_op jit(solution)/shard_map/all_to_all | solution.py:46
  230.3 0.7 copy.16
  231.1 4.7 %all-to-all-done.9 = bf16[4,3,8,1024]{3,2,1,0:T(8,128)(2,1)S(1)} async-done(((bf16[4,3,8,1024]{3,2,1,0:T(8,128)(2,1)}), bf16[4,3,8,1024]{3,2,1,0:T(8,128)(2,1)S(1)}, u32[]{:S(2)}, u32[]{:S(2)}) %all-to-all-start.9) | async-done | bytes 196640 | tf_op jit(solution)/shard_map/all_to_all | solution.py:46
  235.7 0.6 add_convert_fusion
  (19 shorter events, 0.1 us)
Async XLA Ops:
  2.2 15.7 %all-to-all-start = ((f32[32,8,128]{2,1,0:T(8,128)}), f32[32,8,128]{2,1,0:T(8,128)S(1)}, u32[]{:S(2)}, u32[]{:S(2)}) async-start(f32[32,8,128]{2,1,0:T(8,128)} %stats.1), calls=%async_computation | async-start | bytes 262144 | tf_op jit(solution)/shard_map/all_to_all | solution.py:46
  9.5 5.6 %collective-permute-start.2 = (bf16[3,8,1024]{2,1,0:T(8,128)(2,1)}, bf16[3,8,1024]{2,1,0:T(8,128)(2,1)S(1)}, u32[]{:S(2)}, u32[]{:S(2)}) collective-permute-start(bf16[3,8,1024]{2,1,0:T(8,128)(2,1)} %hidden.3), channel_id=1, source_target_pairs={{0,3},{1,2},{2,1},{3,0},{4,7},{5,6},{6,5},{7,4},{8,11},{9,10},{10,... | collective-permute-start | bytes 147464 | tf_op jit(solution)/shard_map/ppermute | solution.py:42
  12.2 4.4 %collective-permute-start.1 = (bf16[3,8,1024]{2,1,0:T(8,128)(2,1)}, bf16[3,8,1024]{2,1,0:T(8,128)(2,1)S(1)}, u32[]{:S(2)}, u32[]{:S(2)}) collective-permute-start(bf16[3,8,1024]{2,1,0:T(8,128)(2,1)} %hidden.3), channel_id=1, source_target_pairs={{0,2},{1,3},{2,0},{3,1},{4,6},{5,7},{6,4},{7,5},{8,10},{9,11},{10,... | collective-permute-start | bytes 147464 | tf_op jit(solution)/shard_map/ppermute | solution.py:42
  12.8 4.4 %collective-permute-start = (bf16[3,8,1024]{2,1,0:T(8,128)(2,1)}, bf16[3,8,1024]{2,1,0:T(8,128)(2,1)S(1)}, u32[]{:S(2)}, u32[]{:S(2)}) collective-permute-start(bf16[3,8,1024]{2,1,0:T(8,128)(2,1)} %hidden.3), channel_id=1, source_target_pairs={{0,1},{1,0},{2,3},{3,2},{4,5},{5,4},{6,7},{7,6},{8,9},{9,8},{10,11... | collective-permute-start | bytes 147464 | tf_op jit(solution)/shard_map/ppermute | solution.py:42
  13.1 11.8 %copy-start.8 = (s32[3]{0:T(128)}, s32[3]{0:T(128)S(1)}, u32[]{:S(2)}) copy-start(s32[3]{0:T(128)S(1)} %pad_add_fusion.ids) | copy-start | bytes 40
  17.9 2.5 %copy-start = (bf16[1024,2560]{1,0:T(8,128)(2,1)S(1)}, bf16[1024,2560]{1,0:T(8,128)(2,1)}, u32[]{:S(2)}) copy-start(bf16[1024,2560]{1,0:T(8,128)(2,1)} %refs_6_.2) | copy-start | bytes 15728644
  20.4 0.8 copy-start.4
  21.2 0.7 copy-start.10
  25.0 41.8 %copy-start.2 = (bf16[1,2,512,1024]{3,2,1,0:T(8,128)(2,1)S(1)}, bf16[1,2,512,1024]{3,2,1,0:T(8,128)(2,1)}, u32[]{:S(2)}) copy-start(bf16[1,2,512,1024]{3,2,1,0:T(8,128)(2,1)} %tree.1) | copy-start | bytes 6291460
  25.0 2.0 collective-permute-start.3
  48.1 18.8 %all-to-all-start.2 = ((bf16[8,4,8,8,128]{4,3,2,1,0:T(8,128)(2,1)}), bf16[8,4,8,8,128]{4,3,2,1,0:T(8,128)(2,1)S(1)}, u32[]{:S(2)}, u32[]{:S(2)}) async-start(bf16[8,4,8,8,128]{4,3,2,1,0:T(8,128)(2,1)} %broadcast_in_dim.13), calls=%async_computation.2 | async-start | bytes 1048576 | tf_op jit(solution)/shard_map/all_to_all | solution.py:46
  66.8 1.6 copy-start.3
  68.4 0.9 copy-start.7
  113.8 2.2 copy-start.1
  116.0 23.3 %copy-start.9 = (s32[3]{0:T(128)S(1)}, s32[3]{0:T(128)}, u32[]{:S(2)}) copy-start(s32[3]{0:T(128)} %copy-done.8) | copy-start | bytes 40
  116.0 23.3 %copy-start.11 = (f32[1024]{0:T(1024)S(1)}, f32[1024]{0:T(1024)}, u32[]{:S(2)}) copy-start(f32[1024]{0:T(1024)} %param.15) | copy-start | bytes 12292
  128.3 11.0 %all-to-all-start.6 = ((f32[32,8,128]{2,1,0:T(8,128)}), f32[32,8,128]{2,1,0:T(8,128)S(1)}, u32[]{:S(2)}, u32[]{:S(2)}) async-start(f32[32,8,128]{2,1,0:T(8,128)} %get-tuple-element.12), calls=%async_computation.6 | async-start | bytes 262144 | tf_op jit(solution)/shard_map/all_to_all | solution.py:46
  130.9 5.6 %collective-permute-start.6 = (bf16[3,8,1024]{2,1,0:T(8,128)(2,1)}, bf16[3,8,1024]{2,1,0:T(8,128)(2,1)S(1)}, u32[]{:S(2)}, u32[]{:S(2)}) collective-permute-start(bf16[3,8,1024]{2,1,0:T(8,128)(2,1)} %get-tuple-element.11.refs_0_), channel_id=1, source_target_pairs={{0,3},{1,2},{2,1},{3,0},{4,7},{5,6},{6,5},{7,4},{8,11},{9,10},{10,... | collective-permute-start | bytes 147464 | tf_op jit(solution)/shard_map/ppermute | solution.py:42
  133.5 4.4 %collective-permute-start.5 = (bf16[3,8,1024]{2,1,0:T(8,128)(2,1)}, bf16[3,8,1024]{2,1,0:T(8,128)(2,1)S(1)}, u32[]{:S(2)}, u32[]{:S(2)}) collective-permute-start(bf16[3,8,1024]{2,1,0:T(8,128)(2,1)} %get-tuple-element.11.refs_0_), channel_id=1, source_target_pairs={{0,2},{1,3},{2,0},{3,1},{4,6},{5,7},{6,4},{7,5},{8,10},{9,11},{10,... | collective-permute-start | bytes 147464 | tf_op jit(solution)/shard_map/ppermute | solution.py:42
  134.0 4.4 %collective-permute-start.4 = (bf16[3,8,1024]{2,1,0:T(8,128)(2,1)}, bf16[3,8,1024]{2,1,0:T(8,128)(2,1)S(1)}, u32[]{:S(2)}, u32[]{:S(2)}) collective-permute-start(bf16[3,8,1024]{2,1,0:T(8,128)(2,1)} %get-tuple-element.11.refs_0_), channel_id=1, source_target_pairs={{0,1},{1,0},{2,3},{3,2},{4,5},{5,4},{6,7},{7,6},{8,9},{9,8},{10,11... | collective-permute-start | bytes 147464 | tf_op jit(solution)/shard_map/ppermute | solution.py:42
  139.3 0.8 copy-start.5
  153.8 3.2 %collective-permute-start.7 = (bf16[4,2,96,896]{3,2,1,0:T(8,128)(2,1)S(1)}, bf16[4,2,96,896]{3,2,1,0:T(8,128)(2,1)S(1)}, u32[]{:S(2)}, u32[]{:S(2)}) collective-permute-start(bf16[4,2,96,896]{3,2,1,0:T(8,128)(2,1)S(1)} %slice_bitcast_fusion), channel_id=1, source_target_pairs={{0,4},{4,0},{1,5},{5,1},{2,6},{6,2},{3,7},{7,3},{8,12},{12,8},{9,1... | collective-permute-start | bytes 4128776 | tf_op jit(solution)/shard_map/ppermute | solution.py:533
  214.7 21.0 %copy-start.6 = (bf16[3,8,1024]{2,1,0:T(8,128)(2,1)S(1)}, bf16[3,8,1024]{2,1,0:T(8,128)(2,1)}, u32[]{:S(2)}) copy-start(bf16[3,8,1024]{2,1,0:T(8,128)(2,1)} %get-tuple-element.11.refs_0_) | copy-start | bytes 147460
  214.7 2.1 collective-permute-start.8
  226.9 8.8 %all-to-all-start.9 = ((bf16[4,3,8,1024]{3,2,1,0:T(8,128)(2,1)}), bf16[4,3,8,1024]{3,2,1,0:T(8,128)(2,1)S(1)}, u32[]{:S(2)}, u32[]{:S(2)}) async-start(bf16[4,3,8,1024]{3,2,1,0:T(8,128)(2,1)} %down.1), calls=%async_computation.9 | async-start | bytes 393216 | tf_op jit(solution)/shard_map/all_to_all | solution.py:46

commit v2 on v1

v2 whole, which is shorter than its diff:
```python
import functools

import jax
import jax.numpy as jnp
from jax import lax
from jax.experimental import pallas as pl
from jax.experimental.pallas import tpu as pltpu
from jax.sharding import Mesh
from jax.sharding import PartitionSpec as P

HEADS = 64
KVH = 8
HD = 128
GROUP = HEADS // KVH
BLK = 512
CORES = 2
SUB = 8
LANE = 128

EPS = 1e-05
ROPE_BASE = 500000.0
FLOOR = -1e30
LOWEST = -1e29
F32 = jnp.float32
BF16 = jnp.bfloat16
AXES = ("z", "core", "branch")


def ceil_div(a, b):
    return -(-a // b)


def whole(shape):
    return pl.BlockSpec(shape, lambda *_: (0,) * len(shape))


def exchange(x, axes):
    return lax.all_to_all(x, axes, split_axis=0, concat_axis=0, tiled=True)


def params(mib):
    return pltpu.CompilerParams(vmem_limit_bytes=mib * 2**20)


IN_HBM = pl.BlockSpec(memory_space=pltpu.HBM)
IN_VMEM = pl.BlockSpec(memory_space=pltpu.VMEM)
IN_SMEM = pl.BlockSpec(memory_space=pltpu.SMEM)


def bits(n):
    return [1 << i for i in range(n.bit_length() - 1)]


def mirror(q, n):
    out = 0
    top = n.bit_length() - 2
    for i in range(top + 1):
        out = out + (((q >> i) & 1) << (top - i))
    return out


def swap(x, axis, bit):
    return lax.ppermute(x, axis, [(i, i ^ bit) for i in range(lax.axis_size(axis))])


def reduce_rounds(x, axis, order):
    for bit in order:
        half = x.shape[0] // 2
        x = x[:half] + swap(x[half:], axis, bit)
    return x[0]


def gather_rounds(x, axis, order):
    x = x[None]
    for bit in order:
        x = jnp.concatenate([x, swap(x, axis, bit)], axis=0)
    return x


def add_round(x, axis, order):
    for bit in order:
        half = x.shape[0] // 2
        kept = x[:half].astype(F32)
        kept = kept + swap(x[half:], axis, bit).astype(F32)
        x = kept.astype(BF16)
    return kept[0]


def add(a, b):
    return (a.astype(F32) + b.astype(F32)).astype(BF16)


def norm_and_gather(x, gain, width):
    value = x.astype(F32)
    squares = jnp.sum(value * value, axis=2)
    squares = squares + swap(squares, "core", 1)
    for bit in bits(lax.axis_size("z")):
        squares = squares + swap(squares, "z", bit)
    scale = lax.rsqrt(squares / width + EPS)
    normed = (value * scale[..., None] * gain).astype(BF16)
    rows = gather_rounds(normed, "branch", bits(lax.axis_size("branch")))
    return rows.reshape(-1, x.shape[2])


def gather_prefix(x):
    x = gather_rounds(x, "z", bits(lax.axis_size("z"))[::-1])
    x = gather_rounds(x, "core", [1])
    return x.reshape((-1,) + x.shape[2:])


def place_table():
    z_count = lax.axis_size("z")
    owner = jnp.arange(z_count * CORES, dtype=jnp.int32)
    far = mirror((owner // CORES) ^ lax.axis_index("z"), z_count)
    return (((owner % CORES) ^ lax.axis_index("core")) * z_count + far).astype(jnp.int32)


def streamed(count, ahead, copies, work):
    for i in range(min(ahead, count)):
        for c in copies(i):
            c.start()

    def step(i, carry):
        for c in copies(i):
            c.wait()

        @pl.when(i + ahead < count)
        def _():
            for c in copies(i + ahead):
                c.start()

        work(i)
        return carry

    lax.fori_loop(0, count, step, 0)


def qkv_kernel(steps, heads_step, tiles, ids, lhs, w, out, buffer, sems):
    count = buffer.shape[0]
    columns = heads_step * HD
    branches = out.shape[2]

    def copies(i):
        at = pl.multiple_of(i * columns, columns)
        return [pltpu.make_async_copy(w.at[:, pl.ds(at, columns)], buffer.at[i], sems.at[i])]

    def work(i):
        acc = jnp.dot(lhs[...], buffer[i], preferred_element_type=F32)
        for hh in range(heads_step):
            for s in range(steps):
                index = (i * heads_step + hh) * steps + s
                owner = index // tiles
                side = (owner % CORES) ^ ids[1]
                for k in range(branches):
                    row = (k * steps + s) * SUB
                    out[side, owner // CORES, ids[2] ^ k, index % tiles] = acc[
                        row : row + SUB, hh * HD : (hh + 1) * HD
                    ]

    streamed(count, min(4, count), copies, work)


def project_qkv(ids, lhs, w, steps, z_count, branches):
    depth, columns = w.shape
    heads = columns // HD
    heads_step = max(n for n in range(1, 5) if heads % n == 0)
    count = heads // heads_step
    tiles = ceil_div(heads * steps, z_count * CORES)
    shape = (CORES, z_count, branches, tiles, SUB, HD)
    return pl.pallas_call(
        functools.partial(qkv_kernel, steps, heads_step, tiles),
        in_specs=[IN_SMEM, IN_VMEM, IN_HBM],
        out_shape=jax.ShapeDtypeStruct(shape, F32),
        scratch_shapes=[
            pltpu.VMEM((count, depth, heads_step * HD), BF16),
            pltpu.SemaphoreType.DMA((count,)),
        ],
        compiler_params=params(62),
        name="qkv",
    )(ids, lhs, w)


def gate_up_kernel(unit, start, ids, lhs, w, out, buffer, sems):
    count = buffer.shape[0]
    part = buffer.shape[3]
    z_count = out.shape[1]

    def copies(i):
        at = pl.multiple_of(i * unit + start, LANE)
        return [
            pltpu.make_async_copy(w.at[g, :, pl.ds(at, part)], buffer.at[i, g], sems.at[i, g])
            for g in range(2)
        ]

    def work(i):
        side = (i % CORES) ^ ids[1]
        far = mirror((i // CORES) ^ ids[0], z_count)
        for g in range(2):
            product = jnp.dot(lhs[...], buffer[i, g], preferred_element_type=F32)
            out[side, far, g] = product.astype(BF16)

    streamed(count, 3, copies, work)


def project_gate_up(ids, lhs, w, unit, start, part, z_count):
    rows = lhs.shape[0]
    _, depth, columns = w.shape
    count = columns // unit
    shape = (CORES, z_count, 2, rows, part)
    return pl.pallas_call(
        functools.partial(gate_up_kernel, unit, start),
        in_specs=[IN_SMEM, IN_VMEM, IN_HBM],
        out_shape=jax.ShapeDtypeStruct(shape, BF16),
        scratch_shapes=[
            pltpu.VMEM((count, 2, depth, part), BF16),
            pltpu.SemaphoreType.DMA((count, 2)),
        ],
        compiler_params=params(52),
        name="gate_up",
    )(ids, lhs, w)


def mix_kernel(steps, table, attended, w, out, lhs, buffer, sems):
    count = buffer.shape[0]
    unit = buffer.shape[2]
    tiles = attended.shape[2]

    def copies(i):
        at = pl.multiple_of(i * unit, LANE)
        return [pltpu.make_async_copy(w.at[:, pl.ds(at, unit)], buffer.at[i], sems.at[i])]

    def build():
        for j in range(lhs.shape[1] // HD):
            column = []
            for b in range(out.shape[0]):
                for s in range(steps):
                    index = j * steps + s
                    tile = attended[table[index // tiles], b, index % tiles]
                    column.append(tile.astype(F32))
            lhs[:, j * HD : (j + 1) * HD] = jnp.concatenate(column, axis=0).astype(BF16)

    for i in range(count):
        copies(i)[0].start()
    build()

    def step(i, carry):
        copies(i)[0].wait()
        acc = jnp.dot(lhs[...], buffer[i], preferred_element_type=F32)
        at = pl.ds(pl.multiple_of(i * unit, LANE), unit)
        for b in range(out.shape[0]):
            for s in range(steps):
                row = (b * steps + s) * SUB
                out[b, s, :, at] = acc[row : row + SUB].astype(BF16)
        return carry

    lax.fori_loop(0, count, step, 0)


def mix_heads(table, attended, w, steps):
    branches = attended.shape[1]
    depth, columns = w.shape
    unit = min(columns, 256)
    count = columns // unit
    rows = branches * steps * SUB
    return pl.pallas_call(
        functools.partial(mix_kernel, steps),
        in_specs=[IN_SMEM, IN_VMEM, IN_HBM],
        out_shape=jax.ShapeDtypeStruct((branches, steps, SUB, columns), BF16),
        scratch_shapes=[
            pltpu.VMEM((rows, depth), BF16),
            pltpu.VMEM((count, depth, unit), BF16),
            pltpu.SemaphoreType.DMA((count,)),
        ],
        compiler_params=params(62),
        name="mix",
    )(table, attended, w)


def down_kernel(unit, start, table, activation, w, out, buffer, sems):
    part = buffer.shape[1]
    out[...] = jnp.zeros_like(out)

    def copies(i):
        at = pl.multiple_of(i * unit + start, LANE)
        return [pltpu.make_async_copy(w.at[pl.ds(at, part), :], buffer.at[i], sems.at[i])]

    def work(i):
        out[...] += jnp.dot(activation[table[i]], buffer[i], preferred_element_type=F32)

    streamed(buffer.shape[0], min(4, buffer.shape[0]), copies, work)


def project_down(table, activation, w, unit, start):
    rows, part = activation.shape[1:]
    columns = w.shape[1]
    count = w.shape[0] // unit
    return pl.pallas_call(
        functools.partial(down_kernel, unit, start),
        in_specs=[IN_SMEM, IN_VMEM, IN_HBM],
        out_shape=jax.ShapeDtypeStruct((rows, columns), F32),
        scratch_shapes=[
            pltpu.VMEM((count, part, columns), BF16),
            pltpu.SemaphoreType.DMA((count,)),
        ],
        compiler_params=params(60),
        name="down",
    )(table, activation, w)


def prepare_kernel(steps, blocks_here, suffix_here, prefix, ids, parent, block_map, leaf, length, pos, bias):
    rows = leaf.shape[0]
    place = ids[0] * CORES + ids[1]
    sub = lax.broadcasted_iota(jnp.int32, (SUB, LANE), 0)
    base = jnp.zeros((SUB, LANE), jnp.int32)
    used = jnp.zeros((SUB, LANE), jnp.int32)
    owned = [jnp.zeros((SUB, LANE), jnp.int32) for _ in range(blocks_here)]
    for r in range(rows):
        current = leaf[r]
        depth = jnp.int32(0)
        hits = [jnp.int32(0)] * blocks_here
        for _ in range(parent.shape[0]):
            valid = current >= 0
            at = jnp.maximum(current, 0)
            slot = jnp.where(valid, block_map[at], -1)
            hits = [h + (slot == place * blocks_here + n).astype(jnp.int32) for n, h in enumerate(hits)]
            depth = depth + valid.astype(jnp.int32)
            current = jnp.where(valid, parent[at], -1)
        base = jnp.where(sub == r, BLK * depth + length[r], base)
        used = jnp.where(sub == r, length[r], used)
        owned = [jnp.where(sub == r, h, o) for h, o in zip(hits, owned)]
    tree = blocks_here * BLK
    keys = SUB * suffix_here
    sub_keys = lax.broadcasted_iota(jnp.int32, (SUB, keys), 0)
    key = lax.broadcasted_iota(jnp.int32, (SUB, keys), 1)
    suffix_ok = (key // suffix_here == sub_keys) & (
        place * suffix_here + key % suffix_here < used[:, :1]
    )
    suffix = jnp.where(suffix_ok, 0.0, FLOOR)
    lane = lax.broadcasted_iota(jnp.int32, (SUB, LANE), 1)
    for s in range(steps):
        pos[s] = (base + s).astype(F32)
        row = slice(s * SUB, (s + 1) * SUB)
        for n in range(blocks_here):
            bias[row, n * BLK : (n + 1) * BLK] = jnp.broadcast_to(
                jnp.where(owned[n][:, :1] > 0, 0.0, FLOOR), (SUB, BLK)
            )
        bias[row, tree : tree + keys] = suffix
        new_ok = (lane % SUB == sub) & (lane // SUB <= s) & (place == 0)
        bias[row, tree + keys : tree + keys + LANE] = jnp.where(new_ok, 0.0, FLOOR)


def prepare(ids, parent, block_map, leaf, length, steps, blocks_here, suffix_here, prefix):
    columns = blocks_here * BLK + SUB * suffix_here + LANE
    smem = pl.BlockSpec(memory_space=pltpu.SMEM)
    return pl.pallas_call(
        functools.partial(prepare_kernel, steps, blocks_here, suffix_here, prefix),
        in_specs=[smem] * 5,
        out_shape=[
            jax.ShapeDtypeStruct((steps, SUB, LANE), F32),
            jax.ShapeDtypeStruct((steps * SUB, columns), F32),
        ],
        name="prepare",
    )(ids, parent, block_map, leaf, length)


def attend_kernel(heads_in, tiles_in, heads_out, tiles_out, table, qkv, cosine, sine, bias, tree, suffix, out, new_kv, sums):
    k = pl.program_id(0)
    steps = cosine.shape[0]
    rows = steps * SUB
    lane = lax.broadcasted_iota(jnp.int32, (SUB, LANE), 1)

    @pl.when(k == 0)
    def _():
        sums[...] = jnp.zeros_like(sums)

    def tile(head, s):
        index = (head % heads_in) * steps + s
        return qkv[table[index // tiles_in], head // heads_in, index % tiles_in].astype(F32)

    def turned(x, s):
        return x * cosine[s] + pltpu.roll(x, HD // 2, 1) * sine[s]

    query = jnp.concatenate(
        [turned(tile(k * GROUP + g, s), s) for g in range(GROUP) for s in range(steps)], axis=0
    ).astype(BF16)
    keys = [turned(tile(HEADS + k, s), s) for s in range(steps)]
    values = [tile(HEADS + KVH + k, s) for s in range(steps)]
    for s in range(steps):
        new_kv[0, s] = keys[s].astype(BF16)
        new_kv[1, s] = values[s].astype(BF16)
    fill = [jnp.zeros((LANE - rows, HD), F32)]
    sources = [
        (tree[:, 0].reshape(-1, HD), tree[:, 1].reshape(-1, HD)),
        (suffix[:, 0].reshape(-1, HD), suffix[:, 1].reshape(-1, HD)),
        (
            jnp.concatenate(keys + fill, axis=0).astype(BF16),
            jnp.concatenate(values + fill, axis=0).astype(BF16),
        ),
    ]
    scores = []
    start = 0
    highest = jnp.full((GROUP, rows, 1), LOWEST, F32)
    for key, _ in sources:
        count = key.shape[0]
        product = lax.dot_general(
            query, key, (((1,), (1,)), ((), ())), preferred_element_type=F32
        ) * (HD**-0.5)
        product = product.reshape(GROUP, rows, count) + bias[:, start : start + count][None]
        highest = jnp.maximum(highest, jnp.max(product, axis=-1, keepdims=True))
        scores.append(product)
        start += count
    total = jnp.zeros((GROUP, rows, 1), F32)
    acc = jnp.zeros((GROUP * rows, HD), F32)
    for product, (_, value) in zip(scores, sources):
        weight = jnp.exp(product - highest)
        total = total + jnp.sum(weight, axis=-1, keepdims=True)
        acc = acc + jnp.dot(
            weight.reshape(GROUP * rows, -1).astype(BF16), value, preferred_element_type=F32
        )
    some = total > 0
    safe = jnp.where(some, total, 1.0)
    result = acc.reshape(GROUP, rows, HD) / safe
    log_sum = jnp.where(some, highest + jnp.log(safe), LOWEST)
    for g in range(GROUP):
        head = k * GROUP + g
        for s in range(steps):
            index = (head % heads_out) * steps + s
            owner, b, at = index // tiles_out, head // heads_out, index % tiles_out
            row = slice(s * SUB, (s + 1) * SUB)
            out[owner, b, at] = result[g, row].astype(BF16)
            sums[owner, b] = jnp.where(lane == at, log_sum[g, row], sums[owner, b])

    @pl.when(k == pl.num_programs(0) - 1)
    def _():
        for p in range(sums.shape[0]):
            for b in range(sums.shape[1]):
                value = sums[p, b]
                high = value.astype(BF16).astype(F32)
                rest = value - high
                middle = rest.astype(BF16).astype(F32)
                low = rest - middle
                packed = jnp.where(
                    lane < 32,
                    high,
                    jnp.where(lane < 64, pltpu.roll(middle, 32, 1), pltpu.roll(low, 64, 1)),
                )
                out[p, b, tiles_out] = packed.astype(BF16)


def attend(table, qkv, cosine, sine, bias, tree_kv, suffix_kv, heads_in, heads_out, prefix):
    _, branches, tiles_in = qkv.shape[:3]
    steps = cosine.shape[0]
    tiles_out = ceil_div(heads_out * steps, prefix)
    shape = (prefix, branches, tiles_out + 1, SUB, HD)

    def by_head(array):
        block = array.shape[:-1] + (HD,)
        return pl.BlockSpec(block, lambda k, _: (0,) * (len(block) - 1) + (k,))

    return pl.pallas_call(
        functools.partial(attend_kernel, heads_in, tiles_in, heads_out, tiles_out),
        grid_spec=pltpu.PrefetchScalarGridSpec(
            num_scalar_prefetch=1,
            grid=(KVH,),
            in_specs=[whole(a.shape) for a in (qkv, cosine, sine, bias)]
            + [by_head(tree_kv), by_head(suffix_kv)],
            out_specs=[
                whole(shape),
                pl.BlockSpec((2, steps, SUB, HD), lambda k, _: (0, 0, 0, k)),
            ],
            scratch_shapes=[pltpu.VMEM((prefix, branches, SUB, LANE), F32)],
        ),
        out_shape=[
            jax.ShapeDtypeStruct(shape, BF16),
            jax.ShapeDtypeStruct((2, steps, SUB, KVH * HD), BF16),
        ],
        compiler_params=params(62),
        name="attend",
    )(table, qkv, cosine, sine, bias, tree_kv, suffix_kv)


def join_kernel(parts, out):
    prefix, branches, count = parts.shape[:3]
    tiles = count - 1
    for b in range(branches):
        logs = []
        for p in range(prefix):
            packed = parts[p, b, tiles].astype(F32)
            logs.append(packed + pltpu.roll(packed, LANE - 32, 1) + pltpu.roll(packed, LANE - 64, 1))
        highest = functools.reduce(jnp.maximum, logs)
        weights = [jnp.exp(x - highest) for x in logs]
        total = functools.reduce(jnp.add, weights)
        weights = [w / total for w in weights]
        for t in range(tiles):
            acc = jnp.zeros((SUB, HD), F32)
            for p in range(prefix):
                acc = acc + parts[p, b, t].astype(F32) * weights[p][:, t : t + 1]
            out[b, t] = acc.astype(BF16)


def join(parts):
    _, branches, count = parts.shape[:3]
    return pl.pallas_call(
        join_kernel,
        in_specs=[IN_VMEM],
        out_specs=IN_VMEM,
        out_shape=jax.ShapeDtypeStruct((branches, count - 1, SUB, HD), BF16),
        name="join",
    )(parts)


def body(
    hidden,
    attn_gain,
    ffn_gain,
    w_qkv,
    w_out,
    w_gate_up,
    w_down,
    tree_kv,
    suffix_kv,
    parent,
    block_map,
    leaf,
    suffix_len,
):
    steps, rows, width_dev = hidden.shape
    z_count = lax.axis_size("z")
    branches = lax.axis_size("branch")
    prefix = z_count * CORES
    devices = prefix * branches
    width = width_dev * prefix
    near = bits(z_count)
    across = bits(branches)
    table = place_table()
    ids = jnp.stack([lax.axis_index(a) for a in AXES]).astype(jnp.int32)

    pos, bias = prepare(
        ids, parent, block_map, leaf, suffix_len, steps, tree_kv.shape[0], suffix_kv.shape[2], prefix
    )
    half = HD // 2
    frequency = ROPE_BASE ** (-(jnp.arange(half, dtype=F32) * 2.0 / HD))
    angles = pos[..., :1] * frequency
    cos, sin = jnp.cos(angles), jnp.sin(angles)
    cosine = jnp.concatenate([cos, cos], axis=-1)
    sine = jnp.concatenate([-sin, sin], axis=-1)

    lhs = norm_and_gather(hidden, attn_gain, width)
    part_sums = project_qkv(ids, lhs, w_qkv, steps, z_count, branches)
    chip_sums = part_sums[0] + swap(part_sums[1], "core", 1)
    tiles = chip_sums.shape[2]
    received = exchange(chip_sums.reshape(z_count * branches, tiles, SUB, HD), ("z", "branch"))
    summed = jnp.sum(received.reshape(z_count, branches, tiles, SUB, HD), axis=0).astype(BF16)
    qkv = gather_prefix(summed)

    heads_in = w_qkv.shape[1] // HD
    heads_out = w_out.shape[0] // HD
    softmax_parts, new_kv = attend(
        table, qkv, cosine, sine, bias, tree_kv, suffix_kv, heads_in, heads_out, prefix
    )
    new_kv = new_kv.transpose(2, 0, 1, 3)
    tiles_out = softmax_parts.shape[2]
    received = exchange(softmax_parts.reshape(devices, tiles_out, SUB, HD), AXES)
    attended = join(received.reshape(prefix, branches, tiles_out, SUB, HD))
    attended = gather_prefix(attended)

    mixed = exchange(mix_heads(table, attended, w_out, steps), "branch")
    mixed = jnp.sum(mixed.astype(F32), axis=0)
    residual = (hidden.astype(F32) + mixed).astype(BF16)

    lhs = norm_and_gather(residual, ffn_gain, width)
    unit = ceil_div(w_gate_up.shape[2] // LANE, prefix) * LANE
    first = ceil_div(unit // LANE, 2) * LANE
    down = None
    for start, part in ((0, first), (first, unit - first)):
        if part == 0:
            continue
        part_sums = project_gate_up(ids, lhs, w_gate_up, unit, start, part, z_count)
        chip_sums = add(part_sums[0], swap(part_sums[1], "core", 1))
        lhs, chip_sums = lax.optimization_barrier((lhs, chip_sums))
        gate, up = add_round(chip_sums, "z", near)
        activation = gather_prefix((jax.nn.silu(gate) * up).astype(BF16))
        product = project_down(table, activation, w_down, unit, start)
        down = product if down is None else down + product
    down = down.astype(BF16).reshape(branches, steps, rows, width_dev)
    down = add_round(down, "branch", across[::-1])
    result = (residual.astype(F32) + down).astype(BF16)
    return (result, new_kv)


def solution(mesh):
    prefix, branches = mesh.shape["prefix"], mesh.shape["branch"]
    split = Mesh(mesh.devices.reshape(prefix // CORES, CORES, branches), AXES)
    along = ("z", "core")
    placed = (
        P(None, "branch", along),
        P(along),
        P(along),
        P(along, "branch"),
        P("branch", along),
        P(None, along, "branch"),
        P("branch", along),
        P(along, None, None, None),
        P("branch", None, along, None),
        P(),
        P(),
        P("branch"),
        P("branch"),
    )
    return jax.shard_map(
        body,
        mesh=split,
        in_specs=placed,
        out_specs=(P(None, "branch", along), P("branch", None, None, None)),
        check_vma=False,
    )
```

time: 238 us -> 227 us (0.954)
  blocking collectives: 118 us -> 49.8 us
  waiting for transfers between devices: 34.1 us -> 88 us
  other arithmetic: 1.66 us -> 13.8 us
  local copies, waits for them, and re-layouts: 13 us -> 2.86 us
  Pallas kernels: 44.8 us -> 49.3 us
  starting transfers between devices: 24 us -> 21.5 us
    ppermute x9 -> x31, waiting for transfers between devices: 15.3 us -> 88 us  [swap(): lax.ppermute(x, axis, [(i, i ^ bit) for i in range(lax.axis_size(axis))])]
    all_to_all x6 -> x3, blocking collectives: 118 us -> 49.8 us  [exchange(): return lax.all_to_all(x, axes, split_axis=0, concat_axis=0, tiled=True)]
    all_to_all x4 -> x0, waiting for transfers between devices: 18.8 us -> none  [exchange(): return lax.all_to_all(x, axes, split_axis=0, concat_axis=0, tiled=True)]
    all_to_all x4 -> x0, starting transfers between devices: 16.7 us -> none  [exchange(): return lax.all_to_all(x, axes, split_axis=0, concat_axis=0, tiled=True)]
    ppermute x9 -> x31, starting transfers between devices: 7.25 us -> 21.5 us  [swap(): lax.ppermute(x, axis, [(i, i ^ bit) for i in range(lax.axis_size(axis))])]
    unnamed x25 -> x11, local copies, waits for them, and re-layouts: 10.2 us -> 0.76 us
    concatenate x0 -> x12, other arithmetic: none -> 5.14 us  [gather_rounds(): x = jnp.concatenate([x, swap(x, axis, bit)], axis=0)]
    pallas_call x7, Pallas kernels: 34.3 us -> 36.9 us  [the longest x2 13.6 us: project_gate_up(): pl.pallas_call(functools.partial(gate_up_kernel, unit, start), in_specs=[...]
  transfers between devices with their start and end apart: 13 -> 31, of which waited for: 13 -> 27; matrix products, arithmetic and copies ran while one was open for 1% -> 2% of each run, Pallas kernels for 1% -> 6%
where the time goes in v2:
time: 227 us; the launch traced here: 226 us
  waiting for transfers between devices  88 us (39%)
  blocking collectives  49.8 us (22%)
  Pallas kernels  49.3 us (22%)
  starting transfers between devices  21.5 us (9%)
  other arithmetic  13.8 us (6%)
  local copies, waits for them, and re-layouts  2.86 us (1%)
    ppermute x31, waiting for transfers between devices, swap(): lax.ppermute(x, axis, [(i, i ^ bit) for i in range(lax.axis_size(axis))])  88 us
    all_to_all x3, blocking collectives, exchange(): return lax.all_to_all(x, axes, split_axis=0, concat_axis=0, tiled=True)  49.8 us
    ppermute x31, starting transfers between devices, swap(): lax.ppermute(x, axis, [(i, i ^ bit) for i in range(lax.axis_size(axis))])  21.5 us
    pallas_call x2, Pallas kernels, project_gate_up(): pl.pallas_call(functools.partial(gate_up_kernel, unit, start), in_specs=[...  13.6 us
    pallas_call x2, Pallas kernels, project_down(): pl.pallas_call(functools.partial(down_kernel, unit, start), in_specs=[IN_...  11.5 us
    pallas_call x1, Pallas kernels, attend(): pl.pallas_call(functools.partial(attend_kernel, heads_in, tiles_in, heads...  10.7 us
    pallas_call x1, Pallas kernels, project_qkv(): pl.pallas_call(functools.partial(qkv_kernel, steps, heads_step, tiles), i...  5.36 us
    concatenate x12, other arithmetic, gather_rounds(): x = jnp.concatenate([x, swap(x, axis, bit)], axis=0)  5.14 us
  transfers between devices with their start and end apart: 31, of which 27 were waited for; matrix products, arithmetic and copies ran while one was open for 2% of the time, Pallas kernels for 6%

profile of v2, /device:TPU:0, one launch (start us, length us, event | category | flops | bytes accessed | tf_op | source)
XLA Modules:
  0.0 226.2 jit_solution(820475420761108980)
XLA Ops:
  0.6 0.9 fusion.8
  2.0 0.8 collective-permute-done
  2.8 2.9 %collective-permute-start.1 = (f32[3,8]{1,0:T(4,128)S(1)}, f32[3,8]{1,0:T(4,128)S(1)}, u32[]{:S(2)}, u32[]{:S(2)}) collective-permute-start(f32[3,8]{1,0:T(4,128)S(1)} %add.98), channel_id=1, source_target_pairs={{0,8},{8,0},{16,24},{24,16},{1,9},{9,1},{17,25},{25,17},{2,10},{10... | collective-permute-start | bytes 296 | tf_op jit(solution)/shard_map/ppermute | solution.py:63
  5.7 1.6 collective-permute-done.1
  7.3 3.0 %collective-permute-start.2 = (f32[3,8]{1,0:T(4,128)S(1)}, f32[3,8]{1,0:T(4,128)S(1)}, u32[]{:S(2)}, u32[]{:S(2)}) collective-permute-start(f32[3,8]{1,0:T(4,128)S(1)} %add.99), channel_id=1, source_target_pairs={{0,16},{8,24},{16,0},{24,8},{1,17},{9,25},{17,1},{25,9},{2,18},{10... | collective-permute-start | bytes 296 | tf_op jit(solution)/shard_map/ppermute | solution.py:63
  10.3 1.6 collective-permute-done.2
  11.9 0.9 fusion.17
  12.8 1.9 collective-permute-start.3
  14.7 2.3 %collective-permute-done.3 = bf16[1,3,8,1024]{3,2,1,0:T(8,128)(2,1)S(1)} collective-permute-done((bf16[1,3,8,1024]{3,2,1,0:T(8,128)(2,1)S(1)}, bf16[1,3,8,1024]{3,2,1,0:T(8,128)(2,1)S(1)}, u32[]{:S(2)}, u32[]{:S(2)}) %collective-permute-start.3) | collective-permute-done | bytes 49184 | tf_op jit(solution)/shard_map/ppermute | solution.py:63
  16.9 1.9 collective-permute-start.4
  19.5 2.1 collective-permute-done.4
  21.6 0.7 pad_maximum_fusion.4
  22.3 5.4 %qkv.1 = f32[2,4,4,8,8,128]{5,4,3,2,1,0:T(8,128)} custom-call(s32[3]{0:T(128)} %pad_add_fusion.ids, bf16[96,1024]{1,0:T(8,128)(2,1)} %bitcast.84, bf16[1024,2560]{1,0:T(8,128)(2,1)} %w.6), custom_call_target="tpu_custom_call" | custom-call | tf_op jit(solution)/shard_map/qkv/pallas_call | solution.py:170
  27.7 1.1 slice_bitcast_fusion.4
  28.8 1.9 collective-permute-done.5
  30.7 1.1 fusion.2
  31.9 22.4 %all_to_all.15 = f32[16,8,8,128]{3,2,1,0:T(8,128)S(1)} all-to-all(f32[16,8,8,128]{3,2,1,0:T(8,128)S(1)} %bitcast.80), channel_id=1, replica_groups=mesh['z'=4,'core'=2,'branch'=4] {'z','branch'}, dimensions={0} | all-to-all | bytes 1048576 | tf_op jit(solution)/shard_map/all_to_all | solution.py:38
  54.3 0.8 collective-permute-start.6
  55.1 4.4 %collective-permute-done.6 = bf16[1,4,8,8,128]{4,3,2,1,0:T(8,128)(2,1)S(1)} collective-permute-done((bf16[1,4,8,8,128]{4,3,2,1,0:T(8,128)(2,1)S(1)}, bf16[1,4,8,8,128]{4,3,2,1,0:T(8,128)(2,1)S(1)}, u32[]{:S(2)}, u32[]{:S(2)}) %collective-permute-start.6) | collective-permute-done | bytes 65568 | tf_op jit(solution)/shard_map/ppermute | solution.py:63
  59.6 1.3 collective-permute-start.7
  60.9 1.6 prepare.1
  62.5 0.8 slice_reduce_fusion
  63.3 1.3 collective-permute-done.7
  66.2 0.9 pad_maximum_fusion.2
  67.1 10.7 %attend.1 = (bf16[8,4,7,8,128]{4,3,2,1,0:T(8,128)(2,1)}, bf16[2,3,8,1024]{3,2,1,0:T(8,128)(2,1)}) custom-call(s32[8]{0:T(128)} %fusion.21.table, bf16[8,4,8,8,128]{4,3,2,1,0:T(8,128)(2,1)} %bitcast.79, f32[3,8,128]{2,1,0:T(8,128)} %get-tuple-element.27.cosine, f32[3,8,128]{2,1,0:T(8,128)} %get-tuple-element.28.sine, f32[24,1152]{1,0:T(8,128)} %get-tuple-element.10.bias, ...), custom_call_target="tpu_custom_call" | custom-call | tf_op jit(solution)/shard_map/attend/pallas_call | solution.py:460
  77.8 18.3 %all_to_all.16 = bf16[32,7,8,128]{3,2,1,0:T(8,128)(2,1)} all-to-all(bf16[32,7,8,128]{3,2,1,0:T(8,128)(2,1)} %bitcast.88), channel_id=1, replica_groups=mesh['z'=4,'core'=2,'branch'=4] {'z','core','branch'}, dimensions={0} | all-to-all | bytes 917504 | tf_op jit(solution)/shard_map/all_to_all | solution.py:38
  96.1 2.3 %join.1 = bf16[4,6,8,128]{3,2,1,0:T(8,128)(2,1)} custom-call(bf16[8,4,7,8,128]{4,3,2,1,0:T(8,128)(2,1)} %bitcast.82), custom_call_target="tpu_custom_call" | custom-call | tf_op jit(solution)/shard_map/join/pallas_call | solution.py:503
  98.4 5.7 %collective-permute-done.9 = bf16[1,4,6,8,128]{4,3,2,1,0:T(8,128)(2,1)S(1)} collective-permute-done((bf16[1,4,6,8,128]{4,3,2,1,0:T(8,128)(2,1)}, bf16[1,4,6,8,128]{4,3,2,1,0:T(8,128)(2,1)S(1)}, u32[]{:S(2)}, u32[]{:S(2)}) %collective-permute-start.9) | collective-permute-done | bytes 49184 | tf_op jit(solution)/shard_map/ppermute | solution.py:63
  104.1 0.8 pad_maximum_fusion.10
  105.4 4.2 %collective-permute-done.10 = bf16[2,4,6,8,128]{4,3,2,1,0:T(8,128)(2,1)S(1)} collective-permute-done((bf16[2,4,6,8,128]{4,3,2,1,0:T(8,128)(2,1)S(1)}, bf16[2,4,6,8,128]{4,3,2,1,0:T(8,128)(2,1)S(1)}, u32[]{:S(2)}, u32[]{:S(2)}) %collective-permute-start.10) | collective-permute-done | bytes 98336 | tf_op jit(solution)/shard_map/ppermute | solution.py:63
  109.6 0.8 maximum_bitcast_fusion.3
  110.5 1.4 collective-permute-done.11
  111.9 0.8 pad_maximum_fusion.3
  112.7 4.2 %mix.1 = bf16[4,3,8,1024]{3,2,1,0:T(8,128)(2,1)} custom-call(s32[8]{0:T(128)} %fusion.21.table, bf16[8,4,6,8,128]{4,3,2,1,0:T(8,128)(2,1)} %bitcast.83, bf16[2048,1024]{1,0:T(8,128)(2,1)} %w.7), custom_call_target="tpu_custom_call" | custom-call | tf_op jit(solution)/shard_map/mix/pallas_call | solution.py:265
  117.0 9.1 %all_to_all.17 = bf16[4,3,8,1024]{3,2,1,0:T(8,128)(2,1)S(1)} all-to-all(bf16[4,3,8,1024]{3,2,1,0:T(8,128)(2,1)} %mix.1), channel_id=1, replica_groups=mesh['z'=4,'core'=2,'branch'=4] {'branch'}, dimensions={0} | all-to-all | bytes 393216 | tf_op jit(solution)/shard_map/all_to_all | solution.py:38
  126.3 1.1 collective-permute-done.12
  127.9 3.1 %collective-permute-done.13 = f32[3,8]{1,0:T(4,128)S(1)} collective-permute-done((f32[3,8]{1,0:T(4,128)S(1)}, f32[3,8]{1,0:T(4,128)S(1)}, u32[]{:S(2)}, u32[]{:S(2)}) %collective-permute-start.13) | collective-permute-done | bytes 128 | tf_op jit(solution)/shard_map/ppermute | solution.py:63
  131.0 4.5 %collective-permute-done.14 = f32[3,8]{1,0:T(4,128)S(1)} collective-permute-done((f32[3,8]{1,0:T(4,128)S(1)}, f32[3,8]{1,0:T(4,128)S(1)}, u32[]{:S(2)}, u32[]{:S(2)}) %collective-permute-start.14) | collective-permute-done | bytes 128 | tf_op jit(solution)/shard_map/ppermute | solution.py:63
  135.6 0.8 collective-permute-start.15
  136.4 3.3 %collective-permute-done.15 = bf16[1,3,8,1024]{3,2,1,0:T(8,128)(2,1)S(1)} collective-permute-done((bf16[1,3,8,1024]{3,2,1,0:T(8,128)(2,1)S(1)}, bf16[1,3,8,1024]{3,2,1,0:T(8,128)(2,1)S(1)}, u32[]{:S(2)}, u32[]{:S(2)}) %collective-permute-start.15) | collective-permute-done | bytes 49184 | tf_op jit(solution)/shard_map/ppermute | solution.py:63
  139.8 0.8 collective-permute-start.16
  140.6 3.9 %collective-permute-done.16 = bf16[2,3,8,1024]{3,2,1,0:T(8,128)(2,1)S(1)} collective-permute-done((bf16[2,3,8,1024]{3,2,1,0:T(8,128)(2,1)S(1)}, bf16[2,3,8,1024]{3,2,1,0:T(8,128)(2,1)S(1)}, u32[]{:S(2)}, u32[]{:S(2)}) %collective-permute-start.16) | collective-permute-done | bytes 98336 | tf_op jit(solution)/shard_map/ppermute | solution.py:63
  144.5 7.4 %gate_up.2 = bf16[2,4,2,96,512]{4,3,2,1,0:T(8,128)(2,1)S(1)} custom-call(s32[3]{0:T(128)S(1)} %copy-done, bf16[96,1024]{1,0:T(8,128)(2,1)S(1)} %bitcast.75, bf16[2,1024,7168]{2,1,0:T(8,128)(2,1)} %w.10), custom_call_target="tpu_custom_call" | custom-call | tf_op jit(solution)/shard_map/gate_up/pallas_call | solution.py:210
  152.0 2.3 %collective-permute-done.17 = bf16[4,2,96,512]{3,2,1,0:T(8,128)(2,1)S(1)} collective-permute-done((bf16[4,2,96,512]{3,2,1,0:T(8,128)(2,1)S(1)}, bf16[4,2,96,512]{3,2,1,0:T(8,128)(2,1)S(1)}, u32[]{:S(2)}, u32[]{:S(2)}) %collective-permute-start.17) | collective-permute-done | bytes 786464 | tf_op jit(solution)/shard_map/ppermute | solution.py:63
  155.0 6.2 %gate_up.3 = bf16[2,4,2,96,384]{4,3,2,1,0:T(8,128)(2,1)S(1)} custom-call(s32[3]{0:T(128)S(1)} %copy-done, bf16[96,1024]{1,0:T(8,128)(2,1)S(1)} %bitcast.76, bf16[2,1024,7168]{2,1,0:T(8,128)(2,1)} %w.10), custom_call_target="tpu_custom_call" | custom-call | tf_op jit(solution)/shard_map/gate_up/pallas_call | solution.py:210
  161.4 4.3 %collective-permute-done.18 = bf16[2,2,96,512]{3,2,1,0:T(8,128)(2,1)S(1)} collective-permute-done((bf16[2,2,96,512]{3,2,1,0:T(8,128)(2,1)S(1)}, bf16[2,2,96,512]{3,2,1,0:T(8,128)(2,1)S(1)}, u32[]{:S(2)}, u32[]{:S(2)}) %collective-permute-start.18) | collective-permute-done | bytes 393248 | tf_op jit(solution)/shard_map/ppermute | solution.py:63
  166.2 1.5 collective-permute-start.24
  167.7 9.5 %collective-permute-done.19 = bf16[1,2,96,512]{3,2,1,0:T(8,128)(2,1)S(1)} collective-permute-done((bf16[1,2,96,512]{3,2,1,0:T(8,128)(2,1)S(1)}, bf16[1,2,96,512]{3,2,1,0:T(8,128)(2,1)S(1)}, u32[]{:S(2)}, u32[]{:S(2)}) %collective-permute-start.19) | collective-permute-done | bytes 196640 | tf_op jit(solution)/shard_map/ppermute | solution.py:63
  177.4 1.3 collective-permute-done.24
  178.8 1.7 collective-permute-start.25
  180.4 6.2 %collective-permute-done.20 = bf16[1,96,512]{2,1,0:T(8,128)(2,1)S(1)} collective-permute-done((bf16[1,96,512]{2,1,0:T(8,128)(2,1)S(1)}, bf16[1,96,512]{2,1,0:T(8,128)(2,1)S(1)}, u32[]{:S(2)}, u32[]{:S(2)}) %collective-permute-start.20) | collective-permute-done | bytes 98336 | tf_op jit(solution)/shard_map/ppermute | solution.py:63
  186.8 3.0 %collective-permute-done.25 = bf16[1,2,96,384]{3,2,1,0:T(8,128)(2,1)S(1)} collective-permute-done((bf16[1,2,96,384]{3,2,1,0:T(8,128)(2,1)S(1)}, bf16[1,2,96,384]{3,2,1,0:T(8,128)(2,1)S(1)}, u32[]{:S(2)}, u32[]{:S(2)}) %collective-permute-start.25) | collective-permute-done | bytes 147488 | tf_op jit(solution)/shard_map/ppermute | solution.py:63
  190.3 5.8 %collective-permute-done.26 = bf16[1,96,384]{2,1,0:T(8,128)(2,1)S(1)} collective-permute-done((bf16[1,96,384]{2,1,0:T(8,128)(2,1)S(1)}, bf16[1,96,384]{2,1,0:T(8,128)(2,1)S(1)}, u32[]{:S(2)}, u32[]{:S(2)}) %collective-permute-start.26) | collective-permute-done | bytes 73760 | tf_op jit(solution)/shard_map/ppermute | solution.py:63
  196.4 5.1 %collective-permute-done.27 = bf16[2,96,384]{2,1,0:T(8,128)(2,1)S(1)} collective-permute-done((bf16[2,96,384]{2,1,0:T(8,128)(2,1)S(1)}, bf16[2,96,384]{2,1,0:T(8,128)(2,1)S(1)}, u32[]{:S(2)}, u32[]{:S(2)}) %collective-permute-start.27) | collective-permute-done | bytes 147488 | tf_op jit(solution)/shard_map/ppermute | solution.py:63
  201.6 1.0 pad_maximum_fusion
  202.6 5.9 %down.2 = f32[96,1024]{1,0:T(8,128)} custom-call(s32[8]{0:T(128)} %fusion.21.table, bf16[8,96,512]{2,1,0:T(8,128)(2,1)} %bitcast.77, bf16[7168,1024]{1,0:T(8,128)(2,1)} %w.11), custom_call_target="tpu_custom_call" | custom-call | tf_op jit(solution)/shard_map/down/pallas_call | solution.py:297
  208.5 0.9 pad_maximum_fusion.1
  209.4 5.5 %down.3 = f32[96,1024]{1,0:T(8,128)} custom-call(s32[8]{0:T(128)} %fusion.21.table, bf16[8,96,384]{2,1,0:T(8,128)(2,1)} %bitcast.78, bf16[7168,1024]{1,0:T(8,128)(2,1)} %w.11), custom_call_target="tpu_custom_call" | custom-call | tf_op jit(solution)/shard_map/down/pallas_call | solution.py:297
  215.0 1.1 add_convert_fusion.2
  216.1 0.8 collective-permute-start.29
  216.9 4.5 %collective-permute-done.29 = bf16[2,3,8,1024]{3,2,1,0:T(8,128)(2,1)S(1)} collective-permute-done((bf16[2,3,8,1024]{3,2,1,0:T(8,128)(2,1)S(1)}, bf16[2,3,8,1024]{3,2,1,0:T(8,128)(2,1)S(1)}, u32[]{:S(2)}, u32[]{:S(2)}) %collective-permute-start.29) | collective-permute-done | bytes 98336 | tf_op jit(solution)/shard_map/ppermute | solution.py:63
  221.4 0.8 collective-permute-start.30
  222.2 0.7 copy.16
  223.0 2.6 %collective-permute-done.30 = bf16[1,3,8,1024]{3,2,1,0:T(8,128)(2,1)S(1)} collective-permute-done((bf16[1,3,8,1024]{3,2,1,0:T(8,128)(2,1)S(1)}, bf16[1,3,8,1024]{3,2,1,0:T(8,128)(2,1)S(1)}, u32[]{:S(2)}, u32[]{:S(2)}) %collective-permute-start.30) | collective-permute-done | bytes 49184 | tf_op jit(solution)/shard_map/ppermute | solution.py:63
  (76 shorter events, 7.5 us)
Async XLA Ops:
  1.5 1.3 collective-permute-start
  2.8 4.5 %collective-permute-start.1 = (f32[3,8]{1,0:T(4,128)S(1)}, f32[3,8]{1,0:T(4,128)S(1)}, u32[]{:S(2)}, u32[]{:S(2)}) collective-permute-start(f32[3,8]{1,0:T(4,128)S(1)} %add.98), channel_id=1, source_target_pairs={{0,8},{8,0},{16,24},{24,16},{1,9},{9,1},{17,25},{25,17},{2,10},{10... | collective-permute-start | bytes 296 | tf_op jit(solution)/shard_map/ppermute | solution.py:63
  7.3 4.6 %collective-permute-start.2 = (f32[3,8]{1,0:T(4,128)S(1)}, f32[3,8]{1,0:T(4,128)S(1)}, u32[]{:S(2)}, u32[]{:S(2)}) collective-permute-start(f32[3,8]{1,0:T(4,128)S(1)} %add.99), channel_id=1, source_target_pairs={{0,16},{8,24},{16,0},{24,8},{1,17},{9,25},{17,1},{25,9},{2,18},{10... | collective-permute-start | bytes 296 | tf_op jit(solution)/shard_map/ppermute | solution.py:63
  12.8 4.2 %collective-permute-start.3 = (bf16[1,3,8,1024]{3,2,1,0:T(8,128)(2,1)S(1)}, bf16[1,3,8,1024]{3,2,1,0:T(8,128)(2,1)S(1)}, u32[]{:S(2)}, u32[]{:S(2)}) collective-permute-start(bf16[1,3,8,1024]{3,2,1,0:T(8,128)(2,1)S(1)} %fusion.17), channel_id=1, source_target_pairs={{0,1},{1,0},{2,3},{3,2},{4,5},{5,4},{6,7},{7,6},{8,9},{9,8},{10,11... | collective-permute-start | bytes 147464 | tf_op jit(solution)/shard_map/ppermute | solution.py:63
  16.9 4.7 %collective-permute-start.4 = (bf16[2,3,8,1024]{3,2,1,0:T(8,128)(2,1)S(1)}, bf16[2,3,8,1024]{3,2,1,0:T(8,128)(2,1)S(1)}, u32[]{:S(2)}, u32[]{:S(2)}) collective-permute-start(bf16[2,3,8,1024]{3,2,1,0:T(8,128)(2,1)S(1)} %pad_maximum_fusion.9), channel_id=1, source_target_pairs={{0,2},{1,3},{2,0},{3,1},{4,6},{5,7},{6,4},{7,5},{8,10},{9,11},{10,... | collective-permute-start | bytes 294920 | tf_op jit(solution)/shard_map/ppermute | solution.py:63
  28.8 2.0 collective-permute-start.5
  54.3 5.3 %collective-permute-start.6 = (bf16[1,4,8,8,128]{4,3,2,1,0:T(8,128)(2,1)S(1)}, bf16[1,4,8,8,128]{4,3,2,1,0:T(8,128)(2,1)S(1)}, u32[]{:S(2)}, u32[]{:S(2)}) collective-permute-start(bf16[1,4,8,8,128]{4,3,2,1,0:T(8,128)(2,1)S(1)} %bitcast.85), channel_id=1, source_target_pairs={{0,16},{8,24},{16,0},{24,8},{1,17},{9,25},{17,1},{25,9},{2,18},{10... | collective-permute-start | bytes 196616 | tf_op jit(solution)/shard_map/ppermute | solution.py:63
  59.6 5.0 %collective-permute-start.7 = (bf16[2,4,8,8,128]{4,3,2,1,0:T(8,128)(2,1)S(1)}, bf16[2,4,8,8,128]{4,3,2,1,0:T(8,128)(2,1)S(1)}, u32[]{:S(2)}, u32[]{:S(2)}) collective-permute-start(bf16[2,4,8,8,128]{4,3,2,1,0:T(8,128)(2,1)S(1)} %pad_maximum_fusion.8), channel_id=1, source_target_pairs={{0,8},{8,0},{16,24},{24,16},{1,9},{9,1},{17,25},{25,17},{2,10},{10... | collective-permute-start | bytes 393224 | tf_op jit(solution)/shard_map/ppermute | solution.py:63
  64.6 1.6 collective-permute-start.8
  98.4 5.7 %collective-permute-start.9 = (bf16[1,4,6,8,128]{4,3,2,1,0:T(8,128)(2,1)}, bf16[1,4,6,8,128]{4,3,2,1,0:T(8,128)(2,1)S(1)}, u32[]{:S(2)}, u32[]{:S(2)}) collective-permute-start(bf16[1,4,6,8,128]{4,3,2,1,0:T(8,128)(2,1)} %bitcast.89), channel_id=1, source_target_pairs={{0,16},{8,24},{16,0},{24,8},{1,17},{9,25},{17,1},{25,9},{2,18},{10... | collective-permute-start | bytes 147464 | tf_op jit(solution)/shard_map/ppermute | solution.py:63
  104.9 4.7 %collective-permute-start.10 = (bf16[2,4,6,8,128]{4,3,2,1,0:T(8,128)(2,1)S(1)}, bf16[2,4,6,8,128]{4,3,2,1,0:T(8,128)(2,1)S(1)}, u32[]{:S(2)}, u32[]{:S(2)}) collective-permute-start(bf16[2,4,6,8,128]{4,3,2,1,0:T(8,128)(2,1)S(1)} %pad_maximum_fusion.10), channel_id=1, source_target_pairs={{0,8},{8,0},{16,24},{24,16},{1,9},{9,1},{17,25},{25,17},{2,10},{10... | collective-permute-start | bytes 294920 | tf_op jit(solution)/shard_map/ppermute | solution.py:63
  110.4 1.5 collective-permute-start.11
  112.7 13.4 %copy-start.2 = (bf16[3,8,1024]{2,1,0:T(8,128)(2,1)S(1)}, bf16[3,8,1024]{2,1,0:T(8,128)(2,1)}, u32[]{:S(2)}) copy-start(bf16[3,8,1024]{2,1,0:T(8,128)(2,1)} %param.13) | copy-start | bytes 147460
  112.7 22.8 %copy-start.4 = (f32[1024]{0:T(1024)S(1)}, f32[1024]{0:T(1024)}, u32[]{:S(2)}) copy-start(f32[1024]{0:T(1024)} %param.15) | copy-start | bytes 12292
  117.0 27.5 %copy-start = (s32[3]{0:T(128)S(1)}, s32[3]{0:T(128)}, u32[]{:S(2)}) copy-start(s32[3]{0:T(128)} %pad_add_fusion.ids) | copy-start | bytes 40
  126.2 1.2 collective-permute-start.12
  127.4 3.6 %collective-permute-start.13 = (f32[3,8]{1,0:T(4,128)S(1)}, f32[3,8]{1,0:T(4,128)S(1)}, u32[]{:S(2)}, u32[]{:S(2)}) collective-permute-start(f32[3,8]{1,0:T(4,128)S(1)} %add.104), channel_id=1, source_target_pairs={{0,8},{8,0},{16,24},{24,16},{1,9},{9,1},{17,25},{25,17},{2,10},{10... | collective-permute-start | bytes 296 | tf_op jit(solution)/shard_map/ppermute | solution.py:63
  131.0 4.5 %collective-permute-start.14 = (f32[3,8]{1,0:T(4,128)S(1)}, f32[3,8]{1,0:T(4,128)S(1)}, u32[]{:S(2)}, u32[]{:S(2)}) collective-permute-start(f32[3,8]{1,0:T(4,128)S(1)} %add.105), channel_id=1, source_target_pairs={{0,16},{8,24},{16,0},{24,8},{1,17},{9,25},{17,1},{25,9},{2,18},{10... | collective-permute-start | bytes 296 | tf_op jit(solution)/shard_map/ppermute | solution.py:63
  135.6 4.2 %collective-permute-start.15 = (bf16[1,3,8,1024]{3,2,1,0:T(8,128)(2,1)S(1)}, bf16[1,3,8,1024]{3,2,1,0:T(8,128)(2,1)S(1)}, u32[]{:S(2)}, u32[]{:S(2)}) collective-permute-start(bf16[1,3,8,1024]{3,2,1,0:T(8,128)(2,1)S(1)} %fusion.16), channel_id=1, source_target_pairs={{0,1},{1,0},{2,3},{3,2},{4,5},{5,4},{6,7},{7,6},{8,9},{9,8},{10,11... | collective-permute-start | bytes 147464 | tf_op jit(solution)/shard_map/ppermute | solution.py:63
  139.8 4.7 %collective-permute-start.16 = (bf16[2,3,8,1024]{3,2,1,0:T(8,128)(2,1)S(1)}, bf16[2,3,8,1024]{3,2,1,0:T(8,128)(2,1)S(1)}, u32[]{:S(2)}, u32[]{:S(2)}) collective-permute-start(bf16[2,3,8,1024]{3,2,1,0:T(8,128)(2,1)S(1)} %pad_maximum_fusion.11), channel_id=1, source_target_pairs={{0,2},{1,3},{2,0},{3,1},{4,6},{5,7},{6,4},{7,5},{8,10},{9,11},{10,... | collective-permute-start | bytes 294920 | tf_op jit(solution)/shard_map/ppermute | solution.py:63
  151.9 2.4 %collective-permute-start.17 = (bf16[4,2,96,512]{3,2,1,0:T(8,128)(2,1)S(1)}, bf16[4,2,96,512]{3,2,1,0:T(8,128)(2,1)S(1)}, u32[]{:S(2)}, u32[]{:S(2)}) collective-permute-start(bf16[4,2,96,512]{3,2,1,0:T(8,128)(2,1)S(1)} %slice_bitcast_fusion), channel_id=1, source_target_pairs={{0,4},{4,0},{1,5},{5,1},{2,6},{6,2},{3,7},{7,3},{8,12},{12,8},{9,1... | collective-permute-start | bytes 2359304 | tf_op jit(solution)/shard_map/ppermute | solution.py:63
  154.5 11.2 %collective-permute-start.18 = (bf16[2,2,96,512]{3,2,1,0:T(8,128)(2,1)S(1)}, bf16[2,2,96,512]{3,2,1,0:T(8,128)(2,1)S(1)}, u32[]{:S(2)}, u32[]{:S(2)}) collective-permute-start(bf16[2,2,96,512]{3,2,1,0:T(8,128)(2,1)S(1)} %slice.71), channel_id=1, source_target_pairs={{0,8},{8,0},{16,24},{24,16},{1,9},{9,1},{17,25},{25,17},{2,10},{10... | collective-permute-start | bytes 1179656 | tf_op jit(solution)/shard_map/ppermute | solution.py:63
  161.3 4.7 %collective-permute-start.23 = (bf16[4,2,96,384]{3,2,1,0:T(8,128)(2,1)S(1)}, bf16[4,2,96,384]{3,2,1,0:T(8,128)(2,1)S(1)}, u32[]{:S(2)}, u32[]{:S(2)}) collective-permute-start(bf16[4,2,96,384]{3,2,1,0:T(8,128)(2,1)S(1)} %slice_bitcast_fusion.2), channel_id=1, source_target_pairs={{0,4},{4,0},{1,5},{5,1},{2,6},{6,2},{3,7},{7,3},{8,12},{12,8},{9,1... | collective-permute-start | bytes 1769480 | tf_op jit(solution)/shard_map/ppermute | solution.py:63
  165.9 11.3 %collective-permute-start.19 = (bf16[1,2,96,512]{3,2,1,0:T(8,128)(2,1)S(1)}, bf16[1,2,96,512]{3,2,1,0:T(8,128)(2,1)S(1)}, u32[]{:S(2)}, u32[]{:S(2)}) collective-permute-start(bf16[1,2,96,512]{3,2,1,0:T(8,128)(2,1)S(1)} %slice.90), channel_id=1, source_target_pairs={{0,16},{8,24},{16,0},{24,8},{1,17},{9,25},{17,1},{25,9},{2,18},{10... | collective-permute-start | bytes 589832 | tf_op jit(solution)/shard_map/ppermute | solution.py:63
  166.2 12.5 %collective-permute-start.24 = (bf16[2,2,96,384]{3,2,1,0:T(8,128)(2,1)S(1)}, bf16[2,2,96,384]{3,2,1,0:T(8,128)(2,1)S(1)}, u32[]{:S(2)}, u32[]{:S(2)}) collective-permute-start(bf16[2,2,96,384]{3,2,1,0:T(8,128)(2,1)S(1)} %slice.77), channel_id=1, source_target_pairs={{0,8},{8,0},{16,24},{24,16},{1,9},{9,1},{17,25},{25,17},{2,10},{10... | collective-permute-start | bytes 884744 | tf_op jit(solution)/shard_map/ppermute | solution.py:63
  177.3 9.4 %collective-permute-start.20 = (bf16[1,96,512]{2,1,0:T(8,128)(2,1)S(1)}, bf16[1,96,512]{2,1,0:T(8,128)(2,1)S(1)}, u32[]{:S(2)}, u32[]{:S(2)}) collective-permute-start(bf16[1,96,512]{2,1,0:T(8,128)(2,1)S(1)} %fusion.4), channel_id=1, source_target_pairs={{0,16},{8,24},{16,0},{24,8},{1,17},{9,25},{17,1},{25,9},{2,18},{10... | collective-permute-start | bytes 294920 | tf_op jit(solution)/shard_map/ppermute | solution.py:63
  178.8 11.0 %collective-permute-start.25 = (bf16[1,2,96,384]{3,2,1,0:T(8,128)(2,1)S(1)}, bf16[1,2,96,384]{3,2,1,0:T(8,128)(2,1)S(1)}, u32[]{:S(2)}, u32[]{:S(2)}) collective-permute-start(bf16[1,2,96,384]{3,2,1,0:T(8,128)(2,1)S(1)} %slice.94), channel_id=1, source_target_pairs={{0,16},{8,24},{16,0},{24,8},{1,17},{9,25},{17,1},{25,9},{2,18},{10... | collective-permute-start | bytes 442376 | tf_op jit(solution)/shard_map/ppermute | solution.py:63
  186.7 9.6 %collective-permute-start.21 = (bf16[2,96,512]{2,1,0:T(8,128)(2,1)S(1)}, bf16[2,96,512]{2,1,0:T(8,128)(2,1)S(1)}, u32[]{:S(2)}, u32[]{:S(2)}) collective-permute-start(bf16[2,96,512]{2,1,0:T(8,128)(2,1)S(1)} %pad_maximum_fusion.6), channel_id=1, source_target_pairs={{0,8},{8,0},{16,24},{24,16},{1,9},{9,1},{17,25},{25,17},{2,10},{10... | collective-permute-start | bytes 589832 | tf_op jit(solution)/shard_map/ppermute | solution.py:63
  189.9 6.3 %collective-permute-start.26 = (bf16[1,96,384]{2,1,0:T(8,128)(2,1)S(1)}, bf16[1,96,384]{2,1,0:T(8,128)(2,1)S(1)}, u32[]{:S(2)}, u32[]{:S(2)}) collective-permute-start(bf16[1,96,384]{2,1,0:T(8,128)(2,1)S(1)} %fusion.7), channel_id=1, source_target_pairs={{0,16},{8,24},{16,0},{24,8},{1,17},{9,25},{17,1},{25,9},{2,18},{10... | collective-permute-start | bytes 221192 | tf_op jit(solution)/shard_map/ppermute | solution.py:63
  196.2 5.3 %collective-permute-start.27 = (bf16[2,96,384]{2,1,0:T(8,128)(2,1)S(1)}, bf16[2,96,384]{2,1,0:T(8,128)(2,1)S(1)}, u32[]{:S(2)}, u32[]{:S(2)}) collective-permute-start(bf16[2,96,384]{2,1,0:T(8,128)(2,1)S(1)} %pad_maximum_fusion.7), channel_id=1, source_target_pairs={{0,8},{8,0},{16,24},{24,16},{1,9},{9,1},{17,25},{25,17},{2,10},{10... | collective-permute-start | bytes 442376 | tf_op jit(solution)/shard_map/ppermute | solution.py:63
  196.3 5.3 %collective-permute-start.22 = (bf16[1,4,96,512]{3,2,1,0:T(8,128)(2,1)S(1)}, bf16[1,4,96,512]{3,2,1,0:T(8,128)(2,1)S(1)}, u32[]{:S(2)}, u32[]{:S(2)}) collective-permute-start(bf16[1,4,96,512]{3,2,1,0:T(8,128)(2,1)S(1)} %maximum_bitcast_fusion), channel_id=1, source_target_pairs={{0,4},{4,0},{1,5},{5,1},{2,6},{6,2},{3,7},{7,3},{8,12},{12,8},{9,1... | collective-permute-start | bytes 1179656 | tf_op jit(solution)/shard_map/ppermute | solution.py:63
  201.5 7.0 %collective-permute-start.28 = (bf16[1,4,96,384]{3,2,1,0:T(8,128)(2,1)S(1)}, bf16[1,4,96,384]{3,2,1,0:T(8,128)(2,1)S(1)}, u32[]{:S(2)}, u32[]{:S(2)}) collective-permute-start(bf16[1,4,96,384]{3,2,1,0:T(8,128)(2,1)S(1)} %maximum_bitcast_fusion.1), channel_id=1, source_target_pairs={{0,4},{4,0},{1,5},{5,1},{2,6},{6,2},{3,7},{7,3},{8,12},{12,8},{9,1... | collective-permute-start | bytes 884744 | tf_op jit(solution)/shard_map/ppermute | solution.py:63
  209.4 5.6 %copy-start.1 = (f32[96,1024]{1,0:T(8,128)S(1)}, f32[96,1024]{1,0:T(8,128)}, u32[]{:S(2)}) copy-start(f32[96,1024]{1,0:T(8,128)} %down.2) | copy-start | bytes 1179652
  215.0 7.2 %copy-start.3 = (bf16[2,3,8,1024]{3,2,1,0:T(8,128)(2,1)S(1)}, bf16[2,3,8,1024]{3,2,1,0:T(8,128)(2,1)}, u32[]{:S(2)}) copy-start(bf16[2,3,8,1024]{3,2,1,0:T(8,128)(2,1)} %get-tuple-element.15) | copy-start | bytes 294916
  216.1 5.2 %collective-permute-start.29 = (bf16[2,3,8,1024]{3,2,1,0:T(8,128)(2,1)S(1)}, bf16[2,3,8,1024]{3,2,1,0:T(8,128)(2,1)S(1)}, u32[]{:S(2)}, u32[]{:S(2)}) collective-permute-start(bf16[2,3,8,1024]{3,2,1,0:T(8,128)(2,1)S(1)} %bitcast.94), channel_id=1, source_target_pairs={{0,2},{1,3},{2,0},{3,1},{4,6},{5,7},{6,4},{7,5},{8,10},{9,11},{10,... | collective-permute-start | bytes 294920 | tf_op jit(solution)/shard_map/ppermute | solution.py:63
  221.4 4.2 %collective-permute-start.30 = (bf16[1,3,8,1024]{3,2,1,0:T(8,128)(2,1)S(1)}, bf16[1,3,8,1024]{3,2,1,0:T(8,128)(2,1)S(1)}, u32[]{:S(2)}, u32[]{:S(2)}) collective-permute-start(bf16[1,3,8,1024]{3,2,1,0:T(8,128)(2,1)S(1)} %slice.98), channel_id=1, source_target_pairs={{0,1},{1,0},{2,3},{3,2},{4,5},{5,4},{6,7},{7,6},{8,9},{9,8},{10,11... | collective-permute-start | bytes 147464 | tf_op jit(solution)/shard_map/ppermute | solution.py:63

commit v3 on v2

v3 whole, which is shorter than its diff:
```python
import functools

import jax
import jax.numpy as jnp
import numpy as np
from jax import lax
from jax.experimental import pallas as pl
from jax.experimental.pallas import tpu as pltpu
from jax.sharding import Mesh
from jax.sharding import PartitionSpec as P

HEADS = 64
KVH = 8
HD = 128
GROUP = HEADS // KVH
BLK = 512
CORES = 2
SUB = 8
LANE = 128

EPS = 1e-05
ROPE_BASE = 500000.0
FLOOR = -1e30
LOWEST = -1e29
F32 = jnp.float32
BF16 = jnp.bfloat16
AXES = ("z", "core", "branch")


def ceil_div(a, b):
    return -(-a // b)


def whole(shape):
    return pl.BlockSpec(shape, lambda *_: (0,) * len(shape))


def cost(rows, w):
    return pl.CostEstimate(
        flops=2 * rows * w[0] * w[1], bytes_accessed=2 * w[0] * w[1], transcendentals=0
    )


def exchange(x, axes):
    return lax.all_to_all(x, axes, split_axis=0, concat_axis=0, tiled=True)


def params(mib):
    return pltpu.CompilerParams(vmem_limit_bytes=mib * 2**20)


IN_HBM = pl.BlockSpec(memory_space=pltpu.HBM)
IN_VMEM = pl.BlockSpec(memory_space=pltpu.VMEM)
IN_SMEM = pl.BlockSpec(memory_space=pltpu.SMEM)


def bits(n):
    return [1 << i for i in range(n.bit_length() - 1)]


def mirror(q, n):
    out = 0
    top = n.bit_length() - 2
    for i in range(top + 1):
        out = out + (((q >> i) & 1) << (top - i))
    return out


def swap(x, axis, bit):
    return lax.ppermute(x, axis, [(i, i ^ bit) for i in range(lax.axis_size(axis))])


def reduce_rounds(x, axis, order):
    for bit in order:
        half = x.shape[0] // 2
        x = x[:half] + swap(x[half:], axis, bit)
    return x[0]


def gather_rounds(x, axis, order):
    x = x[None]
    for bit in order:
        x = jnp.concatenate([x, swap(x, axis, bit)], axis=0)
    return x


def add_round(x, axis, order):
    for bit in order:
        half = x.shape[0] // 2
        kept = x[:half].astype(F32)
        kept = kept + swap(x[half:], axis, bit).astype(F32)
        x = kept.astype(BF16)
    return kept[0]


def add(a, b):
    return (a.astype(F32) + b.astype(F32)).astype(BF16)


def as_tile(x):
    return jnp.pad(x, ((0, -x.shape[0] % SUB), (0, LANE - x.shape[1])))


def normed(x, squares, gain, width):
    scale = lax.rsqrt(squares / width + EPS)
    return (x * scale[..., None] * gain).astype(BF16)


def norm_rows(x, gain, width):
    value = x.astype(F32)
    squares = jnp.sum(value * value, axis=3)
    total = as_tile(squares.reshape(-1, squares.shape[-1]))
    total = total + swap(total, "core", 1)
    for bit in bits(lax.axis_size("z")):
        total = total + swap(total, "z", bit)
    total = total[: squares.shape[0] * squares.shape[1], : squares.shape[2]].reshape(squares.shape)
    return normed(value, total, gain, width).reshape(-1, x.shape[3])


def sum_round(x, bit):
    other = swap(x, "branch", bit).astype(F32)
    shape = other.shape
    other = jnp.flip(other.reshape((shape[0] // (2 * bit), 2, bit) + shape[1:]), axis=1)
    return x.astype(F32) + other.reshape(shape)


def sum_branches(first, second):
    order = bits(lax.axis_size("branch"))
    for one, two in zip(order, order[::-1]):
        first, second = sum_round(first.astype(BF16), one), sum_round(second.astype(BF16), two)
    return jnp.concatenate([first, second], axis=-1)


def own_sum(x):
    n = x.shape[0]
    if n > 4:
        return add_round(x, "branch", bits(n)[::-1])
    arrived = [swap(x[k], "branch", k) for k in range(1, n)]
    return functools.reduce(jnp.add, [a.astype(F32) for a in [x[0]] + arrived])


def gather_prefix(x):
    x = gather_rounds(x, "z", bits(lax.axis_size("z"))[::-1])
    x = gather_rounds(x, "core", [1])
    return x.reshape((-1,) + x.shape[2:])


def place_table():
    z_count = lax.axis_size("z")
    owner = jnp.arange(z_count * CORES, dtype=jnp.int32)
    far = mirror((owner // CORES) ^ lax.axis_index("z"), z_count)
    return (((owner % CORES) ^ lax.axis_index("core")) * z_count + far).astype(jnp.int32)


def key_head(head):
    return head // GROUP if head < HEADS else (head - HEADS) % KVH


def ranks(heads_each, branches):
    rank, most = {}, 0
    for b in range(branches):
        count = [0] * CORES
        for head in range(b * heads_each, (b + 1) * heads_each):
            core = key_head(head) % CORES
            rank[head] = count[core]
            count[core] += 1
        most = max(most, *count)
    return rank, most


def head_tables(steps, z_count, branches):
    heads_in = (HEADS + 2 * KVH) // branches
    heads_out = HEADS // branches
    rank_in, most = ranks(heads_in, branches)
    tiles_in = ceil_div(most * steps, z_count)
    rank_out, most = ranks(heads_out, branches)
    tiles_out = ceil_div(most * steps, z_count)
    kv_core = KVH // CORES
    project = np.zeros((branches, heads_in), np.int32)
    for head, rank in rank_in.items():
        project[head // heads_in, head % heads_in] = rank * steps * CORES + key_head(head) % CORES
    fetch = np.zeros((z_count, CORES, kv_core, GROUP + 2, steps), np.int32)
    send = np.zeros((CORES, kv_core, GROUP, steps), np.int32)
    mix = np.zeros((z_count, CORES, branches, heads_out, steps), np.int32)
    for s in range(steps):
        for core in range(CORES):
            for j in range(kv_core):
                key = j * CORES + core
                heads = [key * GROUP + g for g in range(GROUP)] + [HEADS + key, HEADS + KVH + key]
                for n, head in enumerate(heads):
                    chip, tile = divmod(rank_in[head] * steps + s, tiles_in)
                    for z in range(z_count):
                        row = mirror(chip ^ z, z_count) * branches + head // heads_in
                        fetch[z, core, j, n, s] = row * tiles_in + tile
                    if head < HEADS:
                        chip, tile = divmod(rank_out[head] * steps + s, tiles_out)
                        row = chip * branches + head // heads_out
                        send[core, j, n, s] = row * LANE + tile
        for head, rank in rank_out.items():
            chip, tile = divmod(rank * steps + s, tiles_out)
            for z in range(z_count):
                for core in range(CORES):
                    side = (key_head(head) % CORES) ^ core
                    row = side * z_count + mirror(chip ^ z, z_count)
                    mix[z, core, head // heads_out, head % heads_out, s] = row * LANE + tile
    full = (z_count, CORES, branches)
    parts = [
        np.broadcast_to(project[None, None], full + project.shape[1:]),
        np.broadcast_to(fetch.reshape(z_count, CORES, 1, -1), full + (fetch[0, 0].size,)),
        np.broadcast_to(send.reshape(1, CORES, 1, -1), full + (send[0].size,)),
        mix.reshape(full + (-1,)),
    ]
    starts = np.cumsum([0] + [p.shape[-1] for p in parts]).tolist()
    return tiles_in, tiles_out, np.concatenate(parts, axis=-1), starts


def streamed(count, ahead, copies, work):
    for i in range(min(ahead, count)):
        for c in copies(i):
            c.start()

    def step(i, carry):
        for c in copies(i):
            c.wait()

        @pl.when(i + ahead < count)
        def _():
            for c in copies(i + ahead):
                c.start()

        work(i)
        return carry

    lax.fori_loop(0, count, step, 0)


def qkv_kernel(steps, heads_step, tiles, ids, table, lhs, w, out):
    columns = heads_step * HD
    branches = out.shape[2]
    for i in range(w.shape[1] // columns):
        acc = jnp.dot(
            lhs[...], w[:, i * columns : (i + 1) * columns], preferred_element_type=F32
        )
        for hh in range(heads_step):
            code = table[i * heads_step + hh]
            side = (code % CORES) ^ ids[1]
            for s in range(steps):
                index = code // CORES + s
                for k in range(branches):
                    row = (k * steps + s) * SUB
                    out[side, index // tiles, ids[2] ^ k, index % tiles] = acc[
                        row : row + SUB, hh * HD : (hh + 1) * HD
                    ]


def project_qkv(ids, table, lhs, w, steps, z_count, branches, tiles):
    heads = w.shape[1] // HD
    heads_step = max(n for n in range(1, 5) if heads % n == 0)
    shape = (CORES, z_count, branches, tiles, SUB, HD)
    return pl.pallas_call(
        functools.partial(qkv_kernel, steps, heads_step, tiles),
        in_specs=[IN_SMEM, IN_SMEM, IN_VMEM, IN_VMEM],
        out_shape=jax.ShapeDtypeStruct(shape, F32),
        compiler_params=params(24),
        cost_estimate=cost(lhs.shape[0], w.shape),
        name="qkv",
    )(ids, table, lhs, w)


def gate_up_kernel(unit, start, ids, lhs, w, out, buffer, sems):
    count = buffer.shape[0]
    part = buffer.shape[3]
    z_count = out.shape[1]

    def copies(i):
        at = pl.multiple_of(i * unit + start, LANE)
        return [
            pltpu.make_async_copy(w.at[g, :, pl.ds(at, part)], buffer.at[i, g], sems.at[i, g])
            for g in range(2)
        ]

    def work(i):
        side = (i % CORES) ^ ids[1]
        far = mirror((i // CORES) ^ ids[0], z_count)
        for g in range(2):
            product = jnp.dot(lhs[...], buffer[i, g], preferred_element_type=F32)
            out[side, far, g] = product.astype(BF16)

    streamed(count, 3, copies, work)


def project_gate_up(ids, lhs, w, unit, start, part, z_count):
    rows = lhs.shape[0]
    _, depth, columns = w.shape
    count = columns // unit
    shape = (CORES, z_count, 2, rows, part)
    return pl.pallas_call(
        functools.partial(gate_up_kernel, unit, start),
        in_specs=[IN_SMEM, IN_VMEM, IN_HBM],
        out_shape=jax.ShapeDtypeStruct(shape, BF16),
        scratch_shapes=[
            pltpu.VMEM((count, 2, depth, part), BF16),
            pltpu.SemaphoreType.DMA((count, 2)),
        ],
        compiler_params=params(32),
        cost_estimate=cost(rows, (depth, 2 * count * part)),
        name="gate_up",
    )(ids, lhs, w)


def mix_kernel(steps, base, ids, table, attended, w, first, second, lhs):
    unit = min(first.shape[3], 256)
    count = w.shape[1] // unit
    for j in range(lhs.shape[1] // HD):
        codes = [table[base + j * steps + s] for s in range(steps)]
        column = [
            attended[code // LANE, ids[2] ^ k, code % LANE].astype(F32)
            for k in range(first.shape[0])
            for code in codes
        ]
        lhs[:, j * HD : (j + 1) * HD] = jnp.concatenate(column, axis=0).astype(BF16)
    for i in range(count):
        acc = jnp.dot(lhs[...], w[:, i * unit : (i + 1) * unit], preferred_element_type=F32)
        out = first if i < count // 2 else second
        at = slice(i % (count // 2) * unit, (i % (count // 2) + 1) * unit)
        out[:, :, :, at] = acc.reshape(out.shape[:3] + (unit,)).astype(BF16)


def mix_heads(ids, table, base, attended, w, steps):
    branches = attended.shape[1]
    depth, columns = w.shape
    rows = branches * steps * SUB
    half = jax.ShapeDtypeStruct((branches, steps, SUB, columns // 2), BF16)
    return pl.pallas_call(
        functools.partial(mix_kernel, steps, base),
        in_specs=[IN_SMEM, IN_SMEM, IN_VMEM, IN_VMEM],
        out_shape=[half, half],
        scratch_shapes=[pltpu.VMEM((rows, depth), BF16)],
        compiler_params=params(24),
        cost_estimate=cost(rows, w.shape),
        name="mix",
    )(ids, table, attended, w)


def down_kernel(unit, start, table, *refs):
    *prior, activation, w, out, acc, buffer, sems = refs
    part = buffer.shape[1]
    acc[...] = prior[0][...] if prior else jnp.zeros_like(acc)

    def copies(i):
        at = pl.multiple_of(i * unit + start, LANE)
        return [pltpu.make_async_copy(w.at[pl.ds(at, part), :], buffer.at[i], sems.at[i])]

    def work(i):
        acc[...] += jnp.dot(activation[table[i]], buffer[i], preferred_element_type=F32)

    streamed(buffer.shape[0], min(6, buffer.shape[0]), copies, work)
    out[...] = acc[...].reshape(out.shape).astype(out.dtype)


def project_down(table, prior, activation, w, unit, start, shape):
    rows, part = activation.shape[1:]
    columns = w.shape[1]
    count = w.shape[0] // unit
    last = shape is not None
    result = (shape, BF16) if last else ((rows, columns), F32)
    return pl.pallas_call(
        functools.partial(down_kernel, unit, start),
        in_specs=[IN_SMEM] + [IN_VMEM] * (len(prior) + 1) + [IN_HBM],
        out_specs=IN_VMEM,
        out_shape=jax.ShapeDtypeStruct(*result),
        scratch_shapes=[
            pltpu.VMEM((rows, columns), F32),
            pltpu.VMEM((count, part, columns), BF16),
            pltpu.SemaphoreType.DMA((count,)),
        ],
        compiler_params=params(52),
        cost_estimate=cost(rows, (count * part, columns)),
        name="down",
    )(table, *prior, activation, w)


def prepare_kernel(steps, blocks_here, suffix_here, ids, parent, block_map, leaf, length, pos, bias):
    rows = leaf.shape[0]
    places = [ids[0] * CORES + (ids[1] ^ side) for side in range(CORES)]
    slots = [place * blocks_here + n for place in places for n in range(blocks_here)]
    sub = lax.broadcasted_iota(jnp.int32, (SUB, LANE), 0)
    base = jnp.zeros((SUB, LANE), jnp.int32)
    used = jnp.zeros((SUB, LANE), jnp.int32)
    owned = [jnp.zeros((SUB, LANE), jnp.int32) for _ in slots]
    for r in range(rows):
        current = leaf[r]
        depth = jnp.int32(0)
        hits = [jnp.int32(0)] * len(slots)
        for _ in range(parent.shape[0]):
            valid = current >= 0
            at = jnp.maximum(current, 0)
            found = jnp.where(valid, block_map[at], -1)
            hits = [h + (found == slot).astype(jnp.int32) for slot, h in zip(slots, hits)]
            depth = depth + valid.astype(jnp.int32)
            current = jnp.where(valid, parent[at], -1)
        base = jnp.where(sub == r, BLK * depth + length[r], base)
        used = jnp.where(sub == r, length[r], used)
        owned = [jnp.where(sub == r, h, o) for h, o in zip(hits, owned)]
    keys = SUB * suffix_here
    key_row = lax.broadcasted_iota(jnp.int32, (SUB, keys), 0)
    key = lax.broadcasted_iota(jnp.int32, (SUB, keys), 1)
    columns = [
        jnp.broadcast_to(jnp.where(o[:, :1] > 0, 0.0, FLOOR), (SUB, BLK)) for o in owned
    ]
    for place in places:
        ok = (key // suffix_here == key_row) & (
            place * suffix_here + key % suffix_here < used[:, :1]
        )
        columns.append(jnp.where(ok, 0.0, FLOOR))
    shared = jnp.concatenate(columns, axis=1)
    start = shared.shape[1]
    lane = lax.broadcasted_iota(jnp.int32, (SUB, LANE), 1)
    for s in range(steps):
        pos[s] = (base + s).astype(F32)
        row = slice(s * SUB, (s + 1) * SUB)
        bias[row, :start] = shared
        new_ok = (lane % SUB == sub) & (lane // SUB <= s) & (ids[0] == 0)
        bias[row, start : start + LANE] = jnp.where(new_ok, 0.0, FLOOR)


def prepare(ids, parent, block_map, leaf, length, steps, blocks_here, suffix_here):
    columns = CORES * (blocks_here * BLK + SUB * suffix_here) + LANE
    return pl.pallas_call(
        functools.partial(prepare_kernel, steps, blocks_here, suffix_here),
        in_specs=[IN_SMEM] * 5,
        out_specs=[IN_VMEM, IN_VMEM],
        out_shape=[
            jax.ShapeDtypeStruct((steps, SUB, LANE), F32),
            jax.ShapeDtypeStruct((steps * SUB, columns), F32),
        ],
        cost_estimate=pl.CostEstimate(flops=2**22, bytes_accessed=2**20, transcendentals=0),
        name="prepare",
    )(ids, parent, block_map, leaf, length)


def attend_kernel(
    fetch, send, table, qkv, cosine, sine, bias, tree, tree_two, suffix, suffix_two, out, new_kv, sums
):
    steps = cosine.shape[0]
    rows = steps * SUB
    tiles_out = out.shape[1] - 1
    kv_core = KVH // CORES
    lane = lax.broadcasted_iota(jnp.int32, (SUB, LANE), 1)
    sums[...] = jnp.zeros_like(sums)

    def turned(x, s):
        return x * cosine[s] + pltpu.roll(x, HD // 2, 1) * sine[s]

    for j in range(kv_core):

        def tile(n, s):
            return qkv[table[fetch + (j * (GROUP + 2) + n) * steps + s]].astype(F32)

        query = jnp.concatenate(
            [turned(tile(g, s), s) for g in range(GROUP) for s in range(steps)], axis=0
        ).astype(BF16)
        keys = [turned(tile(GROUP, s), s) for s in range(steps)]
        values = [tile(GROUP + 1, s) for s in range(steps)]
        at = slice(j * HD, (j + 1) * HD)
        for s in range(steps):
            new_kv[0, s, :, at] = keys[s].astype(BF16)
            new_kv[1, s, :, at] = values[s].astype(BF16)
        fill = [jnp.zeros((LANE - rows, HD), F32)]
        sources = [
            (kv[:, 0, :, at].reshape(-1, HD), kv[:, 1, :, at].reshape(-1, HD))
            for kv in (tree, tree_two, suffix, suffix_two)
        ]
        sources.append(
            (
                jnp.concatenate(keys + fill, axis=0).astype(BF16),
                jnp.concatenate(values + fill, axis=0).astype(BF16),
            )
        )
        scores = []
        start = 0
        highest = jnp.full((GROUP, rows, 1), LOWEST, F32)
        for key, _ in sources:
            count = key.shape[0]
            product = lax.dot_general(
                query, key, (((1,), (1,)), ((), ())), preferred_element_type=F32
            ) * (HD**-0.5)
            product = product.reshape(GROUP, rows, count) + bias[:, start : start + count][None]
            highest = jnp.maximum(highest, jnp.max(product, axis=-1, keepdims=True))
            scores.append(product)
            start += count
        total = jnp.zeros((GROUP, rows, 1), F32)
        acc = jnp.zeros((GROUP * rows, HD), F32)
        for product, (_, value) in zip(scores, sources):
            weight = jnp.exp(product - highest)
            total = total + jnp.sum(weight, axis=-1, keepdims=True)
            acc = acc + jnp.dot(
                weight.reshape(GROUP * rows, -1).astype(BF16), value, preferred_element_type=F32
            )
        some = total > 0
        safe = jnp.where(some, total, 1.0)
        result = acc.reshape(GROUP, rows, HD) / safe
        log_sum = jnp.where(some, highest + jnp.log(safe), LOWEST)
        for g in range(GROUP):
            for s in range(steps):
                code = table[send + (j * GROUP + g) * steps + s]
                place, t = code // LANE, code % LANE
                row = slice(s * SUB, (s + 1) * SUB)
                out[place, t] = result[g, row].astype(BF16)
                sums[place] = jnp.where(lane == t, log_sum[g, row], sums[place])

    for p in range(sums.shape[0]):
        out[p, tiles_out] = pack_sums(sums[p])


def pack_sums(value):
    lane = lax.broadcasted_iota(jnp.int32, (SUB, LANE), 1)
    high = value.astype(BF16).astype(F32)
    rest = value - high
    middle = rest.astype(BF16).astype(F32)
    low = rest - middle
    lows = jnp.where(lane < 64, pltpu.roll(middle, 32, 1), pltpu.roll(low, 64, 1))
    return jnp.where(lane < 32, high, lows).astype(BF16)


def attend(table, fetch, send, qkv, cosine, sine, bias, sources, devices, tiles):
    steps = cosine.shape[0]
    kv_core = KVH // CORES
    shape = (devices, tiles + 1, SUB, HD)
    return pl.pallas_call(
        functools.partial(attend_kernel, fetch, send),
        in_specs=[IN_SMEM] + [IN_VMEM] * 8,
        out_specs=[IN_VMEM, IN_VMEM],
        out_shape=[
            jax.ShapeDtypeStruct(shape, BF16),
            jax.ShapeDtypeStruct((2, steps, SUB, kv_core * HD), BF16),
        ],
        scratch_shapes=[pltpu.VMEM((devices, SUB, LANE), F32)],
        compiler_params=params(32),
        cost_estimate=pl.CostEstimate(
            flops=2**30, bytes_accessed=2 * sum(a.size for a in sources), transcendentals=2**21
        ),
        name="attend",
    )(table, qkv, cosine, sine, bias, *sources)


def trade_heads(kv):
    heads = [kv[..., n * HD : (n + 1) * HD] for n in range(KVH)]
    even = jnp.concatenate(heads[0::CORES], axis=-1)
    odd = jnp.concatenate(heads[1::CORES], axis=-1)
    first = lax.axis_index("core") == 0
    return [jnp.where(first, even, odd), swap(jnp.where(first, odd, even), "core", 1)]


def both_cores(own):
    other = swap(own, "core", 1)
    first = lax.axis_index("core") == 0
    even, odd = jnp.where(first, own, other), jnp.where(first, other, own)
    count = own.shape[-1] // HD
    spans = [slice(n * HD, (n + 1) * HD) for n in range(count)]
    return jnp.concatenate([x[..., at] for at in spans for x in (even, odd)], axis=-1)


def join_kernel(parts, out):
    prefix, branches, count = parts.shape[:3]
    tiles = count - 1
    for b in range(branches):
        logs = []
        for p in range(prefix):
            packed = parts[p, b, tiles].astype(F32)
            logs.append(packed + pltpu.roll(packed, LANE - 32, 1) + pltpu.roll(packed, LANE - 64, 1))
        highest = functools.reduce(jnp.maximum, logs)
        weights = [jnp.exp(x - highest) for x in logs]
        total = functools.reduce(jnp.add, weights)
        weights = [w / total for w in weights]
        for t in range(tiles):
            acc = jnp.zeros((SUB, HD), F32)
            for p in range(prefix):
                acc = acc + parts[p, b, t].astype(F32) * weights[p][:, t : t + 1]
            out[b, t] = acc.astype(BF16)


def join(parts):
    _, branches, count = parts.shape[:3]
    return pl.pallas_call(
        join_kernel,
        in_specs=[IN_VMEM],
        out_specs=IN_VMEM,
        out_shape=jax.ShapeDtypeStruct((branches, count - 1, SUB, HD), BF16),
        name="join",
    )(parts)


def body(
    hidden,
    attn_gain,
    ffn_gain,
    w_qkv,
    w_out,
    w_gate_up,
    w_down,
    tree_kv,
    suffix_kv,
    parent,
    block_map,
    leaf,
    suffix_len,
):
    steps, rows, width_dev = hidden.shape
    z_count = lax.axis_size("z")
    branches = lax.axis_size("branch")
    prefix = z_count * CORES
    width = width_dev * prefix
    near = bits(z_count)
    across = bits(branches)
    places = place_table()
    ids = jnp.stack([lax.axis_index(a) for a in AXES]).astype(jnp.int32)

    tiles_in, tiles_out, table, (_, fetch, send, mix, _) = head_tables(steps, z_count, branches)
    table = jnp.asarray(table)[tuple(lax.axis_index(a) for a in AXES)]
    pos, bias = prepare(
        ids, parent, block_map, leaf, suffix_len, steps, tree_kv.shape[0], suffix_kv.shape[2]
    )
    half = HD // 2
    frequency = ROPE_BASE ** (-(jnp.arange(half, dtype=F32) * 2.0 / HD))
    angles = pos[..., :1] * frequency
    cos, sin = jnp.cos(angles), jnp.sin(angles)
    cosine = jnp.concatenate([cos, cos], axis=-1)
    sine = jnp.concatenate([-sin, sin], axis=-1)

    every_row = gather_rounds(hidden, "branch", across)
    lhs = norm_rows(every_row, attn_gain, width)
    sources = trade_heads(tree_kv) + trade_heads(suffix_kv)
    lhs, table, sources, cosine, sine, bias = lax.optimization_barrier(
        (lhs, table, sources, cosine, sine, bias)
    )
    part_sums = project_qkv(ids, table, lhs, w_qkv, steps, z_count, branches, tiles_in)
    chip_sums = part_sums[0] + swap(part_sums[1], "core", 1)
    plane = z_count * branches
    received = exchange(chip_sums.reshape(plane, tiles_in, SUB, HD), ("z", "branch"))
    summed = jnp.sum(received.reshape(z_count, branches, tiles_in, SUB, HD), axis=0).astype(BF16)
    qkv = gather_rounds(summed, "z", near[::-1]).reshape(-1, SUB, HD)

    softmax_parts, new_kv = attend(
        table, fetch, send, qkv, cosine, sine, bias, sources, plane, tiles_out
    )
    received = exchange(softmax_parts, ("z", "branch"))
    attended = join(received.reshape(z_count, branches, tiles_out + 1, SUB, HD))
    attended = gather_prefix(attended)
    new_kv = both_cores(new_kv).transpose(2, 0, 1, 3)

    mixed = sum_branches(*mix_heads(ids, table, mix, attended, w_out, steps))
    residual = (every_row.astype(F32) + mixed).astype(BF16)
    lhs = norm_rows(residual, ffn_gain, width)

    unit = ceil_div(w_gate_up.shape[2] // LANE, prefix) * LANE
    first = ceil_div(unit // LANE, 2) * LANE
    spans = [(at, size) for at, size in ((0, first), (first, unit - first)) if size]
    down = []
    for start, part in spans:
        part_sums = project_gate_up(ids, lhs, w_gate_up, unit, start, part, z_count)
        chip_sums = add(part_sums[0], swap(part_sums[1], "core", 1))
        lhs, chip_sums = lax.optimization_barrier((lhs, chip_sums))
        gate, up = add_round(chip_sums, "z", near)
        activation = gather_prefix((jax.nn.silu(gate) * up).astype(BF16))
        shape = (branches, steps, rows, width_dev) if start == spans[-1][0] else None
        down = [project_down(places, down, activation, w_down, unit, start, shape)]
    result = (residual[0].astype(F32) + own_sum(down[0])).astype(BF16)
    return (result, new_kv)


def solution(mesh):
    prefix, branches = mesh.shape["prefix"], mesh.shape["branch"]
    split = Mesh(mesh.devices.reshape(prefix // CORES, CORES, branches), AXES)
    along = ("z", "core")
    placed = (
        P(None, "branch", along),
        P(along),
        P(along),
        P(along, "branch"),
        P("branch", along),
        P(None, along, "branch"),
        P("branch", along),
        P(along, None, None, None),
        P("branch", None, along, None),
        P(),
        P(),
        P("branch"),
        P("branch"),
    )
    return jax.shard_map(
        body,
        mesh=split,
        in_specs=placed,
        out_specs=(P(None, "branch", along), P("branch", None, None, None)),
        check_vma=False,
    )
```

time: 227 us -> 204 us (0.90)
  Pallas kernels: 49.3 us -> 34.1 us
  blocking collectives: 49.8 us -> 35.2 us
  local copies, waits for them, and re-layouts: 2.86 us -> 10.4 us
  starting transfers between devices: 21.5 us -> 24.2 us
    all_to_all x3 -> x2, blocking collectives: 49.8 us -> 35.2 us  [exchange(): return lax.all_to_all(x, axes, split_axis=0, concat_axis=0, tiled=True)]
    pallas_call x2, Pallas kernels: 14.9 us -> 6.25 us  [the longest x1 4.71 us: attend(): pl.pallas_call(functools.partial(attend_kernel, fetch, send), in_specs=[I...]
    unnamed x11 -> x32, local copies, waits for them, and re-layouts: 0.76 us -> 6.13 us
    select_n x0 -> x3, other arithmetic: none -> 3.64 us  [the longest x2 3.63 us: trade_heads(): jnp.where(first, odd, even)]
    pallas_call x1, Pallas kernels: 5.36 us -> 2.03 us  [project_qkv(): pl.pallas_call(functools.partial(qkv_kernel, steps, heads_step, tiles), i...]
    pallas_call x2, Pallas kernels: 11.5 us -> 8.63 us  [project_down(): pl.pallas_call(functools.partial(down_kernel, unit, start), in_specs=[IN_...]
    ppermute x31 -> x36, starting transfers between devices: 21.5 us -> 24.2 us  [swap(): lax.ppermute(x, axis, [(i, i ^ bit) for i in range(lax.axis_size(axis))])]
    slice x0 -> x2, local copies, waits for them, and re-layouts: none -> 2.28 us  [trade_heads(): heads = [kv[..., n * HD:(n + 1) * HD] for n in range(KVH)]]
  transfers between devices with their start and end apart: 31 -> 36, of which waited for: 27 -> 28; matrix products, arithmetic and copies ran while one was open for 2% -> 5% of each run, Pallas kernels for 6% -> 10%
where the time goes in v3:
time: 204 us
  waiting for transfers between devices  86.4 us (42%)
  blocking collectives  35.2 us (17%)
  Pallas kernels  34.1 us (17%)
  starting transfers between devices  24.2 us (12%)
  other arithmetic  12 us (6%)
  local copies, waits for them, and re-layouts  10.4 us (5%)
    ppermute x36, waiting for transfers between devices, swap(): lax.ppermute(x, axis, [(i, i ^ bit) for i in range(lax.axis_size(axis))])  86.4 us
    all_to_all x2, blocking collectives, exchange(): return lax.all_to_all(x, axes, split_axis=0, concat_axis=0, tiled=True)  35.2 us
    ppermute x36, starting transfers between devices, swap(): lax.ppermute(x, axis, [(i, i ^ bit) for i in range(lax.axis_size(axis))])  24.2 us
    pallas_call x2, Pallas kernels, project_gate_up(): pl.pallas_call(functools.partial(gate_up_kernel, unit, start), in_specs=[...  13.6 us
    pallas_call x2, Pallas kernels, project_down(): pl.pallas_call(functools.partial(down_kernel, unit, start), in_specs=[IN_...  8.63 us
    unnamed x32, local copies, waits for them, and re-layouts  6.13 us
    pallas_call x1, Pallas kernels, attend(): pl.pallas_call(functools.partial(attend_kernel, fetch, send), in_specs=[I...  4.71 us
  transfers between devices with their start and end apart: 36, of which 28 were waited for; matrix products, arithmetic and copies ran while one was open for 5% of the time, Pallas kernels for 10%

profile of v3, /device:TPU:0, one launch (start us, length us, event | category | flops | bytes accessed | tf_op | source)
XLA Modules:
  0.0 203.7 jit_solution(17093231989942899167)
XLA Ops:
  0.6 3.0 %collective-permute-start = (bf16[1,3,8,1024]{3,2,1,0:T(8,128)(2,1)}, bf16[1,3,8,1024]{3,2,1,0:T(8,128)(2,1)S(1)}, u32[]{:S(2)}, u32[]{:S(2)}) collective-permute-start(bf16[1,3,8,1024]{3,2,1,0:T(8,128)(2,1)} %bitcast.117), channel_id=1, source_target_pairs={{0,1},{1,0},{2,3},{3,2},{4,5},{5,4},{6,7},{7,6},{8,9},{9,8},{10,11... | collective-permute-start | bytes 147464 | tf_op jit(solution)/shard_map/ppermute | solution.py:70
  3.6 1.7 fusion.31
  5.4 1.7 broadcast_select_fusion.2
  7.7 1.9 broadcast_select_fusion
  10.7 1.7 prepare.1
  12.5 1.6 collective-permute-start.1
  14.1 0.8 slice_reduce_fusion
  14.9 2.4 %collective-permute-done.1 = bf16[2,3,8,1024]{3,2,1,0:T(8,128)(2,1)S(1)} collective-permute-done((bf16[2,3,8,1024]{3,2,1,0:T(8,128)(2,1)S(1)}, bf16[2,3,8,1024]{3,2,1,0:T(8,128)(2,1)S(1)}, u32[]{:S(2)}, u32[]{:S(2)}) %collective-permute-start.1) | collective-permute-done | bytes 98336 | tf_op jit(solution)/shard_map/ppermute | solution.py:70
  17.5 1.1 collective-permute-done.2
  18.6 1.6 collective-permute-start.3
  20.4 1.9 collective-permute-done.3
  22.3 2.6 %collective-permute-start.4 = (f32[16,128]{1,0:T(8,128)S(1)}, f32[16,128]{1,0:T(8,128)S(1)}, u32[]{:S(2)}, u32[]{:S(2)}) collective-permute-start(f32[16,128]{1,0:T(8,128)S(1)} %add.134), channel_id=1, source_target_pairs={{0,16},{8,24},{16,0},{24,8},{1,17},{9,25},{17,1},{25,9},{2,18},{10... | collective-permute-start | bytes 24584 | tf_op jit(solution)/shard_map/ppermute | solution.py:70
  25.7 1.2 collective-permute-done.4
  27.1 2.5 %copy-done = bf16[1024,2560]{1,0:T(8,128)(2,1)S(1)} copy-done((bf16[1024,2560]{1,0:T(8,128)(2,1)S(1)}, bf16[1024,2560]{1,0:T(8,128)(2,1)}, u32[]{:S(2)}) %copy-start) | copy-done | bytes 5242904
  30.2 2.0 qkv.1
  32.4 2.0 collective-permute-done.7
  34.4 23.6 %all_to_all.10 = f32[16,9,8,128]{3,2,1,0:T(8,128)} all-to-all(f32[16,9,8,128]{3,2,1,0:T(8,128)S(1)} %bitcast.113), channel_id=1, replica_groups=mesh['z'=4,'core'=2,'branch'=4] {'z','branch'}, dimensions={0} | all-to-all | bytes 1179648 | tf_op jit(solution)/shard_map/all_to_all | solution.py:45
  58.1 1.7 reduce_sum.28
  60.3 5.7 %collective-permute-done.8 = bf16[1,4,9,8,128]{4,3,2,1,0:T(8,128)(2,1)S(1)} collective-permute-done((bf16[1,4,9,8,128]{4,3,2,1,0:T(8,128)(2,1)}, bf16[1,4,9,8,128]{4,3,2,1,0:T(8,128)(2,1)S(1)}, u32[]{:S(2)}, u32[]{:S(2)}) %collective-permute-start.8) | collective-permute-done | bytes 73760 | tf_op jit(solution)/shard_map/ppermute | solution.py:70
  66.1 0.9 pad_maximum_fusion.10
  67.0 5.1 %collective-permute-done.9 = bf16[2,4,9,8,128]{4,3,2,1,0:T(8,128)(2,1)S(1)} collective-permute-done((bf16[2,4,9,8,128]{4,3,2,1,0:T(8,128)(2,1)S(1)}, bf16[2,4,9,8,128]{4,3,2,1,0:T(8,128)(2,1)S(1)}, u32[]{:S(2)}, u32[]{:S(2)}) %collective-permute-start.9) | collective-permute-done | bytes 147488 | tf_op jit(solution)/shard_map/ppermute | solution.py:70
  72.2 0.9 pad_maximum_fusion.7
  73.1 4.7 %attend.1 = (bf16[16,7,8,128]{3,2,1,0:T(8,128)(2,1)S(1)}, bf16[2,3,8,512]{3,2,1,0:T(8,128)(2,1)S(1)}) custom-call(s32[284]{0:T(512)S(1)} %dynamic-slice_reduce_fusion.table, bf16[144,8,128]{2,1,0:T(8,128)(2,1)S(1)} %bitcast.112, f32[3,8,128]{2,1,0:T(8,128)S(1)} %get-tuple-element.24.cosine, f32[3,8,128]{2,1,0:T(8,128)S(1)} %get-tuple-element.25.sine, ...), custom_call_target="tpu_custom_call" | custom-call | flops 1073741824 | bytes 4194304 | tf_op jit(solution)/shard_map/attend/pallas_call | solution.py:530
  77.8 11.6 %all_to_all.11 = bf16[16,7,8,128]{3,2,1,0:T(8,128)(2,1)} all-to-all(bf16[16,7,8,128]{3,2,1,0:T(8,128)(2,1)S(1)} %get-tuple-element.31), channel_id=1, replica_groups=mesh['z'=4,'core'=2,'branch'=4] {'z','branch'}, dimensions={0} | all-to-all | bytes 458752 | tf_op jit(solution)/shard_map/all_to_all | solution.py:45
  89.4 1.9 join.1
  91.3 1.0 collective-permute-start.10
  92.3 4.7 %collective-permute-done.10 = bf16[1,4,6,8,128]{4,3,2,1,0:T(8,128)(2,1)S(1)} collective-permute-done((bf16[1,4,6,8,128]{4,3,2,1,0:T(8,128)(2,1)}, bf16[1,4,6,8,128]{4,3,2,1,0:T(8,128)(2,1)S(1)}, u32[]{:S(2)}, u32[]{:S(2)}) %collective-permute-start.10) | collective-permute-done | bytes 49184 | tf_op jit(solution)/shard_map/ppermute | solution.py:70
  97.0 0.8 pad_maximum_fusion.13
  98.2 4.3 %collective-permute-done.11 = bf16[2,4,6,8,128]{4,3,2,1,0:T(8,128)(2,1)S(1)} collective-permute-done((bf16[2,4,6,8,128]{4,3,2,1,0:T(8,128)(2,1)S(1)}, bf16[2,4,6,8,128]{4,3,2,1,0:T(8,128)(2,1)S(1)}, u32[]{:S(2)}, u32[]{:S(2)}) %collective-permute-start.11) | collective-permute-done | bytes 98336 | tf_op jit(solution)/shard_map/ppermute | solution.py:70
  102.5 0.8 maximum_bitcast_fusion.2
  103.4 1.4 collective-permute-done.12
  104.9 2.2 %copy-done.1 = bf16[2048,1024]{1,0:T(8,128)(2,1)S(1)} copy-done((bf16[2048,1024]{1,0:T(8,128)(2,1)S(1)}, bf16[2048,1024]{1,0:T(8,128)(2,1)}, u32[]{:S(2)}) %copy-start.1) | copy-done | bytes 4194328
  107.1 1.5 mix.1
  108.7 0.9 collective-permute-start.13
  110.0 3.6 %collective-permute-done.13 = bf16[4,3,8,512]{3,2,1,0:T(8,128)(2,1)S(1)} collective-permute-done((bf16[4,3,8,512]{3,2,1,0:T(8,128)(2,1)S(1)}, bf16[4,3,8,512]{3,2,1,0:T(8,128)(2,1)S(1)}, u32[]{:S(2)}, u32[]{:S(2)}) %collective-permute-start.13) | collective-permute-done | bytes 98336 | tf_op jit(solution)/shard_map/ppermute | solution.py:70
  113.6 0.8 collective-permute-start.14
  114.5 1.0 collective-permute-start.16
  115.5 2.8 %collective-permute-done.14 = bf16[4,3,8,512]{3,2,1,0:T(8,128)(2,1)S(1)} collective-permute-done((bf16[4,3,8,512]{3,2,1,0:T(8,128)(2,1)S(1)}, bf16[4,3,8,512]{3,2,1,0:T(8,128)(2,1)S(1)}, u32[]{:S(2)}, u32[]{:S(2)}) %collective-permute-start.14) | collective-permute-done | bytes 98336 | tf_op jit(solution)/shard_map/ppermute | solution.py:70
  118.4 0.8 collective-permute-done.16
  119.5 1.2 collective-permute-done.17
  121.1 3.2 %collective-permute-done.18 = f32[16,128]{1,0:T(8,128)S(1)} collective-permute-done((f32[16,128]{1,0:T(8,128)S(1)}, f32[16,128]{1,0:T(8,128)S(1)}, u32[]{:S(2)}, u32[]{:S(2)}) %collective-permute-start.18) | collective-permute-done | bytes 8224 | tf_op jit(solution)/shard_map/ppermute | solution.py:70
  124.3 0.8 collective-permute-start.19
  125.0 3.8 %collective-permute-done.19 = f32[16,128]{1,0:T(8,128)S(1)} collective-permute-done((f32[16,128]{1,0:T(8,128)S(1)}, f32[16,128]{1,0:T(8,128)S(1)}, u32[]{:S(2)}, u32[]{:S(2)}) %collective-permute-start.19) | collective-permute-done | bytes 8224 | tf_op jit(solution)/shard_map/ppermute | solution.py:70
  129.1 7.4 %gate_up.2 = bf16[2,4,2,96,512]{4,3,2,1,0:T(8,128)(2,1)S(1)} custom-call(s32[3]{0:T(128)S(1)} %copy-done.4, bf16[96,1024]{1,0:T(8,128)(2,1)S(1)} %multiply_convert_fusion.lhs, bf16[2,1024,7168]{2,1,0:T(8,128)(2,1)} %w.7), custom_call_target="tpu_custom_call" | custom-call | flops 1610612736 | bytes 16777216 | tf_op jit(solution)/shard_map/gate_up/pallas_call | solution.py:297
  136.6 2.2 %collective-permute-done.20 = bf16[4,2,96,512]{3,2,1,0:T(8,128)(2,1)S(1)} collective-permute-done((bf16[4,2,96,512]{3,2,1,0:T(8,128)(2,1)S(1)}, bf16[4,2,96,512]{3,2,1,0:T(8,128)(2,1)S(1)}, u32[]{:S(2)}, u32[]{:S(2)}) %collective-permute-start.20) | collective-permute-done | bytes 786464 | tf_op jit(solution)/shard_map/ppermute | solution.py:70
  139.6 6.2 %gate_up.3 = bf16[2,4,2,96,384]{4,3,2,1,0:T(8,128)(2,1)S(1)} custom-call(s32[3]{0:T(128)S(1)} %copy-done.4, bf16[96,1024]{1,0:T(8,128)(2,1)S(1)} %multiply_convert_fusion.lhs, bf16[2,1024,7168]{2,1,0:T(8,128)(2,1)} %w.7), custom_call_target="tpu_custom_call" | custom-call | flops 1207959552 | bytes 12582912 | tf_op jit(solution)/shard_map/gate_up/pallas_call | solution.py:297
  146.0 4.3 %collective-permute-done.21 = bf16[2,2,96,512]{3,2,1,0:T(8,128)(2,1)S(1)} collective-permute-done((bf16[2,2,96,512]{3,2,1,0:T(8,128)(2,1)S(1)}, bf16[2,2,96,512]{3,2,1,0:T(8,128)(2,1)S(1)}, u32[]{:S(2)}, u32[]{:S(2)}) %collective-permute-start.21) | collective-permute-done | bytes 393248 | tf_op jit(solution)/shard_map/ppermute | solution.py:70
  150.4 0.8 collective-permute-start.22
  151.4 1.6 collective-permute-start.27
  153.1 8.7 %collective-permute-done.22 = bf16[1,2,96,512]{3,2,1,0:T(8,128)(2,1)S(1)} collective-permute-done((bf16[1,2,96,512]{3,2,1,0:T(8,128)(2,1)S(1)}, bf16[1,2,96,512]{3,2,1,0:T(8,128)(2,1)S(1)}, u32[]{:S(2)}, u32[]{:S(2)}) %collective-permute-start.22) | collective-permute-done | bytes 196640 | tf_op jit(solution)/shard_map/ppermute | solution.py:70
  161.9 1.7 collective-permute-done.27
  163.8 1.2 collective-permute-start.28
  165.0 6.9 %collective-permute-done.23 = bf16[1,96,512]{2,1,0:T(8,128)(2,1)S(1)} collective-permute-done((bf16[1,96,512]{2,1,0:T(8,128)(2,1)S(1)}, bf16[1,96,512]{2,1,0:T(8,128)(2,1)S(1)}, u32[]{:S(2)}, u32[]{:S(2)}) %collective-permute-start.23) | collective-permute-done | bytes 98336 | tf_op jit(solution)/shard_map/ppermute | solution.py:70
  172.0 3.0 %collective-permute-done.28 = bf16[1,2,96,384]{3,2,1,0:T(8,128)(2,1)S(1)} collective-permute-done((bf16[1,2,96,384]{3,2,1,0:T(8,128)(2,1)S(1)}, bf16[1,2,96,384]{3,2,1,0:T(8,128)(2,1)S(1)}, u32[]{:S(2)}, u32[]{:S(2)}) %collective-permute-start.28) | collective-permute-done | bytes 147488 | tf_op jit(solution)/shard_map/ppermute | solution.py:70
  175.2 4.5 %collective-permute-done.24 = bf16[2,96,512]{2,1,0:T(8,128)(2,1)S(1)} collective-permute-done((bf16[2,96,512]{2,1,0:T(8,128)(2,1)S(1)}, bf16[2,96,512]{2,1,0:T(8,128)(2,1)S(1)}, u32[]{:S(2)}, u32[]{:S(2)}) %collective-permute-start.24) | collective-permute-done | bytes 196640 | tf_op jit(solution)/shard_map/ppermute | solution.py:70
  179.9 1.8 collective-permute-done.29
  181.8 5.3 %collective-permute-done.30 = bf16[2,96,384]{2,1,0:T(8,128)(2,1)S(1)} collective-permute-done((bf16[2,96,384]{2,1,0:T(8,128)(2,1)S(1)}, bf16[2,96,384]{2,1,0:T(8,128)(2,1)S(1)}, u32[]{:S(2)}, u32[]{:S(2)}) %collective-permute-start.30) | collective-permute-done | bytes 147488 | tf_op jit(solution)/shard_map/ppermute | solution.py:70
  187.4 4.6 %down.2.refs_0_ = f32[96,1024]{1,0:T(8,128)S(1)} custom-call(s32[8]{0:T(128)S(1)} %fusion.27.table, bf16[8,96,512]{2,1,0:T(8,128)(2,1)S(1)} %bitcast.109, bf16[7168,1024]{1,0:T(8,128)(2,1)} %refs_2_.1), custom_call_target="tpu_custom_call" | custom-call | flops 805306368 | bytes 8388608 | tf_op jit(solution)/shard_map/down/pallas_call | solution.py:367
  192.0 4.0 %down.3 = bf16[4,3,8,1024]{3,2,1,0:T(8,128)(2,1)S(1)} custom-call(s32[8]{0:T(128)S(1)} %fusion.27.table, f32[96,1024]{1,0:T(8,128)S(1)} %down.2.refs_0_, bf16[8,96,384]{2,1,0:T(8,128)(2,1)S(1)} %bitcast.110, bf16[7168,1024]{1,0:T(8,128)(2,1)} %refs_2_.1), custom_call_target="tpu_custom_call" | custom-call | flops 603979776 | bytes 6291456 | tf_op jit(solution)/shard_map/down/pallas_call | solution.py:367
  196.1 0.9 collective-permute-start.32
  197.0 1.8 collective-permute-start.34
  198.8 0.9 collective-permute-start.33
  200.7 1.4 collective-permute-done.34
  202.0 1.0 collective-permute-done.33
  (119 shorter events, 10.5 us)
Async XLA Ops:
  0.6 11.8 %collective-permute-start = (bf16[1,3,8,1024]{3,2,1,0:T(8,128)(2,1)}, bf16[1,3,8,1024]{3,2,1,0:T(8,128)(2,1)S(1)}, u32[]{:S(2)}, u32[]{:S(2)}) collective-permute-start(bf16[1,3,8,1024]{3,2,1,0:T(8,128)(2,1)} %bitcast.117), channel_id=1, source_target_pairs={{0,1},{1,0},{2,3},{3,2},{4,5},{5,4},{6,7},{7,6},{8,9},{9,8},{10,11... | collective-permute-start | bytes 147464 | tf_op jit(solution)/shard_map/ppermute | solution.py:70
  5.4 1.7 copy-start.5
  7.1 20.0 %collective-permute-start.5 = (bf16[1,2,512,512]{3,2,1,0:T(8,128)(2,1)}, bf16[1,2,512,512]{3,2,1,0:T(8,128)(2,1)S(1)}, u32[]{:S(2)}, u32[]{:S(2)}) collective-permute-start(bf16[1,2,512,512]{3,2,1,0:T(8,128)(2,1)} %get-tuple-element.54), channel_id=1, source_target_pairs={{0,4},{4,0},{1,5},{5,1},{2,6},{6,2},{3,7},{7,3},{8,12},{12,8},{9,1... | collective-permute-start | bytes 3145736 | tf_op jit(solution)/shard_map/ppermute | solution.py:70
  7.7 4.8 %copy-start.6 = (bf16[3,8,1024]{2,1,0:T(8,128)(2,1)S(1)}, bf16[3,8,1024]{2,1,0:T(8,128)(2,1)}, u32[]{:S(2)}) copy-start(bf16[3,8,1024]{2,1,0:T(8,128)(2,1)} %param.14) | copy-start | bytes 147460
  7.7 19.3 %copy-start.10 = (f32[1024]{0:T(1024)S(1)}, f32[1024]{0:T(1024)}, u32[]{:S(2)}) copy-start(f32[1024]{0:T(1024)} %param.15) | copy-start | bytes 12292
  9.6 17.5 %collective-permute-start.6 = (bf16[8,2,64,512]{3,2,1,0:T(8,128)(2,1)}, bf16[8,2,64,512]{3,2,1,0:T(8,128)(2,1)}, u32[]{:S(2)}, u32[]{:S(2)}) collective-permute-start(bf16[8,2,64,512]{3,2,1,0:T(8,128)(2,1)} %get-tuple-element.44), channel_id=1, source_target_pairs={{0,4},{4,0},{1,5},{5,1},{2,6},{6,2},{3,7},{7,3},{8,12},{12,8},{9,1... | collective-permute-start | bytes 3145736 | tf_op jit(solution)/shard_map/ppermute | solution.py:70
  12.5 19.8 %copy-start.8 = (bf16[1,3,8,1024]{3,2,1,0:T(8,128)(2,1)}, bf16[1,3,8,1024]{3,2,1,0:T(8,128)(2,1)S(1)}, u32[]{:S(2)}) copy-start(bf16[1,3,8,1024]{3,2,1,0:T(8,128)(2,1)S(1)} %collective-permute-done) | copy-start | bytes 147460
  12.5 4.8 %collective-permute-start.1 = (bf16[2,3,8,1024]{3,2,1,0:T(8,128)(2,1)S(1)}, bf16[2,3,8,1024]{3,2,1,0:T(8,128)(2,1)S(1)}, u32[]{:S(2)}, u32[]{:S(2)}) collective-permute-start(bf16[2,3,8,1024]{3,2,1,0:T(8,128)(2,1)S(1)} %pad_maximum_fusion.12), channel_id=1, source_target_pairs={{0,2},{1,3},{2,0},{3,1},{4,6},{5,7},{6,4},{7,5},{8,10},{9,11},{10,... | collective-permute-start | bytes 294920 | tf_op jit(solution)/shard_map/ppermute | solution.py:70
  17.4 1.2 collective-permute-start.2
  18.6 3.7 %collective-permute-start.3 = (f32[16,128]{1,0:T(8,128)S(1)}, f32[16,128]{1,0:T(8,128)S(1)}, u32[]{:S(2)}, u32[]{:S(2)}) collective-permute-start(f32[16,128]{1,0:T(8,128)S(1)} %pad_add_fusion.2), channel_id=1, source_target_pairs={{0,8},{8,0},{16,24},{24,16},{1,9},{9,1},{17,25},{25,17},{2,10},{10... | collective-permute-start | bytes 24584 | tf_op jit(solution)/shard_map/ppermute | solution.py:70
  22.3 4.5 %collective-permute-start.4 = (f32[16,128]{1,0:T(8,128)S(1)}, f32[16,128]{1,0:T(8,128)S(1)}, u32[]{:S(2)}, u32[]{:S(2)}) collective-permute-start(f32[16,128]{1,0:T(8,128)S(1)} %add.134), channel_id=1, source_target_pairs={{0,16},{8,24},{16,0},{24,8},{1,17},{9,25},{17,1},{25,9},{2,18},{10... | collective-permute-start | bytes 24584 | tf_op jit(solution)/shard_map/ppermute | solution.py:70
  27.1 2.5 %copy-start = (bf16[1024,2560]{1,0:T(8,128)(2,1)S(1)}, bf16[1024,2560]{1,0:T(8,128)(2,1)}, u32[]{:S(2)}) copy-start(bf16[1024,2560]{1,0:T(8,128)(2,1)} %w.4) | copy-start | bytes 15728644
  29.6 0.6 copy-start.3
  32.3 40.8 %copy-start.2 = (f32[24,2176]{1,0:T(8,128)S(1)}, f32[24,2176]{1,0:T(8,128)}, u32[]{:S(2)}) copy-start(f32[24,2176]{1,0:T(8,128)} %get-tuple-element.26.bias) | copy-start | bytes 626692
  32.3 2.1 %collective-permute-start.7 = (f32[4,4,9,8,128]{4,3,2,1,0:T(8,128)S(1)}, f32[4,4,9,8,128]{4,3,2,1,0:T(8,128)S(1)}, u32[]{:S(2)}, u32[]{:S(2)}) collective-permute-start(f32[4,4,9,8,128]{4,3,2,1,0:T(8,128)S(1)} %slice_bitcast_fusion.4), channel_id=1, source_target_pairs={{0,4},{4,0},{1,5},{5,1},{2,6},{6,2},{3,7},{7,3},{8,12},{12,8},{9,1... | collective-permute-start | bytes 1769480 | tf_op jit(solution)/shard_map/ppermute | solution.py:70
  59.8 6.3 %collective-permute-start.8 = (bf16[1,4,9,8,128]{4,3,2,1,0:T(8,128)(2,1)}, bf16[1,4,9,8,128]{4,3,2,1,0:T(8,128)(2,1)S(1)}, u32[]{:S(2)}, u32[]{:S(2)}) collective-permute-start(bf16[1,4,9,8,128]{4,3,2,1,0:T(8,128)(2,1)} %bitcast.124), channel_id=1, source_target_pairs={{0,16},{8,24},{16,0},{24,8},{1,17},{9,25},{17,1},{25,9},{2,18},{10... | collective-permute-start | bytes 221192 | tf_op jit(solution)/shard_map/ppermute | solution.py:70
  67.0 5.2 %collective-permute-start.9 = (bf16[2,4,9,8,128]{4,3,2,1,0:T(8,128)(2,1)S(1)}, bf16[2,4,9,8,128]{4,3,2,1,0:T(8,128)(2,1)S(1)}, u32[]{:S(2)}, u32[]{:S(2)}) collective-permute-start(bf16[2,4,9,8,128]{4,3,2,1,0:T(8,128)(2,1)S(1)} %pad_maximum_fusion.10), channel_id=1, source_target_pairs={{0,8},{8,0},{16,24},{24,16},{1,9},{9,1},{17,25},{25,17},{2,10},{10... | collective-permute-start | bytes 442376 | tf_op jit(solution)/shard_map/ppermute | solution.py:70
  77.8 27.1 %copy-start.4 = (s32[3]{0:T(128)S(1)}, s32[3]{0:T(128)}, u32[]{:S(2)}) copy-start(s32[3]{0:T(128)} %pad_add_fusion.ids) | copy-start | bytes 40
  91.3 5.7 %collective-permute-start.10 = (bf16[1,4,6,8,128]{4,3,2,1,0:T(8,128)(2,1)}, bf16[1,4,6,8,128]{4,3,2,1,0:T(8,128)(2,1)S(1)}, u32[]{:S(2)}, u32[]{:S(2)}) collective-permute-start(bf16[1,4,6,8,128]{4,3,2,1,0:T(8,128)(2,1)} %bitcast.127), channel_id=1, source_target_pairs={{0,16},{8,24},{16,0},{24,8},{1,17},{9,25},{17,1},{25,9},{2,18},{10... | collective-permute-start | bytes 147464 | tf_op jit(solution)/shard_map/ppermute | solution.py:70
  97.8 4.7 %collective-permute-start.11 = (bf16[2,4,6,8,128]{4,3,2,1,0:T(8,128)(2,1)S(1)}, bf16[2,4,6,8,128]{4,3,2,1,0:T(8,128)(2,1)S(1)}, u32[]{:S(2)}, u32[]{:S(2)}) collective-permute-start(bf16[2,4,6,8,128]{4,3,2,1,0:T(8,128)(2,1)S(1)} %pad_maximum_fusion.13), channel_id=1, source_target_pairs={{0,8},{8,0},{16,24},{24,16},{1,9},{9,1},{17,25},{25,17},{2,10},{10... | collective-permute-start | bytes 294920 | tf_op jit(solution)/shard_map/ppermute | solution.py:70
  103.3 1.5 collective-permute-start.12
  104.9 2.2 %copy-start.1 = (bf16[2048,1024]{1,0:T(8,128)(2,1)S(1)}, bf16[2048,1024]{1,0:T(8,128)(2,1)}, u32[]{:S(2)}) copy-start(bf16[2048,1024]{1,0:T(8,128)(2,1)} %w.5) | copy-start | bytes 12582916
  108.6 10.5 %copy-start.7 = (bf16[3,8,1024]{2,1,0:T(8,128)(2,1)S(1)}, bf16[3,8,1024]{2,1,0:T(8,128)(2,1)}, u32[]{:S(2)}) copy-start(bf16[3,8,1024]{2,1,0:T(8,128)(2,1)} %param.14) | copy-start | bytes 147460
  108.7 10.5 %copy-start.9 = (bf16[1,3,8,1024]{3,2,1,0:T(8,128)(2,1)S(1)}, bf16[1,3,8,1024]{3,2,1,0:T(8,128)(2,1)}, u32[]{:S(2)}) copy-start(bf16[1,3,8,1024]{3,2,1,0:T(8,128)(2,1)} %copy-done.8) | copy-start | bytes 147460
  108.7 20.3 %copy-start.11 = (f32[1024]{0:T(1024)S(1)}, f32[1024]{0:T(1024)}, u32[]{:S(2)}) copy-start(f32[1024]{0:T(1024)} %param.16) | copy-start | bytes 12292
  108.7 4.9 %collective-permute-start.13 = (bf16[4,3,8,512]{3,2,1,0:T(8,128)(2,1)S(1)}, bf16[4,3,8,512]{3,2,1,0:T(8,128)(2,1)S(1)}, u32[]{:S(2)}, u32[]{:S(2)}) collective-permute-start(bf16[4,3,8,512]{3,2,1,0:T(8,128)(2,1)S(1)} %get-tuple-element.32), channel_id=1, source_target_pairs={{0,1},{1,0},{2,3},{3,2},{4,5},{5,4},{6,7},{7,6},{8,9},{9,8},{10,11... | collective-permute-start | bytes 294920 | tf_op jit(solution)/shard_map/ppermute | solution.py:70
  109.5 4.9 %collective-permute-start.15 = (bf16[4,3,8,512]{3,2,1,0:T(8,128)(2,1)S(1)}, bf16[4,3,8,512]{3,2,1,0:T(8,128)(2,1)S(1)}, u32[]{:S(2)}, u32[]{:S(2)}) collective-permute-start(bf16[4,3,8,512]{3,2,1,0:T(8,128)(2,1)S(1)} %get-tuple-element.33), channel_id=1, source_target_pairs={{0,2},{1,3},{2,0},{3,1},{4,6},{5,7},{6,4},{7,5},{8,10},{9,11},{10,... | collective-permute-start | bytes 294920 | tf_op jit(solution)/shard_map/ppermute | solution.py:70
  113.6 4.7 %collective-permute-start.14 = (bf16[4,3,8,512]{3,2,1,0:T(8,128)(2,1)S(1)}, bf16[4,3,8,512]{3,2,1,0:T(8,128)(2,1)S(1)}, u32[]{:S(2)}, u32[]{:S(2)}) collective-permute-start(bf16[4,3,8,512]{3,2,1,0:T(8,128)(2,1)S(1)} %fusion.11), channel_id=1, source_target_pairs={{0,2},{1,3},{2,0},{3,1},{4,6},{5,7},{6,4},{7,5},{8,10},{9,11},{10,... | collective-permute-start | bytes 294920 | tf_op jit(solution)/shard_map/ppermute | solution.py:70
  114.5 4.7 %collective-permute-start.16 = (bf16[4,3,8,512]{3,2,1,0:T(8,128)(2,1)S(1)}, bf16[4,3,8,512]{3,2,1,0:T(8,128)(2,1)S(1)}, u32[]{:S(2)}, u32[]{:S(2)}) collective-permute-start(bf16[4,3,8,512]{3,2,1,0:T(8,128)(2,1)S(1)} %fusion.10), channel_id=1, source_target_pairs={{0,1},{1,0},{2,3},{3,2},{4,5},{5,4},{6,7},{7,6},{8,9},{9,8},{10,11... | collective-permute-start | bytes 294920 | tf_op jit(solution)/shard_map/ppermute | solution.py:70
  119.4 1.2 collective-permute-start.17
  120.6 3.7 %collective-permute-start.18 = (f32[16,128]{1,0:T(8,128)S(1)}, f32[16,128]{1,0:T(8,128)S(1)}, u32[]{:S(2)}, u32[]{:S(2)}) collective-permute-start(f32[16,128]{1,0:T(8,128)S(1)} %pad_add_fusion.1), channel_id=1, source_target_pairs={{0,8},{8,0},{16,24},{24,16},{1,9},{9,1},{17,25},{25,17},{2,10},{10... | collective-permute-start | bytes 24584 | tf_op jit(solution)/shard_map/ppermute | solution.py:70
  124.3 4.5 %collective-permute-start.19 = (f32[16,128]{1,0:T(8,128)S(1)}, f32[16,128]{1,0:T(8,128)S(1)}, u32[]{:S(2)}, u32[]{:S(2)}) collective-permute-start(f32[16,128]{1,0:T(8,128)S(1)} %add.151), channel_id=1, source_target_pairs={{0,16},{8,24},{16,0},{24,8},{1,17},{9,25},{17,1},{25,9},{2,18},{10... | collective-permute-start | bytes 24584 | tf_op jit(solution)/shard_map/ppermute | solution.py:70
  125.0 11.5 %collective-permute-start.35 = (bf16[2,3,8,512]{3,2,1,0:T(8,128)(2,1)S(1)}, bf16[2,3,8,512]{3,2,1,0:T(8,128)(2,1)S(1)}, u32[]{:S(2)}, u32[]{:S(2)}) collective-permute-start(bf16[2,3,8,512]{3,2,1,0:T(8,128)(2,1)S(1)} %get-tuple-element.37), channel_id=1, source_target_pairs={{0,4},{4,0},{1,5},{5,1},{2,6},{6,2},{3,7},{7,3},{8,12},{12,8},{9,1... | collective-permute-start | bytes 147464 | tf_op jit(solution)/shard_map/ppermute | solution.py:70
  136.5 2.4 %collective-permute-start.20 = (bf16[4,2,96,512]{3,2,1,0:T(8,128)(2,1)S(1)}, bf16[4,2,96,512]{3,2,1,0:T(8,128)(2,1)S(1)}, u32[]{:S(2)}, u32[]{:S(2)}) collective-permute-start(bf16[4,2,96,512]{3,2,1,0:T(8,128)(2,1)S(1)} %slice_bitcast_fusion), channel_id=1, source_target_pairs={{0,4},{4,0},{1,5},{5,1},{2,6},{6,2},{3,7},{7,3},{8,12},{12,8},{9,1... | collective-permute-start | bytes 2359304 | tf_op jit(solution)/shard_map/ppermute | solution.py:70
  139.1 11.2 %collective-permute-start.21 = (bf16[2,2,96,512]{3,2,1,0:T(8,128)(2,1)S(1)}, bf16[2,2,96,512]{3,2,1,0:T(8,128)(2,1)S(1)}, u32[]{:S(2)}, u32[]{:S(2)}) collective-permute-start(bf16[2,2,96,512]{3,2,1,0:T(8,128)(2,1)S(1)} %slice.167), channel_id=1, source_target_pairs={{0,8},{8,0},{16,24},{24,16},{1,9},{9,1},{17,25},{25,17},{2,10},{10... | collective-permute-start | bytes 1179656 | tf_op jit(solution)/shard_map/ppermute | solution.py:70
  145.9 5.4 %collective-permute-start.26 = (bf16[4,2,96,384]{3,2,1,0:T(8,128)(2,1)S(1)}, bf16[4,2,96,384]{3,2,1,0:T(8,128)(2,1)S(1)}, u32[]{:S(2)}, u32[]{:S(2)}) collective-permute-start(bf16[4,2,96,384]{3,2,1,0:T(8,128)(2,1)S(1)} %slice_bitcast_fusion.2), channel_id=1, source_target_pairs={{0,4},{4,0},{1,5},{5,1},{2,6},{6,2},{3,7},{7,3},{8,12},{12,8},{9,1... | collective-permute-start | bytes 1769480 | tf_op jit(solution)/shard_map/ppermute | solution.py:70
  150.4 11.3 %collective-permute-start.22 = (bf16[1,2,96,512]{3,2,1,0:T(8,128)(2,1)S(1)}, bf16[1,2,96,512]{3,2,1,0:T(8,128)(2,1)S(1)}, u32[]{:S(2)}, u32[]{:S(2)}) collective-permute-start(bf16[1,2,96,512]{3,2,1,0:T(8,128)(2,1)S(1)} %slice.198), channel_id=1, source_target_pairs={{0,16},{8,24},{16,0},{24,8},{1,17},{9,25},{17,1},{25,9},{2,18},{10... | collective-permute-start | bytes 589832 | tf_op jit(solution)/shard_map/ppermute | solution.py:70
  151.4 12.2 %collective-permute-start.27 = (bf16[2,2,96,384]{3,2,1,0:T(8,128)(2,1)S(1)}, bf16[2,2,96,384]{3,2,1,0:T(8,128)(2,1)S(1)}, u32[]{:S(2)}, u32[]{:S(2)}) collective-permute-start(bf16[2,2,96,384]{3,2,1,0:T(8,128)(2,1)S(1)} %slice.173), channel_id=1, source_target_pairs={{0,8},{8,0},{16,24},{24,16},{1,9},{9,1},{17,25},{25,17},{2,10},{10... | collective-permute-start | bytes 884744 | tf_op jit(solution)/shard_map/ppermute | solution.py:70
  161.8 10.1 %collective-permute-start.23 = (bf16[1,96,512]{2,1,0:T(8,128)(2,1)S(1)}, bf16[1,96,512]{2,1,0:T(8,128)(2,1)S(1)}, u32[]{:S(2)}, u32[]{:S(2)}) collective-permute-start(bf16[1,96,512]{2,1,0:T(8,128)(2,1)S(1)} %fusion.9), channel_id=1, source_target_pairs={{0,16},{8,24},{16,0},{24,8},{1,17},{9,25},{17,1},{25,9},{2,18},{10... | collective-permute-start | bytes 294920 | tf_op jit(solution)/shard_map/ppermute | solution.py:70
  163.8 11.3 %collective-permute-start.28 = (bf16[1,2,96,384]{3,2,1,0:T(8,128)(2,1)S(1)}, bf16[1,2,96,384]{3,2,1,0:T(8,128)(2,1)S(1)}, u32[]{:S(2)}, u32[]{:S(2)}) collective-permute-start(bf16[1,2,96,384]{3,2,1,0:T(8,128)(2,1)S(1)} %slice.202), channel_id=1, source_target_pairs={{0,16},{8,24},{16,0},{24,8},{1,17},{9,25},{17,1},{25,9},{2,18},{10... | collective-permute-start | bytes 442376 | tf_op jit(solution)/shard_map/ppermute | solution.py:70
  172.0 7.8 %collective-permute-start.24 = (bf16[2,96,512]{2,1,0:T(8,128)(2,1)S(1)}, bf16[2,96,512]{2,1,0:T(8,128)(2,1)S(1)}, u32[]{:S(2)}, u32[]{:S(2)}) collective-permute-start(bf16[2,96,512]{2,1,0:T(8,128)(2,1)S(1)} %pad_maximum_fusion.9), channel_id=1, source_target_pairs={{0,8},{8,0},{16,24},{24,16},{1,9},{9,1},{17,25},{25,17},{2,10},{10... | collective-permute-start | bytes 589832 | tf_op jit(solution)/shard_map/ppermute | solution.py:70
  175.2 6.5 %collective-permute-start.29 = (bf16[1,96,384]{2,1,0:T(8,128)(2,1)S(1)}, bf16[1,96,384]{2,1,0:T(8,128)(2,1)S(1)}, u32[]{:S(2)}, u32[]{:S(2)}) collective-permute-start(bf16[1,96,384]{2,1,0:T(8,128)(2,1)S(1)} %fusion.13), channel_id=1, source_target_pairs={{0,16},{8,24},{16,0},{24,8},{1,17},{9,25},{17,1},{25,9},{2,18},{10... | collective-permute-start | bytes 221192 | tf_op jit(solution)/shard_map/ppermute | solution.py:70
  179.8 7.5 %collective-permute-start.25 = (bf16[1,4,96,512]{3,2,1,0:T(8,128)(2,1)S(1)}, bf16[1,4,96,512]{3,2,1,0:T(8,128)(2,1)S(1)}, u32[]{:S(2)}, u32[]{:S(2)}) collective-permute-start(bf16[1,4,96,512]{3,2,1,0:T(8,128)(2,1)S(1)} %maximum_bitcast_fusion), channel_id=1, source_target_pairs={{0,4},{4,0},{1,5},{5,1},{2,6},{6,2},{3,7},{7,3},{8,12},{12,8},{9,1... | collective-permute-start | bytes 1179656 | tf_op jit(solution)/shard_map/ppermute | solution.py:70
  181.7 5.4 %collective-permute-start.30 = (bf16[2,96,384]{2,1,0:T(8,128)(2,1)S(1)}, bf16[2,96,384]{2,1,0:T(8,128)(2,1)S(1)}, u32[]{:S(2)}, u32[]{:S(2)}) collective-permute-start(bf16[2,96,384]{2,1,0:T(8,128)(2,1)S(1)} %pad_maximum_fusion.11), channel_id=1, source_target_pairs={{0,8},{8,0},{16,24},{24,16},{1,9},{9,1},{17,25},{25,17},{2,10},{10... | collective-permute-start | bytes 442376 | tf_op jit(solution)/shard_map/ppermute | solution.py:70
  187.2 4.8 %collective-permute-start.31 = (bf16[1,4,96,384]{3,2,1,0:T(8,128)(2,1)S(1)}, bf16[1,4,96,384]{3,2,1,0:T(8,128)(2,1)S(1)}, u32[]{:S(2)}, u32[]{:S(2)}) collective-permute-start(bf16[1,4,96,384]{3,2,1,0:T(8,128)(2,1)S(1)} %maximum_bitcast_fusion.1), channel_id=1, source_target_pairs={{0,4},{4,0},{1,5},{5,1},{2,6},{6,2},{3,7},{7,3},{8,12},{12,8},{9,1... | collective-permute-start | bytes 884744 | tf_op jit(solution)/shard_map/ppermute | solution.py:70
  196.1 4.6 %collective-permute-start.32 = (bf16[3,8,1024]{2,1,0:T(8,128)(2,1)S(1)}, bf16[3,8,1024]{2,1,0:T(8,128)(2,1)S(1)}, u32[]{:S(2)}, u32[]{:S(2)}) collective-permute-start(bf16[3,8,1024]{2,1,0:T(8,128)(2,1)S(1)} %get-tuple-element.64), channel_id=1, source_target_pairs={{0,1},{1,0},{2,3},{3,2},{4,5},{5,4},{6,7},{7,6},{8,9},{9,8},{10,11... | collective-permute-start | bytes 147464 | tf_op jit(solution)/shard_map/ppermute | solution.py:70
  197.0 5.0 %collective-permute-start.34 = (bf16[3,8,1024]{2,1,0:T(8,128)(2,1)S(1)}, bf16[3,8,1024]{2,1,0:T(8,128)(2,1)S(1)}, u32[]{:S(2)}, u32[]{:S(2)}) collective-permute-start(bf16[3,8,1024]{2,1,0:T(8,128)(2,1)S(1)} %get-tuple-element.65), channel_id=1, source_target_pairs={{0,3},{1,2},{2,1},{3,0},{4,7},{5,6},{6,5},{7,4},{8,11},{9,10},{10,... | collective-permute-start | bytes 147464 | tf_op jit(solution)/shard_map/ppermute | solution.py:70
  198.8 4.2 %collective-permute-start.33 = (bf16[3,8,1024]{2,1,0:T(8,128)(2,1)S(1)}, bf16[3,8,1024]{2,1,0:T(8,128)(2,1)S(1)}, u32[]{:S(2)}, u32[]{:S(2)}) collective-permute-start(bf16[3,8,1024]{2,1,0:T(8,128)(2,1)S(1)} %get-tuple-element.66), channel_id=1, source_target_pairs={{0,2},{1,3},{2,0},{3,1},{4,6},{5,7},{6,4},{7,5},{8,10},{9,11},{10,... | collective-permute-start | bytes 147464 | tf_op jit(solution)/shard_map/ppermute | solution.py:70

commit v4 on v3

--- a/solution.py
+++ b/solution.py
@@ -84,6 +84,22 @@
     return x
 
 
+def gather(x, axis):
+    n = lax.axis_size(axis)
+    if n > 4:
+        return gather_rounds(x, axis, bits(n))
+    return jnp.stack([x] + [swap(x, axis, k) for k in range(1, n)])
+
+
+def total_along(x, axis):
+    n = lax.axis_size(axis)
+    if n > 4:
+        for bit in bits(n):
+            x = x + swap(x, axis, bit)
+        return x
+    return functools.reduce(jnp.add, [x] + [swap(x, axis, k) for k in range(1, n)])
+
+
 def add_round(x, axis, order):
     for bit in order:
         half = x.shape[0] // 2
@@ -111,8 +127,7 @@
     squares = jnp.sum(value * value, axis=3)
     total = as_tile(squares.reshape(-1, squares.shape[-1]))
     total = total + swap(total, "core", 1)
-    for bit in bits(lax.axis_size("z")):
-        total = total + swap(total, "z", bit)
+    total = total_along(total, "z")
     total = total[: squares.shape[0] * squares.shape[1], : squares.shape[2]].reshape(squares.shape)
     return normed(value, total, gain, width).reshape(-1, x.shape[3])
 
@@ -190,7 +205,7 @@
                 for n, head in enumerate(heads):
                     chip, tile = divmod(rank_in[head] * steps + s, tiles_in)
                     for z in range(z_count):
-                        row = mirror(chip ^ z, z_count) * branches + head // heads_in
+                        row = (chip ^ z) * branches + head // heads_in
                         fetch[z, core, j, n, s] = row * tiles_in + tile
                     if head < HEADS:
                         chip, tile = divmod(rank_out[head] * steps + s, tiles_out)
@@ -201,7 +216,7 @@
             for z in range(z_count):
                 for core in range(CORES):
                     side = (key_head(head) % CORES) ^ core
-                    row = side * z_count + mirror(chip ^ z, z_count)
+                    row = side * z_count + (chip ^ z)
                     mix[z, core, head // heads_out, head % heads_out, s] = row * LANE + tile
     full = (z_count, CORES, branches)
     parts = [
@@ -544,12 +559,47 @@
     )(table, qkv, cosine, sine, bias, *sources)
 
 
-def trade_heads(kv):
-    heads = [kv[..., n * HD : (n + 1) * HD] for n in range(KVH)]
-    even = jnp.concatenate(heads[0::CORES], axis=-1)
-    odd = jnp.concatenate(heads[1::CORES], axis=-1)
-    first = lax.axis_index("core") == 0
-    return [jnp.where(first, even, odd), swap(jnp.where(first, odd, even), "core", 1)]
+def cut_kernel(ids, *refs):
+    *arrays, sems = refs
+    sources, outs = arrays[: len(arrays) // 3], arrays[len(arrays) // 3 :]
+    copies = []
+    for n, source in enumerate(sources):
+        for side in range(CORES):
+            for j in range(KVH // CORES):
+                head = j * CORES + (ids[1] ^ side)
+                at = pl.ds(pl.multiple_of(head * HD, HD), HD)
+                copies.append(
+                    pltpu.make_async_copy(
+                        source.at[:, :, :, at],
+                        outs[n * CORES + side].at[:, :, :, pl.ds(j * HD, HD)],
+                        sems.at[len(copies)],
+                    )
+                )
+    for c in copies:
+        c.start()
+    for c in copies:
+        c.wait()
+
+
+def trade_heads(ids, *arrays):
+    halves = [
+        jax.ShapeDtypeStruct(a.shape[:-1] + (a.shape[-1] // CORES,), BF16)
+        for a in arrays
+        for _ in range(CORES)
+    ]
+    cut = pl.pallas_call(
+        cut_kernel,
+        in_specs=[IN_SMEM] + [IN_HBM] * len(arrays),
+        out_specs=[IN_HBM] * len(halves),
+        out_shape=halves,
+        scratch_shapes=[pltpu.SemaphoreType.DMA((len(arrays) * KVH,))],
+        compiler_params=params(4),
+        cost_estimate=pl.CostEstimate(flops=0, bytes_accessed=2**23, transcendentals=0),
+        name="cut",
+    )(ids, *arrays)
+    return [
+        x if n % CORES == 0 else swap(x, "core", 1) for n, x in enumerate(cut)
+    ]
 
 
 def both_cores(own):
@@ -587,6 +637,7 @@
         in_specs=[IN_VMEM],
         out_specs=IN_VMEM,
         out_shape=jax.ShapeDtypeStruct((branches, count - 1, SUB, HD), BF16),
+        compiler_params=params(8),
         name="join",
     )(parts)
 
@@ -628,9 +679,10 @@
     cosine = jnp.concatenate([cos, cos], axis=-1)
     sine = jnp.concatenate([-sin, sin], axis=-1)
 
-    every_row = gather_rounds(hidden, "branch", across)
+    every_row = gather(hidden, "branch")
+    every_row, tree_kv, suffix_kv = lax.optimization_barrier((every_row, tree_kv, suffix_kv))
     lhs = norm_rows(every_row, attn_gain, width)
-    sources = trade_heads(tree_kv) + trade_heads(suffix_kv)
+    sources = trade_heads(ids, tree_kv, suffix_kv)
     lhs, table, sources, cosine, sine, bias = lax.optimization_barrier(
         (lhs, table, sources, cosine, sine, bias)
     )
@@ -639,14 +691,15 @@
     plane = z_count * branches
     received = exchange(chip_sums.reshape(plane, tiles_in, SUB, HD), ("z", "branch"))
     summed = jnp.sum(received.reshape(z_count, branches, tiles_in, SUB, HD), axis=0).astype(BF16)
-    qkv = gather_rounds(summed, "z", near[::-1]).reshape(-1, SUB, HD)
+    qkv = gather(summed, "z").reshape(-1, SUB, HD)
 
     softmax_parts, new_kv = attend(
         table, fetch, send, qkv, cosine, sine, bias, sources, plane, tiles_out
     )
     received = exchange(softmax_parts, ("z", "branch"))
     attended = join(received.reshape(z_count, branches, tiles_out + 1, SUB, HD))
-    attended = gather_prefix(attended)
+    attended = gather_rounds(gather(attended, "z"), "core", [1])
+    attended = attended.reshape((prefix,) + attended.shape[2:])
     new_kv = both_cores(new_kv).transpose(2, 0, 1, 3)
 
     mixed = sum_branches(*mix_heads(ids, table, mix, attended, w_out, steps))

time: 204 us -> 188 us (0.922)
  waiting for transfers between devices: 86.4 us -> 65.3 us
  starting transfers between devices: 24.2 us -> 36.7 us
  other arithmetic: 12 us -> 6.35 us
    ppermute x36 -> x41, waiting for transfers between devices: 86.4 us -> 65.3 us  [swap(): lax.ppermute(x, axis, [(i, i ^ bit) for i in range(lax.axis_size(axis))])]
    ppermute x36 -> x41, starting transfers between devices: 24.2 us -> 36.7 us  [swap(): lax.ppermute(x, axis, [(i, i ^ bit) for i in range(lax.axis_size(axis))])]
    select_n x2 -> x0, other arithmetic: 3.63 us -> none  [trade_heads(): jnp.where(first, odd, even)]
    concatenate x9 -> x5, other arithmetic: 2.86 us -> 0.22 us  [gather_rounds(): x = jnp.concatenate([x, swap(x, axis, bit)], axis=0)]
    pallas_call x0 -> x1, Pallas kernels: none -> 2.32 us  [trade_heads(): pl.pallas_call(cut_kernel, in_specs=[IN_SMEM] + [IN_HBM] * len(arrays), o...]
    slice x2 -> x0, local copies, waits for them, and re-layouts: 2.28 us -> none  [trade_heads(): heads = [kv[..., n * HD:(n + 1) * HD] for n in range(KVH)]]
    unnamed x32 -> x30, local copies, waits for them, and re-layouts: 6.13 us -> 7.1 us
  transfers between devices with their start and end apart: 36 -> 41, of which waited for: 28 -> 30; matrix products, arithmetic and copies ran while one was open for 5% -> 2% of each run, Pallas kernels for 10% -> 11%
where the time goes in v4:
time: 188 us
  waiting for transfers between devices  65.3 us (35%)
  starting transfers between devices  36.7 us (20%)
  Pallas kernels  35.1 us (19%)
  blocking collectives  34.3 us (18%)
  local copies, waits for them, and re-layouts  9 us (5%)
  other arithmetic  6.35 us (3%)
    ppermute x41, waiting for transfers between devices, swap(): lax.ppermute(x, axis, [(i, i ^ bit) for i in range(lax.axis_size(axis))])  65.3 us
    ppermute x41, starting transfers between devices, swap(): lax.ppermute(x, axis, [(i, i ^ bit) for i in range(lax.axis_size(axis))])  36.7 us
    all_to_all x2, blocking collectives, exchange(): return lax.all_to_all(x, axes, split_axis=0, concat_axis=0, tiled=True)  34.3 us
    pallas_call x2, Pallas kernels, project_gate_up(): pl.pallas_call(functools.partial(gate_up_kernel, unit, start), in_specs=[...  13.6 us
    pallas_call x2, Pallas kernels, project_down(): pl.pallas_call(functools.partial(down_kernel, unit, start), in_specs=[IN_...  8.63 us
    unnamed x30, local copies, waits for them, and re-layouts  7.1 us
    pallas_call x1, Pallas kernels, attend(): pl.pallas_call(functools.partial(attend_kernel, fetch, send), in_specs=[I...  4.92 us
  transfers between devices with their start and end apart: 41, of which 30 were waited for; matrix products, arithmetic and copies ran while one was open for 2% of the time, Pallas kernels for 11%

profile of v4, /device:TPU:0, one launch (start us, length us, event | category | flops | bytes accessed | tf_op | source)
XLA Modules:
  0.0 187.8 jit_solution(9737889810868439742)
XLA Ops:
  0.6 3.0 %collective-permute-start = (bf16[3,8,1024]{2,1,0:T(8,128)(2,1)}, bf16[3,8,1024]{2,1,0:T(8,128)(2,1)S(1)}, u32[]{:S(2)}, u32[]{:S(2)}) collective-permute-start(bf16[3,8,1024]{2,1,0:T(8,128)(2,1)} %param.14), channel_id=1, source_target_pairs={{0,1},{1,0},{2,3},{3,2},{4,5},{5,4},{6,7},{7,6},{8,9},{9,8},{10,11... | collective-permute-start | bytes 147464 | tf_op jit(solution)/shard_map/ppermute | solution.py:70
  3.6 1.5 collective-permute-start.2
  5.8 1.7 prepare.1
  7.5 0.8 slice_reduce_fusion
  9.4 0.8 pad_maximum_fusion.4
  10.3 1.6 copy-done.2
  11.8 1.6 copy-done.3
  14.1 2.3 %cut.1 = (bf16[1,2,512,512]{3,2,1,0:T(8,128)(2,1)S(1)}, bf16[1,2,512,512]{3,2,1,0:T(8,128)(2,1)}, bf16[8,2,64,512]{3,2,1,0:T(8,128)(2,1)S(1)}, bf16[8,2,64,512]{3,2,1,0:T(8,128)(2,1)}) custom-call(s32[3]{0:T(128)S(1)} %copy-done.5, bf16[1,2,512,1024]{3,2,1,0:T(8,128)(2,1)S(1)} %copy-done.2, bf16[8,2,64,1024]{3,2,1,0:T(8,128)(2,1)S(1)} %copy-done.3), custom_call_target="tpu_custom_call" | custom-call | bytes 8388608 | tf_op jit(solution)/shard_map/cut/pallas_call | solution.py:590
  17.4 2.5 %collective-permute-done.3 = f32[16,128]{1,0:T(8,128)S(1)} collective-permute-done((f32[16,128]{1,0:T(8,128)S(1)}, f32[16,128]{1,0:T(8,128)S(1)}, u32[]{:S(2)}, u32[]{:S(2)}) %collective-permute-start.3) | collective-permute-done | bytes 8224 | tf_op jit(solution)/shard_map/ppermute | solution.py:70
  19.9 3.6 %collective-permute-start.6 = (f32[16,128]{1,0:T(8,128)S(1)}, f32[16,128]{1,0:T(8,128)S(1)}, u32[]{:S(2)}, u32[]{:S(2)}) collective-permute-start(f32[16,128]{1,0:T(8,128)S(1)} %pad_add_fusion.2), channel_id=1, source_target_pairs={{0,24},{8,16},{16,8},{24,0},{1,25},{9,17},{17,9},{25,1},{2,26},{10... | collective-permute-start | bytes 24584 | tf_op jit(solution)/shard_map/ppermute | solution.py:70
  23.5 0.8 collective-permute-start.4
  24.3 0.7 dynamic-slice_reduce_fusion.table
  25.3 2.7 %collective-permute-done.5 = f32[16,128]{1,0:T(8,128)S(1)} collective-permute-done((f32[16,128]{1,0:T(8,128)S(1)}, f32[16,128]{1,0:T(8,128)S(1)}, u32[]{:S(2)}, u32[]{:S(2)}) %collective-permute-start.5) | collective-permute-done | bytes 8224 | tf_op jit(solution)/shard_map/ppermute | solution.py:70
  28.2 2.5 %copy-done = bf16[1024,2560]{1,0:T(8,128)(2,1)S(1)} copy-done((bf16[1024,2560]{1,0:T(8,128)(2,1)S(1)}, bf16[1024,2560]{1,0:T(8,128)(2,1)}, u32[]{:S(2)}) %copy-start) | copy-done | bytes 5242904
  30.7 2.0 %qkv.1 = f32[2,4,4,9,8,128]{5,4,3,2,1,0:T(8,128)S(1)} custom-call(s32[3]{0:T(128)S(1)} %copy-done.6, s32[284]{0:T(512)S(1)} %dynamic-slice_reduce_fusion.table, bf16[96,1024]{1,0:T(8,128)(2,1)S(1)} %bitcast.114, bf16[1024,2560]{1,0:T(8,128)(2,1)S(1)} %copy-done), custom_call_target="tpu_custom_call" | custom-call | flops 503316480 | bytes 5242880 | tf_op jit(solution)/shard_map/qkv/pallas_call | solution.py:275
  32.9 2.0 %collective-permute-done.9 = f32[4,4,9,8,128]{4,3,2,1,0:T(8,128)S(1)} collective-permute-done((f32[4,4,9,8,128]{4,3,2,1,0:T(8,128)S(1)}, f32[4,4,9,8,128]{4,3,2,1,0:T(8,128)S(1)}, u32[]{:S(2)}, u32[]{:S(2)}) %collective-permute-start.9) | collective-permute-done | bytes 589856 | tf_op jit(solution)/shard_map/ppermute | solution.py:70
  34.9 22.5 %all_to_all.10 = f32[16,9,8,128]{3,2,1,0:T(8,128)} all-to-all(f32[16,9,8,128]{3,2,1,0:T(8,128)S(1)} %bitcast.116), channel_id=1, replica_groups=mesh['z'=4,'core'=2,'branch'=4] {'z','branch'}, dimensions={0} | all-to-all | bytes 1179648 | tf_op jit(solution)/shard_map/all_to_all | solution.py:45
  57.4 1.1 reduce_sum.28
  59.1 1.6 collective-permute-start.10
  60.6 2.3 %collective-permute-start.12 = (bf16[4,9,8,128]{3,2,1,0:T(8,128)(2,1)S(1)}, bf16[4,9,8,128]{3,2,1,0:T(8,128)(2,1)S(1)}, u32[]{:S(2)}, u32[]{:S(2)}) collective-permute-start(bf16[4,9,8,128]{3,2,1,0:T(8,128)(2,1)S(1)} %reduce_sum.28), channel_id=1, source_target_pairs={{0,24},{8,16},{16,8},{24,0},{1,25},{9,17},{17,9},{25,1},{2,26},{10... | collective-permute-start | bytes 221192 | tf_op jit(solution)/shard_map/ppermute | solution.py:70
  63.0 2.5 %collective-permute-done.11 = bf16[4,9,8,128]{3,2,1,0:T(8,128)(2,1)S(1)} collective-permute-done((bf16[4,9,8,128]{3,2,1,0:T(8,128)(2,1)S(1)}, bf16[4,9,8,128]{3,2,1,0:T(8,128)(2,1)S(1)}, u32[]{:S(2)}, u32[]{:S(2)}) %collective-permute-start.11) | collective-permute-done | bytes 73760 | tf_op jit(solution)/shard_map/ppermute | solution.py:70
  65.5 1.4 collective-permute-done.12
  67.0 4.9 %attend.1 = (bf16[16,7,8,128]{3,2,1,0:T(8,128)(2,1)S(1)}, bf16[2,3,8,512]{3,2,1,0:T(8,128)(2,1)S(1)}) custom-call(s32[284]{0:T(512)S(1)} %dynamic-slice_reduce_fusion.table, bf16[144,8,128]{2,1,0:T(8,128)(2,1)S(1)} %bitcast.112, f32[3,8,128]{2,1,0:T(8,128)S(1)} %get-tuple-element.38.cosine, f32[3,8,128]{2,1,0:T(8,128)S(1)} %get-tuple-element.39.sine, ...), custom_call_target="tpu_custom_call" | custom-call | flops 1073741824 | bytes 4194304 | tf_op jit(solution)/shard_map/attend/pallas_call | solution.py:545
  71.9 11.8 %all_to_all.11 = bf16[16,7,8,128]{3,2,1,0:T(8,128)(2,1)S(1)} all-to-all(bf16[16,7,8,128]{3,2,1,0:T(8,128)(2,1)S(1)} %get-tuple-element.45), channel_id=1, replica_groups=mesh['z'=4,'core'=2,'branch'=4] {'z','branch'}, dimensions={0} | all-to-all | bytes 458752 | tf_op jit(solution)/shard_map/all_to_all | solution.py:45
  84.0 1.7 collective-permute-start.15
  86.2 2.2 %collective-permute-start.13 = (bf16[4,6,8,128]{3,2,1,0:T(8,128)(2,1)S(1)}, bf16[4,6,8,128]{3,2,1,0:T(8,128)(2,1)S(1)}, u32[]{:S(2)}, u32[]{:S(2)}) collective-permute-start(bf16[4,6,8,128]{3,2,1,0:T(8,128)(2,1)S(1)} %join.1), channel_id=1, source_target_pairs={{0,8},{8,0},{16,24},{24,16},{1,9},{9,1},{17,25},{25,17},{2,10},{10... | collective-permute-start | bytes 147464 | tf_op jit(solution)/shard_map/ppermute | solution.py:70
  88.4 1.5 collective-permute-done.15
  89.9 1.1 collective-permute-done.14
  91.1 1.4 collective-permute-done.16
  92.6 1.5 mix.1
  94.2 1.3 collective-permute-start.17
  95.5 3.6 %collective-permute-done.17 = bf16[4,3,8,512]{3,2,1,0:T(8,128)(2,1)S(1)} collective-permute-done((bf16[4,3,8,512]{3,2,1,0:T(8,128)(2,1)S(1)}, bf16[4,3,8,512]{3,2,1,0:T(8,128)(2,1)S(1)}, u32[]{:S(2)}, u32[]{:S(2)}) %collective-permute-start.17) | collective-permute-done | bytes 98336 | tf_op jit(solution)/shard_map/ppermute | solution.py:70
  99.1 0.8 collective-permute-start.18
  100.2 0.8 collective-permute-start.20
  101.0 2.8 %collective-permute-done.18 = bf16[4,3,8,512]{3,2,1,0:T(8,128)(2,1)S(1)} collective-permute-done((bf16[4,3,8,512]{3,2,1,0:T(8,128)(2,1)S(1)}, bf16[4,3,8,512]{3,2,1,0:T(8,128)(2,1)S(1)}, u32[]{:S(2)}, u32[]{:S(2)}) %collective-permute-start.18) | collective-permute-done | bytes 98336 | tf_op jit(solution)/shard_map/ppermute | solution.py:70
  103.9 1.0 collective-permute-done.20
  105.2 1.2 collective-permute-done.21
  106.3 1.9 %collective-permute-start.24 = (f32[16,128]{1,0:T(8,128)S(1)}, f32[16,128]{1,0:T(8,128)S(1)}, u32[]{:S(2)}, u32[]{:S(2)}) collective-permute-start(f32[16,128]{1,0:T(8,128)S(1)} %pad_add_fusion.1), channel_id=1, source_target_pairs={{0,24},{8,16},{16,8},{24,0},{1,25},{9,17},{17,9},{25,1},{2,26},{10... | collective-permute-start | bytes 24584 | tf_op jit(solution)/shard_map/ppermute | solution.py:70
  108.2 1.1 collective-permute-start.23
  109.4 1.3 collective-permute-start.22
  110.7 1.1 collective-permute-done.24
  111.8 1.0 collective-permute-done.23
  113.2 7.4 %gate_up.2 = bf16[2,4,2,96,512]{4,3,2,1,0:T(8,128)(2,1)S(1)} custom-call(s32[3]{0:T(128)S(1)} %copy-done.6, bf16[96,1024]{1,0:T(8,128)(2,1)S(1)} %bitcast.109, bf16[2,1024,7168]{2,1,0:T(8,128)(2,1)} %w.7), custom_call_target="tpu_custom_call" | custom-call | flops 1610612736 | bytes 16777216 | tf_op jit(solution)/shard_map/gate_up/pallas_call | solution.py:312
  120.8 2.3 %collective-permute-done.25 = bf16[4,2,96,512]{3,2,1,0:T(8,128)(2,1)} collective-permute-done((bf16[4,2,96,512]{3,2,1,0:T(8,128)(2,1)S(1)}, bf16[4,2,96,512]{3,2,1,0:T(8,128)(2,1)}, u32[]{:S(2)}, u32[]{:S(2)}) %collective-permute-start.25) | collective-permute-done | bytes 786464 | tf_op jit(solution)/shard_map/ppermute | solution.py:70
  123.1 1.4 fusion
  124.5 1.4 collective-permute-start.26
  125.9 6.2 %gate_up.3 = bf16[2,4,2,96,384]{4,3,2,1,0:T(8,128)(2,1)S(1)} custom-call(s32[3]{0:T(128)S(1)} %copy-done.6, bf16[96,1024]{1,0:T(8,128)(2,1)S(1)} %bitcast.110, bf16[2,1024,7168]{2,1,0:T(8,128)(2,1)} %w.7), custom_call_target="tpu_custom_call" | custom-call | flops 1207959552 | bytes 12582912 | tf_op jit(solution)/shard_map/gate_up/pallas_call | solution.py:312
  132.3 3.4 %collective-permute-done.26 = bf16[2,2,96,512]{3,2,1,0:T(8,128)(2,1)S(1)} collective-permute-done((bf16[2,2,96,512]{3,2,1,0:T(8,128)(2,1)S(1)}, bf16[2,2,96,512]{3,2,1,0:T(8,128)(2,1)S(1)}, u32[]{:S(2)}, u32[]{:S(2)}) %collective-permute-start.26) | collective-permute-done | bytes 393248 | tf_op jit(solution)/shard_map/ppermute | solution.py:70
  135.8 1.9 collective-permute-start.27
  138.4 8.8 %collective-permute-done.27 = bf16[1,2,96,512]{3,2,1,0:T(8,128)(2,1)S(1)} collective-permute-done((bf16[1,2,96,512]{3,2,1,0:T(8,128)(2,1)S(1)}, bf16[1,2,96,512]{3,2,1,0:T(8,128)(2,1)S(1)}, u32[]{:S(2)}, u32[]{:S(2)}) %collective-permute-start.27) | collective-permute-done | bytes 196640 | tf_op jit(solution)/shard_map/ppermute | solution.py:70
  147.4 1.8 collective-permute-done.32
  149.4 2.5 %collective-permute-start.33 = (bf16[1,2,96,384]{3,2,1,0:T(8,128)(2,1)S(1)}, bf16[1,2,96,384]{3,2,1,0:T(8,128)(2,1)S(1)}, u32[]{:S(2)}, u32[]{:S(2)}) collective-permute-start(bf16[1,2,96,384]{3,2,1,0:T(8,128)(2,1)S(1)} %slice.142), channel_id=1, source_target_pairs={{0,16},{8,24},{16,0},{24,8},{1,17},{9,25},{17,1},{25,9},{2,18},{10... | collective-permute-start | bytes 442376 | tf_op jit(solution)/shard_map/ppermute | solution.py:70
  151.9 5.8 %collective-permute-done.28 = bf16[1,96,512]{2,1,0:T(8,128)(2,1)S(1)} collective-permute-done((bf16[1,96,512]{2,1,0:T(8,128)(2,1)S(1)}, bf16[1,96,512]{2,1,0:T(8,128)(2,1)S(1)}, u32[]{:S(2)}, u32[]{:S(2)}) %collective-permute-start.28) | collective-permute-done | bytes 98336 | tf_op jit(solution)/shard_map/ppermute | solution.py:70
  157.7 2.3 %collective-permute-done.33 = bf16[1,2,96,384]{3,2,1,0:T(8,128)(2,1)S(1)} collective-permute-done((bf16[1,2,96,384]{3,2,1,0:T(8,128)(2,1)S(1)}, bf16[1,2,96,384]{3,2,1,0:T(8,128)(2,1)S(1)}, u32[]{:S(2)}, u32[]{:S(2)}) %collective-permute-start.33) | collective-permute-done | bytes 147488 | tf_op jit(solution)/shard_map/ppermute | solution.py:70
  160.4 4.6 %collective-permute-done.29 = bf16[2,96,512]{2,1,0:T(8,128)(2,1)S(1)} collective-permute-done((bf16[2,96,512]{2,1,0:T(8,128)(2,1)S(1)}, bf16[2,96,512]{2,1,0:T(8,128)(2,1)S(1)}, u32[]{:S(2)}, u32[]{:S(2)}) %collective-permute-start.29) | collective-permute-done | bytes 196640 | tf_op jit(solution)/shard_map/ppermute | solution.py:70
  165.9 5.6 %collective-permute-done.35 = bf16[2,96,384]{2,1,0:T(8,128)(2,1)S(1)} collective-permute-done((bf16[2,96,384]{2,1,0:T(8,128)(2,1)S(1)}, bf16[2,96,384]{2,1,0:T(8,128)(2,1)S(1)}, u32[]{:S(2)}, u32[]{:S(2)}) %collective-permute-start.35) | collective-permute-done | bytes 147488 | tf_op jit(solution)/shard_map/ppermute | solution.py:70
  171.7 4.6 %down.2.refs_0_ = f32[96,1024]{1,0:T(8,128)S(1)} custom-call(s32[8]{0:T(128)S(1)} %fusion.29.table, bf16[8,96,512]{2,1,0:T(8,128)(2,1)S(1)} %bitcast.107, bf16[7168,1024]{1,0:T(8,128)(2,1)} %refs_2_.1), custom_call_target="tpu_custom_call" | custom-call | flops 805306368 | bytes 8388608 | tf_op jit(solution)/shard_map/down/pallas_call | solution.py:382
  176.4 4.0 %down.3 = bf16[4,3,8,1024]{3,2,1,0:T(8,128)(2,1)S(1)} custom-call(s32[8]{0:T(128)S(1)} %fusion.29.table, f32[96,1024]{1,0:T(8,128)S(1)} %down.2.refs_0_, bf16[8,96,384]{2,1,0:T(8,128)(2,1)S(1)} %bitcast.108, bf16[7168,1024]{1,0:T(8,128)(2,1)} %refs_2_.1), custom_call_target="tpu_custom_call" | custom-call | flops 603979776 | bytes 6291456 | tf_op jit(solution)/shard_map/down/pallas_call | solution.py:382
  180.4 0.7 collective-permute-start.37
  181.2 1.8 collective-permute-start.39
  182.9 1.0 collective-permute-start.38
  184.0 0.7 copy.17
  184.7 1.4 collective-permute-done.39
  186.2 1.0 collective-permute-done.38
  (120 shorter events, 10.3 us)
Async XLA Ops:
  0.6 7.7 %collective-permute-start = (bf16[3,8,1024]{2,1,0:T(8,128)(2,1)}, bf16[3,8,1024]{2,1,0:T(8,128)(2,1)S(1)}, u32[]{:S(2)}, u32[]{:S(2)}) collective-permute-start(bf16[3,8,1024]{2,1,0:T(8,128)(2,1)} %param.14), channel_id=1, source_target_pairs={{0,1},{1,0},{2,3},{3,2},{4,5},{5,4},{6,7},{7,6},{8,9},{9,8},{10,11... | collective-permute-start | bytes 147464 | tf_op jit(solution)/shard_map/ppermute | solution.py:70
  3.6 5.2 %collective-permute-start.2 = (bf16[3,8,1024]{2,1,0:T(8,128)(2,1)}, bf16[3,8,1024]{2,1,0:T(8,128)(2,1)S(1)}, u32[]{:S(2)}, u32[]{:S(2)}) collective-permute-start(bf16[3,8,1024]{2,1,0:T(8,128)(2,1)} %param.14), channel_id=1, source_target_pairs={{0,3},{1,2},{2,1},{3,0},{4,7},{5,6},{6,5},{7,4},{8,11},{9,10},{10,... | collective-permute-start | bytes 147464 | tf_op jit(solution)/shard_map/ppermute | solution.py:70
  5.1 4.3 %collective-permute-start.1 = (bf16[3,8,1024]{2,1,0:T(8,128)(2,1)}, bf16[3,8,1024]{2,1,0:T(8,128)(2,1)S(1)}, u32[]{:S(2)}, u32[]{:S(2)}) collective-permute-start(bf16[3,8,1024]{2,1,0:T(8,128)(2,1)} %param.14), channel_id=1, source_target_pairs={{0,2},{1,3},{2,0},{3,1},{4,6},{5,7},{6,4},{7,5},{8,10},{9,11},{10,... | collective-permute-start | bytes 147464 | tf_op jit(solution)/shard_map/ppermute | solution.py:70
  10.3 1.6 copy-start.2
  11.8 1.6 copy-start.3
  13.4 0.6 copy-start.5
  14.0 14.0 %copy-start.7 = (bf16[4,3,8,1024]{3,2,1,0:T(8,128)(2,1)}, bf16[4,3,8,1024]{3,2,1,0:T(8,128)(2,1)S(1)}, u32[]{:S(2)}) copy-start(bf16[4,3,8,1024]{3,2,1,0:T(8,128)(2,1)S(1)} %pad_maximum_fusion.4) | copy-start | bytes 589828
  14.1 14.0 %copy-start.9 = (f32[1024]{0:T(1024)S(1)}, f32[1024]{0:T(1024)}, u32[]{:S(2)}) copy-start(f32[1024]{0:T(1024)} %param.15) | copy-start | bytes 12292
  14.1 14.1 %copy-start.6 = (s32[3]{0:T(128)S(1)}, s32[3]{0:T(128)}, u32[]{:S(2)}) copy-start(s32[3]{0:T(128)} %pad_add_fusion.ids) | copy-start | bytes 40
  16.4 11.8 %collective-permute-start.7 = (bf16[1,2,512,512]{3,2,1,0:T(8,128)(2,1)}, bf16[1,2,512,512]{3,2,1,0:T(8,128)(2,1)S(1)}, u32[]{:S(2)}, u32[]{:S(2)}) collective-permute-start(bf16[1,2,512,512]{3,2,1,0:T(8,128)(2,1)} %get-tuple-element.31), channel_id=1, source_target_pairs={{0,4},{4,0},{1,5},{5,1},{2,6},{6,2},{3,7},{7,3},{8,12},{12,8},{9,1... | collective-permute-start | bytes 3145736 | tf_op jit(solution)/shard_map/ppermute | solution.py:70
  16.5 11.7 %collective-permute-start.8 = (bf16[8,2,64,512]{3,2,1,0:T(8,128)(2,1)}, bf16[8,2,64,512]{3,2,1,0:T(8,128)(2,1)}, u32[]{:S(2)}, u32[]{:S(2)}) collective-permute-start(bf16[8,2,64,512]{3,2,1,0:T(8,128)(2,1)} %get-tuple-element.33), channel_id=1, source_target_pairs={{0,4},{4,0},{1,5},{5,1},{2,6},{6,2},{3,7},{7,3},{8,12},{12,8},{9,1... | collective-permute-start | bytes 3145736 | tf_op jit(solution)/shard_map/ppermute | solution.py:70
  17.1 2.7 %collective-permute-start.3 = (f32[16,128]{1,0:T(8,128)S(1)}, f32[16,128]{1,0:T(8,128)S(1)}, u32[]{:S(2)}, u32[]{:S(2)}) collective-permute-start(f32[16,128]{1,0:T(8,128)S(1)} %pad.7), channel_id=1, source_target_pairs={{0,4},{4,0},{1,5},{5,1},{2,6},{6,2},{3,7},{7,3},{8,12},{12,8},{9,1... | collective-permute-start | bytes 24584 | tf_op jit(solution)/shard_map/ppermute | solution.py:70
  19.9 5.4 %collective-permute-start.6 = (f32[16,128]{1,0:T(8,128)S(1)}, f32[16,128]{1,0:T(8,128)S(1)}, u32[]{:S(2)}, u32[]{:S(2)}) collective-permute-start(f32[16,128]{1,0:T(8,128)S(1)} %pad_add_fusion.2), channel_id=1, source_target_pairs={{0,24},{8,16},{16,8},{24,0},{1,25},{9,17},{17,9},{25,1},{2,26},{10... | collective-permute-start | bytes 24584 | tf_op jit(solution)/shard_map/ppermute | solution.py:70
  23.5 4.5 %collective-permute-start.5 = (f32[16,128]{1,0:T(8,128)S(1)}, f32[16,128]{1,0:T(8,128)S(1)}, u32[]{:S(2)}, u32[]{:S(2)}) collective-permute-start(f32[16,128]{1,0:T(8,128)S(1)} %pad_add_fusion.2), channel_id=1, source_target_pairs={{0,16},{8,24},{16,0},{24,8},{1,17},{9,25},{17,1},{25,9},{2,18},{10... | collective-permute-start | bytes 24584 | tf_op jit(solution)/shard_map/ppermute | solution.py:70
  23.5 4.5 %collective-permute-start.4 = (f32[16,128]{1,0:T(8,128)S(1)}, f32[16,128]{1,0:T(8,128)S(1)}, u32[]{:S(2)}, u32[]{:S(2)}) collective-permute-start(f32[16,128]{1,0:T(8,128)S(1)} %pad_add_fusion.2), channel_id=1, source_target_pairs={{0,8},{8,0},{16,24},{24,16},{1,9},{9,1},{17,25},{25,17},{2,10},{10... | collective-permute-start | bytes 24584 | tf_op jit(solution)/shard_map/ppermute | solution.py:70
  28.2 2.5 %copy-start = (bf16[1024,2560]{1,0:T(8,128)(2,1)S(1)}, bf16[1024,2560]{1,0:T(8,128)(2,1)}, u32[]{:S(2)}) copy-start(bf16[1024,2560]{1,0:T(8,128)(2,1)} %w.4) | copy-start | bytes 15728644
  32.8 2.1 %collective-permute-start.9 = (f32[4,4,9,8,128]{4,3,2,1,0:T(8,128)S(1)}, f32[4,4,9,8,128]{4,3,2,1,0:T(8,128)S(1)}, u32[]{:S(2)}, u32[]{:S(2)}) collective-permute-start(f32[4,4,9,8,128]{4,3,2,1,0:T(8,128)S(1)} %slice_bitcast_fusion.4), channel_id=1, source_target_pairs={{0,4},{4,0},{1,5},{5,1},{2,6},{6,2},{3,7},{7,3},{8,12},{12,8},{9,1... | collective-permute-start | bytes 1769480 | tf_op jit(solution)/shard_map/ppermute | solution.py:70
  34.9 32.0 %copy-start.4 = (f32[24,2176]{1,0:T(8,128)S(1)}, f32[24,2176]{1,0:T(8,128)}, u32[]{:S(2)}) copy-start(f32[24,2176]{1,0:T(8,128)} %get-tuple-element.40.bias) | copy-start | bytes 626692
  58.5 7.0 %collective-permute-start.11 = (bf16[4,9,8,128]{3,2,1,0:T(8,128)(2,1)S(1)}, bf16[4,9,8,128]{3,2,1,0:T(8,128)(2,1)S(1)}, u32[]{:S(2)}, u32[]{:S(2)}) collective-permute-start(bf16[4,9,8,128]{3,2,1,0:T(8,128)(2,1)S(1)} %reduce_sum.28), channel_id=1, source_target_pairs={{0,16},{8,24},{16,0},{24,8},{1,17},{9,25},{17,1},{25,9},{2,18},{10... | collective-permute-start | bytes 221192 | tf_op jit(solution)/shard_map/ppermute | solution.py:70
  59.1 6.4 %collective-permute-start.10 = (bf16[4,9,8,128]{3,2,1,0:T(8,128)(2,1)S(1)}, bf16[4,9,8,128]{3,2,1,0:T(8,128)(2,1)S(1)}, u32[]{:S(2)}, u32[]{:S(2)}) collective-permute-start(bf16[4,9,8,128]{3,2,1,0:T(8,128)(2,1)S(1)} %reduce_sum.28), channel_id=1, source_target_pairs={{0,8},{8,0},{16,24},{24,16},{1,9},{9,1},{17,25},{25,17},{2,10},{10... | collective-permute-start | bytes 221192 | tf_op jit(solution)/shard_map/ppermute | solution.py:70
  60.6 6.3 %collective-permute-start.12 = (bf16[4,9,8,128]{3,2,1,0:T(8,128)(2,1)S(1)}, bf16[4,9,8,128]{3,2,1,0:T(8,128)(2,1)S(1)}, u32[]{:S(2)}, u32[]{:S(2)}) collective-permute-start(bf16[4,9,8,128]{3,2,1,0:T(8,128)(2,1)S(1)} %reduce_sum.28), channel_id=1, source_target_pairs={{0,24},{8,16},{16,8},{24,0},{1,25},{9,17},{17,9},{25,1},{2,26},{10... | collective-permute-start | bytes 221192 | tf_op jit(solution)/shard_map/ppermute | solution.py:70
  66.9 25.7 %copy-start.1 = (bf16[2048,1024]{1,0:T(8,128)(2,1)S(1)}, bf16[2048,1024]{1,0:T(8,128)(2,1)}, u32[]{:S(2)}) copy-start(bf16[2048,1024]{1,0:T(8,128)(2,1)} %w.5) | copy-start | bytes 12582916
  84.0 6.0 %collective-permute-start.15 = (bf16[4,6,8,128]{3,2,1,0:T(8,128)(2,1)S(1)}, bf16[4,6,8,128]{3,2,1,0:T(8,128)(2,1)S(1)}, u32[]{:S(2)}, u32[]{:S(2)}) collective-permute-start(bf16[4,6,8,128]{3,2,1,0:T(8,128)(2,1)S(1)} %join.1), channel_id=1, source_target_pairs={{0,24},{8,16},{16,8},{24,0},{1,25},{9,17},{17,9},{25,1},{2,26},{10... | collective-permute-start | bytes 147464 | tf_op jit(solution)/shard_map/ppermute | solution.py:70
  85.7 5.4 %collective-permute-start.14 = (bf16[4,6,8,128]{3,2,1,0:T(8,128)(2,1)S(1)}, bf16[4,6,8,128]{3,2,1,0:T(8,128)(2,1)S(1)}, u32[]{:S(2)}, u32[]{:S(2)}) collective-permute-start(bf16[4,6,8,128]{3,2,1,0:T(8,128)(2,1)S(1)} %join.1), channel_id=1, source_target_pairs={{0,16},{8,24},{16,0},{24,8},{1,17},{9,25},{17,1},{25,9},{2,18},{10... | collective-permute-start | bytes 147464 | tf_op jit(solution)/shard_map/ppermute | solution.py:70
  86.2 4.8 %collective-permute-start.13 = (bf16[4,6,8,128]{3,2,1,0:T(8,128)(2,1)S(1)}, bf16[4,6,8,128]{3,2,1,0:T(8,128)(2,1)S(1)}, u32[]{:S(2)}, u32[]{:S(2)}) collective-permute-start(bf16[4,6,8,128]{3,2,1,0:T(8,128)(2,1)S(1)} %join.1), channel_id=1, source_target_pairs={{0,8},{8,0},{16,24},{24,16},{1,9},{9,1},{17,25},{25,17},{2,10},{10... | collective-permute-start | bytes 147464 | tf_op jit(solution)/shard_map/ppermute | solution.py:70
  91.1 1.5 collective-permute-start.16
  94.2 10.7 %copy-start.8 = (bf16[4,3,8,1024]{3,2,1,0:T(8,128)(2,1)S(1)}, bf16[4,3,8,1024]{3,2,1,0:T(8,128)(2,1)}, u32[]{:S(2)}) copy-start(bf16[4,3,8,1024]{3,2,1,0:T(8,128)(2,1)} %copy-done.7) | copy-start | bytes 589828
  94.2 4.9 %collective-permute-start.17 = (bf16[4,3,8,512]{3,2,1,0:T(8,128)(2,1)S(1)}, bf16[4,3,8,512]{3,2,1,0:T(8,128)(2,1)S(1)}, u32[]{:S(2)}, u32[]{:S(2)}) collective-permute-start(bf16[4,3,8,512]{3,2,1,0:T(8,128)(2,1)S(1)} %get-tuple-element.46), channel_id=1, source_target_pairs={{0,1},{1,0},{2,3},{3,2},{4,5},{5,4},{6,7},{7,6},{8,9},{9,8},{10,11... | collective-permute-start | bytes 294920 | tf_op jit(solution)/shard_map/ppermute | solution.py:70
  95.5 4.6 %collective-permute-start.19 = (bf16[4,3,8,512]{3,2,1,0:T(8,128)(2,1)S(1)}, bf16[4,3,8,512]{3,2,1,0:T(8,128)(2,1)S(1)}, u32[]{:S(2)}, u32[]{:S(2)}) collective-permute-start(bf16[4,3,8,512]{3,2,1,0:T(8,128)(2,1)S(1)} %get-tuple-element.47), channel_id=1, source_target_pairs={{0,2},{1,3},{2,0},{3,1},{4,6},{5,7},{6,4},{7,5},{8,10},{9,11},{10,... | collective-permute-start | bytes 294920 | tf_op jit(solution)/shard_map/ppermute | solution.py:70
  99.1 4.7 %collective-permute-start.18 = (bf16[4,3,8,512]{3,2,1,0:T(8,128)(2,1)S(1)}, bf16[4,3,8,512]{3,2,1,0:T(8,128)(2,1)S(1)}, u32[]{:S(2)}, u32[]{:S(2)}) collective-permute-start(bf16[4,3,8,512]{3,2,1,0:T(8,128)(2,1)S(1)} %fusion.13), channel_id=1, source_target_pairs={{0,2},{1,3},{2,0},{3,1},{4,6},{5,7},{6,4},{7,5},{8,10},{9,11},{10,... | collective-permute-start | bytes 294920 | tf_op jit(solution)/shard_map/ppermute | solution.py:70
  100.1 12.9 %copy-start.10 = (f32[1024]{0:T(1024)S(1)}, f32[1024]{0:T(1024)}, u32[]{:S(2)}) copy-start(f32[1024]{0:T(1024)} %param.16) | copy-start | bytes 12292
  100.2 4.7 %collective-permute-start.20 = (bf16[4,3,8,512]{3,2,1,0:T(8,128)(2,1)S(1)}, bf16[4,3,8,512]{3,2,1,0:T(8,128)(2,1)S(1)}, u32[]{:S(2)}, u32[]{:S(2)}) collective-permute-start(bf16[4,3,8,512]{3,2,1,0:T(8,128)(2,1)S(1)} %fusion.12), channel_id=1, source_target_pairs={{0,1},{1,0},{2,3},{3,2},{4,5},{5,4},{6,7},{7,6},{8,9},{9,8},{10,11... | collective-permute-start | bytes 294920 | tf_op jit(solution)/shard_map/ppermute | solution.py:70
  105.1 1.2 collective-permute-start.21
  106.3 5.5 %collective-permute-start.24 = (f32[16,128]{1,0:T(8,128)S(1)}, f32[16,128]{1,0:T(8,128)S(1)}, u32[]{:S(2)}, u32[]{:S(2)}) collective-permute-start(f32[16,128]{1,0:T(8,128)S(1)} %pad_add_fusion.1), channel_id=1, source_target_pairs={{0,24},{8,16},{16,8},{24,0},{1,25},{9,17},{17,9},{25,1},{2,26},{10... | collective-permute-start | bytes 24584 | tf_op jit(solution)/shard_map/ppermute | solution.py:70
  108.2 4.5 %collective-permute-start.23 = (f32[16,128]{1,0:T(8,128)S(1)}, f32[16,128]{1,0:T(8,128)S(1)}, u32[]{:S(2)}, u32[]{:S(2)}) collective-permute-start(f32[16,128]{1,0:T(8,128)S(1)} %pad_add_fusion.1), channel_id=1, source_target_pairs={{0,16},{8,24},{16,0},{24,8},{1,17},{9,25},{17,1},{25,9},{2,18},{10... | collective-permute-start | bytes 24584 | tf_op jit(solution)/shard_map/ppermute | solution.py:70
  109.4 3.7 %collective-permute-start.22 = (f32[16,128]{1,0:T(8,128)S(1)}, f32[16,128]{1,0:T(8,128)S(1)}, u32[]{:S(2)}, u32[]{:S(2)}) collective-permute-start(f32[16,128]{1,0:T(8,128)S(1)} %pad_add_fusion.1), channel_id=1, source_target_pairs={{0,8},{8,0},{16,24},{24,16},{1,9},{9,1},{17,25},{25,17},{2,10},{10... | collective-permute-start | bytes 24584 | tf_op jit(solution)/shard_map/ppermute | solution.py:70
  110.7 10.0 %collective-permute-start.40 = (bf16[2,3,8,512]{3,2,1,0:T(8,128)(2,1)S(1)}, bf16[2,3,8,512]{3,2,1,0:T(8,128)(2,1)S(1)}, u32[]{:S(2)}, u32[]{:S(2)}) collective-permute-start(bf16[2,3,8,512]{3,2,1,0:T(8,128)(2,1)S(1)} %get-tuple-element.51), channel_id=1, source_target_pairs={{0,4},{4,0},{1,5},{5,1},{2,6},{6,2},{3,7},{7,3},{8,12},{12,8},{9,1... | collective-permute-start | bytes 147464 | tf_op jit(solution)/shard_map/ppermute | solution.py:70
  120.6 2.5 %collective-permute-start.25 = (bf16[4,2,96,512]{3,2,1,0:T(8,128)(2,1)S(1)}, bf16[4,2,96,512]{3,2,1,0:T(8,128)(2,1)}, u32[]{:S(2)}, u32[]{:S(2)}) collective-permute-start(bf16[4,2,96,512]{3,2,1,0:T(8,128)(2,1)S(1)} %slice_bitcast_fusion), channel_id=1, source_target_pairs={{0,4},{4,0},{1,5},{5,1},{2,6},{6,2},{3,7},{7,3},{8,12},{12,8},{9,1... | collective-permute-start | bytes 2359304 | tf_op jit(solution)/shard_map/ppermute | solution.py:70
  124.5 11.2 %collective-permute-start.26 = (bf16[2,2,96,512]{3,2,1,0:T(8,128)(2,1)S(1)}, bf16[2,2,96,512]{3,2,1,0:T(8,128)(2,1)S(1)}, u32[]{:S(2)}, u32[]{:S(2)}) collective-permute-start(bf16[2,2,96,512]{3,2,1,0:T(8,128)(2,1)S(1)} %slice.103), channel_id=1, source_target_pairs={{0,8},{8,0},{16,24},{24,16},{1,9},{9,1},{17,25},{25,17},{2,10},{10... | collective-permute-start | bytes 1179656 | tf_op jit(solution)/shard_map/ppermute | solution.py:70
  132.2 5.5 %collective-permute-start.31 = (bf16[4,2,96,384]{3,2,1,0:T(8,128)(2,1)S(1)}, bf16[4,2,96,384]{3,2,1,0:T(8,128)(2,1)S(1)}, u32[]{:S(2)}, u32[]{:S(2)}) collective-permute-start(bf16[4,2,96,384]{3,2,1,0:T(8,128)(2,1)S(1)} %slice_bitcast_fusion.2), channel_id=1, source_target_pairs={{0,4},{4,0},{1,5},{5,1},{2,6},{6,2},{3,7},{7,3},{8,12},{12,8},{9,1... | collective-permute-start | bytes 1769480 | tf_op jit(solution)/shard_map/ppermute | solution.py:70
  135.8 11.4 %collective-permute-start.27 = (bf16[1,2,96,512]{3,2,1,0:T(8,128)(2,1)S(1)}, bf16[1,2,96,512]{3,2,1,0:T(8,128)(2,1)S(1)}, u32[]{:S(2)}, u32[]{:S(2)}) collective-permute-start(bf16[1,2,96,512]{3,2,1,0:T(8,128)(2,1)S(1)} %slice.138), channel_id=1, source_target_pairs={{0,16},{8,24},{16,0},{24,8},{1,17},{9,25},{17,1},{25,9},{2,18},{10... | collective-permute-start | bytes 589832 | tf_op jit(solution)/shard_map/ppermute | solution.py:70
  137.9 11.4 %collective-permute-start.32 = (bf16[2,2,96,384]{3,2,1,0:T(8,128)(2,1)S(1)}, bf16[2,2,96,384]{3,2,1,0:T(8,128)(2,1)S(1)}, u32[]{:S(2)}, u32[]{:S(2)}) collective-permute-start(bf16[2,2,96,384]{3,2,1,0:T(8,128)(2,1)S(1)} %slice.109), channel_id=1, source_target_pairs={{0,8},{8,0},{16,24},{24,16},{1,9},{9,1},{17,25},{25,17},{2,10},{10... | collective-permute-start | bytes 884744 | tf_op jit(solution)/shard_map/ppermute | solution.py:70
  147.4 10.3 %collective-permute-start.28 = (bf16[1,96,512]{2,1,0:T(8,128)(2,1)S(1)}, bf16[1,96,512]{2,1,0:T(8,128)(2,1)S(1)}, u32[]{:S(2)}, u32[]{:S(2)}) collective-permute-start(bf16[1,96,512]{2,1,0:T(8,128)(2,1)S(1)} %fusion.11), channel_id=1, source_target_pairs={{0,16},{8,24},{16,0},{24,8},{1,17},{9,25},{17,1},{25,9},{2,18},{10... | collective-permute-start | bytes 294920 | tf_op jit(solution)/shard_map/ppermute | solution.py:70
  149.4 10.7 %collective-permute-start.33 = (bf16[1,2,96,384]{3,2,1,0:T(8,128)(2,1)S(1)}, bf16[1,2,96,384]{3,2,1,0:T(8,128)(2,1)S(1)}, u32[]{:S(2)}, u32[]{:S(2)}) collective-permute-start(bf16[1,2,96,384]{3,2,1,0:T(8,128)(2,1)S(1)} %slice.142), channel_id=1, source_target_pairs={{0,16},{8,24},{16,0},{24,8},{1,17},{9,25},{17,1},{25,9},{2,18},{10... | collective-permute-start | bytes 442376 | tf_op jit(solution)/shard_map/ppermute | solution.py:70
  157.7 7.3 %collective-permute-start.29 = (bf16[2,96,512]{2,1,0:T(8,128)(2,1)S(1)}, bf16[2,96,512]{2,1,0:T(8,128)(2,1)S(1)}, u32[]{:S(2)}, u32[]{:S(2)}) collective-permute-start(bf16[2,96,512]{2,1,0:T(8,128)(2,1)S(1)} %pad_maximum_fusion.5), channel_id=1, source_target_pairs={{0,8},{8,0},{16,24},{24,16},{1,9},{9,1},{17,25},{25,17},{2,10},{10... | collective-permute-start | bytes 589832 | tf_op jit(solution)/shard_map/ppermute | solution.py:70
  160.2 5.6 %collective-permute-start.34 = (bf16[1,96,384]{2,1,0:T(8,128)(2,1)S(1)}, bf16[1,96,384]{2,1,0:T(8,128)(2,1)S(1)}, u32[]{:S(2)}, u32[]{:S(2)}) collective-permute-start(bf16[1,96,384]{2,1,0:T(8,128)(2,1)S(1)} %fusion.15), channel_id=1, source_target_pairs={{0,16},{8,24},{16,0},{24,8},{1,17},{9,25},{17,1},{25,9},{2,18},{10... | collective-permute-start | bytes 221192 | tf_op jit(solution)/shard_map/ppermute | solution.py:70
  165.0 6.6 %collective-permute-start.30 = (bf16[1,4,96,512]{3,2,1,0:T(8,128)(2,1)S(1)}, bf16[1,4,96,512]{3,2,1,0:T(8,128)(2,1)S(1)}, u32[]{:S(2)}, u32[]{:S(2)}) collective-permute-start(bf16[1,4,96,512]{3,2,1,0:T(8,128)(2,1)S(1)} %maximum_bitcast_fusion), channel_id=1, source_target_pairs={{0,4},{4,0},{1,5},{5,1},{2,6},{6,2},{3,7},{7,3},{8,12},{12,8},{9,1... | collective-permute-start | bytes 1179656 | tf_op jit(solution)/shard_map/ppermute | solution.py:70
  165.8 5.7 %collective-permute-start.35 = (bf16[2,96,384]{2,1,0:T(8,128)(2,1)S(1)}, bf16[2,96,384]{2,1,0:T(8,128)(2,1)S(1)}, u32[]{:S(2)}, u32[]{:S(2)}) collective-permute-start(bf16[2,96,384]{2,1,0:T(8,128)(2,1)S(1)} %pad_maximum_fusion.6), channel_id=1, source_target_pairs={{0,8},{8,0},{16,24},{24,16},{1,9},{9,1},{17,25},{25,17},{2,10},{10... | collective-permute-start | bytes 442376 | tf_op jit(solution)/shard_map/ppermute | solution.py:70
  171.5 4.8 %collective-permute-start.36 = (bf16[1,4,96,384]{3,2,1,0:T(8,128)(2,1)S(1)}, bf16[1,4,96,384]{3,2,1,0:T(8,128)(2,1)S(1)}, u32[]{:S(2)}, u32[]{:S(2)}) collective-permute-start(bf16[1,4,96,384]{3,2,1,0:T(8,128)(2,1)S(1)} %maximum_bitcast_fusion.1), channel_id=1, source_target_pairs={{0,4},{4,0},{1,5},{5,1},{2,6},{6,2},{3,7},{7,3},{8,12},{12,8},{9,1... | collective-permute-start | bytes 884744 | tf_op jit(solution)/shard_map/ppermute | solution.py:70
  180.4 4.3 %collective-permute-start.37 = (bf16[3,8,1024]{2,1,0:T(8,128)(2,1)S(1)}, bf16[3,8,1024]{2,1,0:T(8,128)(2,1)S(1)}, u32[]{:S(2)}, u32[]{:S(2)}) collective-permute-start(bf16[3,8,1024]{2,1,0:T(8,128)(2,1)S(1)} %get-tuple-element.58), channel_id=1, source_target_pairs={{0,1},{1,0},{2,3},{3,2},{4,5},{5,4},{6,7},{7,6},{8,9},{9,8},{10,11... | collective-permute-start | bytes 147464 | tf_op jit(solution)/shard_map/ppermute | solution.py:70
  181.2 5.0 %collective-permute-start.39 = (bf16[3,8,1024]{2,1,0:T(8,128)(2,1)S(1)}, bf16[3,8,1024]{2,1,0:T(8,128)(2,1)S(1)}, u32[]{:S(2)}, u32[]{:S(2)}) collective-permute-start(bf16[3,8,1024]{2,1,0:T(8,128)(2,1)S(1)} %get-tuple-element.59), channel_id=1, source_target_pairs={{0,3},{1,2},{2,1},{3,0},{4,7},{5,6},{6,5},{7,4},{8,11},{9,10},{10,... | collective-permute-start | bytes 147464 | tf_op jit(solution)/shard_map/ppermute | solution.py:70
  182.9 4.2 %collective-permute-start.38 = (bf16[3,8,1024]{2,1,0:T(8,128)(2,1)S(1)}, bf16[3,8,1024]{2,1,0:T(8,128)(2,1)S(1)}, u32[]{:S(2)}, u32[]{:S(2)}) collective-permute-start(bf16[3,8,1024]{2,1,0:T(8,128)(2,1)S(1)} %get-tuple-element.60), channel_id=1, source_target_pairs={{0,2},{1,3},{2,0},{3,1},{4,6},{5,7},{6,4},{7,5},{8,10},{9,11},{10,... | collective-permute-start | bytes 147464 | tf_op jit(solution)/shard_map/ppermute | solution.py:70

commit v5 on v4

--- a/solution.py
+++ b/solution.py
@@ -100,6 +100,13 @@
     return functools.reduce(jnp.add, [x] + [swap(x, axis, k) for k in range(1, n)])
 
 
+def sum_chips(x):
+    n = x.shape[0]
+    if n > 4:
+        return reduce_rounds(x, "z", bits(n)[::-1])
+    return functools.reduce(jnp.add, [x[0]] + [swap(x[k], "z", k) for k in range(1, n)])
+
+
 def add_round(x, axis, order):
     for bit in order:
         half = x.shape[0] // 2
@@ -154,16 +161,17 @@
     return functools.reduce(jnp.add, [a.astype(F32) for a in [x[0]] + arrived])
 
 
-def gather_prefix(x):
-    x = gather_rounds(x, "z", bits(lax.axis_size("z"))[::-1])
+def gather_prefix(x, direct):
+    x = gather(x, "z") if direct else gather_rounds(x, "z", bits(lax.axis_size("z"))[::-1])
     x = gather_rounds(x, "core", [1])
     return x.reshape((-1,) + x.shape[2:])
 
 
-def place_table():
+def place_table(direct):
     z_count = lax.axis_size("z")
     owner = jnp.arange(z_count * CORES, dtype=jnp.int32)
-    far = mirror((owner // CORES) ^ lax.axis_index("z"), z_count)
+    far = (owner // CORES) ^ lax.axis_index("z")
+    far = far if direct else mirror(far, z_count)
     return (((owner % CORES) ^ lax.axis_index("core")) * z_count + far).astype(jnp.int32)
 
 
@@ -194,7 +202,7 @@
     project = np.zeros((branches, heads_in), np.int32)
     for head, rank in rank_in.items():
         project[head // heads_in, head % heads_in] = rank * steps * CORES + key_head(head) % CORES
-    fetch = np.zeros((z_count, CORES, kv_core, GROUP + 2, steps), np.int32)
+    fetch = np.zeros((z_count, CORES, branches, kv_core, GROUP + 2, steps), np.int32)
     send = np.zeros((CORES, kv_core, GROUP, steps), np.int32)
     mix = np.zeros((z_count, CORES, branches, heads_out, steps), np.int32)
     for s in range(steps):
@@ -205,8 +213,9 @@
                 for n, head in enumerate(heads):
                     chip, tile = divmod(rank_in[head] * steps + s, tiles_in)
                     for z in range(z_count):
-                        row = (chip ^ z) * branches + head // heads_in
-                        fetch[z, core, j, n, s] = row * tiles_in + tile
+                        for b in range(branches):
+                            row = (chip ^ z) * branches + (head // heads_in ^ b)
+                            fetch[z, core, b, j, n, s] = row * tiles_in + tile
                     if head < HEADS:
                         chip, tile = divmod(rank_out[head] * steps + s, tiles_out)
                         row = chip * branches + head // heads_out
@@ -221,7 +230,7 @@
     full = (z_count, CORES, branches)
     parts = [
         np.broadcast_to(project[None, None], full + project.shape[1:]),
-        np.broadcast_to(fetch.reshape(z_count, CORES, 1, -1), full + (fetch[0, 0].size,)),
+        fetch.reshape(full + (-1,)),
         np.broadcast_to(send.reshape(1, CORES, 1, -1), full + (send[0].size,)),
         mix.reshape(full + (-1,)),
     ]
@@ -263,7 +272,7 @@
                 index = code // CORES + s
                 for k in range(branches):
                     row = (k * steps + s) * SUB
-                    out[side, index // tiles, ids[2] ^ k, index % tiles] = acc[
+                    out[side, (index // tiles) ^ ids[0], k, index % tiles] = acc[
                         row : row + SUB, hh * HD : (hh + 1) * HD
                     ]
 
@@ -664,7 +673,6 @@
     width = width_dev * prefix
     near = bits(z_count)
     across = bits(branches)
-    places = place_table()
     ids = jnp.stack([lax.axis_index(a) for a in AXES]).astype(jnp.int32)
 
     tiles_in, tiles_out, table, (_, fetch, send, mix, _) = head_tables(steps, z_count, branches)
@@ -689,8 +697,8 @@
     part_sums = project_qkv(ids, table, lhs, w_qkv, steps, z_count, branches, tiles_in)
     chip_sums = part_sums[0] + swap(part_sums[1], "core", 1)
     plane = z_count * branches
-    received = exchange(chip_sums.reshape(plane, tiles_in, SUB, HD), ("z", "branch"))
-    summed = jnp.sum(received.reshape(z_count, branches, tiles_in, SUB, HD), axis=0).astype(BF16)
+    summed = sum_chips(chip_sums).astype(BF16)
+    summed = jnp.stack([summed[0]] + [swap(summed[k], "branch", k) for k in range(1, branches)])
     qkv = gather(summed, "z").reshape(-1, SUB, HD)
 
     softmax_parts, new_kv = attend(
@@ -698,8 +706,7 @@
     )
     received = exchange(softmax_parts, ("z", "branch"))
     attended = join(received.reshape(z_count, branches, tiles_out + 1, SUB, HD))
-    attended = gather_rounds(gather(attended, "z"), "core", [1])
-    attended = attended.reshape((prefix,) + attended.shape[2:])
+    attended = gather_prefix(attended, True)
     new_kv = both_cores(new_kv).transpose(2, 0, 1, 3)
 
     mixed = sum_branches(*mix_heads(ids, table, mix, attended, w_out, steps))
@@ -715,9 +722,10 @@
         chip_sums = add(part_sums[0], swap(part_sums[1], "core", 1))
         lhs, chip_sums = lax.optimization_barrier((lhs, chip_sums))
         gate, up = add_round(chip_sums, "z", near)
-        activation = gather_prefix((jax.nn.silu(gate) * up).astype(BF16))
-        shape = (branches, steps, rows, width_dev) if start == spans[-1][0] else None
-        down = [project_down(places, down, activation, w_down, unit, start, shape)]
+        last = start == spans[-1][0]
+        activation = gather_prefix((jax.nn.silu(gate) * up).astype(BF16), last)
+        shape = (branches, steps, rows, width_dev) if last else None
+        down = [project_down(place_table(last), down, activation, w_down, unit, start, shape)]
     result = (residual[0].astype(F32) + own_sum(down[0])).astype(BF16)
     return (result, new_kv)
 

time: 188 us -> 203 us (1.080)
  waiting for transfers between devices: 65.3 us -> 88.1 us
  blocking collectives: 34.3 us -> 14 us
  starting transfers between devices: 36.7 us -> 49.2 us
    ppermute x41 -> x48, waiting for transfers between devices: 65.3 us -> 88.1 us  [swap(): lax.ppermute(x, axis, [(i, i ^ bit) for i in range(lax.axis_size(axis))])]
    all_to_all x2 -> x1, blocking collectives: 34.3 us -> 14 us  [exchange(): return lax.all_to_all(x, axes, split_axis=0, concat_axis=0, tiled=True)]
    ppermute x41 -> x48, starting transfers between devices: 36.7 us -> 49.2 us  [swap(): lax.ppermute(x, axis, [(i, i ^ bit) for i in range(lax.axis_size(axis))])]
    unnamed x30 -> x28, local copies, waits for them, and re-layouts: 7.1 us -> 7.1 us
  transfers between devices with their start and end apart: 41 -> 48, of which waited for: 30 -> 29; matrix products, arithmetic and copies ran while one was open for 2% -> 2% of each run, Pallas kernels for 11% -> 7%
where the time goes in v5:
time: 203 us; the launch traced here: 202 us
  waiting for transfers between devices  88.1 us (43%)
  starting transfers between devices  49.2 us (24%)
  Pallas kernels  34.7 us (17%)
  blocking collectives  14 us (7%)
  local copies, waits for them, and re-layouts  9.03 us (4%)
  other arithmetic  6.16 us (3%)
    ppermute x48, waiting for transfers between devices, swap(): lax.ppermute(x, axis, [(i, i ^ bit) for i in range(lax.axis_size(axis))])  88.1 us
    ppermute x48, starting transfers between devices, swap(): lax.ppermute(x, axis, [(i, i ^ bit) for i in range(lax.axis_size(axis))])  49.2 us
    all_to_all x1, blocking collectives, exchange(): return lax.all_to_all(x, axes, split_axis=0, concat_axis=0, tiled=True)  14 us
    pallas_call x2, Pallas kernels, project_gate_up(): pl.pallas_call(functools.partial(gate_up_kernel, unit, start), in_specs=[...  13.6 us
    pallas_call x2, Pallas kernels, project_down(): pl.pallas_call(functools.partial(down_kernel, unit, start), in_specs=[IN_...  8.66 us
    unnamed x28, local copies, waits for them, and re-layouts  7.1 us
    pallas_call x1, Pallas kernels, attend(): pl.pallas_call(functools.partial(attend_kernel, fetch, send), in_specs=[I...  4.85 us
  transfers between devices with their start and end apart: 48, of which 29 were waited for; matrix products, arithmetic and copies ran while one was open for 2% of the time, Pallas kernels for 7%

profile of v5, /device:TPU:0, one launch (start us, length us, event | category | flops | bytes accessed | tf_op | source)
XLA Modules:
  0.0 202.4 jit_solution(11033206768134038318)
XLA Ops:
  0.6 3.0 %collective-permute-start = (bf16[3,8,1024]{2,1,0:T(8,128)(2,1)}, bf16[3,8,1024]{2,1,0:T(8,128)(2,1)S(1)}, u32[]{:S(2)}, u32[]{:S(2)}) collective-permute-start(bf16[3,8,1024]{2,1,0:T(8,128)(2,1)} %param.14), channel_id=1, source_target_pairs={{0,1},{1,0},{2,3},{3,2},{4,5},{5,4},{6,7},{7,6},{8,9},{9,8},{10,11... | collective-permute-start | bytes 147464 | tf_op jit(solution)/shard_map/ppermute | solution.py:70
  3.6 1.5 collective-permute-start.1
  5.8 1.7 prepare.1
  8.3 2.0 %collective-permute-done.2 = bf16[3,8,1024]{2,1,0:T(8,128)(2,1)S(1)} collective-permute-done((bf16[3,8,1024]{2,1,0:T(8,128)(2,1)}, bf16[3,8,1024]{2,1,0:T(8,128)(2,1)S(1)}, u32[]{:S(2)}, u32[]{:S(2)}) %collective-permute-start.2) | collective-permute-done | bytes 49184 | tf_op jit(solution)/shard_map/ppermute | solution.py:70
  10.4 0.8 pad_maximum_fusion.4
  11.2 1.6 copy-done.2
  12.8 1.6 copy-done.3
  15.0 2.3 %cut.1 = (bf16[1,2,512,512]{3,2,1,0:T(8,128)(2,1)S(1)}, bf16[1,2,512,512]{3,2,1,0:T(8,128)(2,1)}, bf16[8,2,64,512]{3,2,1,0:T(8,128)(2,1)S(1)}, bf16[8,2,64,512]{3,2,1,0:T(8,128)(2,1)}) custom-call(s32[3]{0:T(128)S(1)} %copy-done.5, bf16[1,2,512,1024]{3,2,1,0:T(8,128)(2,1)S(1)} %copy-done.2, bf16[8,2,64,1024]{3,2,1,0:T(8,128)(2,1)S(1)} %copy-done.3), custom_call_target="tpu_custom_call" | custom-call | bytes 8388608 | tf_op jit(solution)/shard_map/cut/pallas_call | solution.py:599
  18.3 2.5 %collective-permute-done.3 = f32[16,128]{1,0:T(8,128)S(1)} collective-permute-done((f32[16,128]{1,0:T(8,128)S(1)}, f32[16,128]{1,0:T(8,128)S(1)}, u32[]{:S(2)}, u32[]{:S(2)}) %collective-permute-start.3) | collective-permute-done | bytes 8224 | tf_op jit(solution)/shard_map/ppermute | solution.py:70
  20.8 1.6 collective-permute-start.4
  22.3 2.6 %collective-permute-start.5 = (f32[16,128]{1,0:T(8,128)S(1)}, f32[16,128]{1,0:T(8,128)S(1)}, u32[]{:S(2)}, u32[]{:S(2)}) collective-permute-start(f32[16,128]{1,0:T(8,128)S(1)} %pad_add_fusion.2), channel_id=1, source_target_pairs={{0,16},{8,24},{16,0},{24,8},{1,17},{9,25},{17,1},{25,9},{2,18},{10... | collective-permute-start | bytes 24584 | tf_op jit(solution)/shard_map/ppermute | solution.py:70
  26.0 0.9 collective-permute-done.5
  26.9 3.5 %collective-permute-done.6 = f32[16,128]{1,0:T(8,128)S(1)} collective-permute-done((f32[16,128]{1,0:T(8,128)S(1)}, f32[16,128]{1,0:T(8,128)S(1)}, u32[]{:S(2)}, u32[]{:S(2)}) %collective-permute-start.6) | collective-permute-done | bytes 8224 | tf_op jit(solution)/shard_map/ppermute | solution.py:70
  30.6 2.5 %copy-done = bf16[1024,2560]{1,0:T(8,128)(2,1)S(1)} copy-done((bf16[1024,2560]{1,0:T(8,128)(2,1)S(1)}, bf16[1024,2560]{1,0:T(8,128)(2,1)}, u32[]{:S(2)}) %copy-start) | copy-done | bytes 5242904
  33.1 1.7 qkv.1
  34.9 2.0 collective-permute-done.9
  37.9 3.6 %collective-permute-start.12 = (f32[4,9,8,128]{3,2,1,0:T(8,128)S(1)}, f32[4,9,8,128]{3,2,1,0:T(8,128)S(1)}, u32[]{:S(2)}, u32[]{:S(2)}) collective-permute-start(f32[4,9,8,128]{3,2,1,0:T(8,128)S(1)} %get-tuple-element.59), channel_id=1, source_target_pairs={{0,24},{8,16},{16,8},{24,0},{1,25},{9,17},{17,9},{25,1},{2,26},{10... | collective-permute-start | bytes 442376 | tf_op jit(solution)/shard_map/ppermute | solution.py:70
  41.5 2.7 %collective-permute-done.10 = f32[4,9,8,128]{3,2,1,0:T(8,128)S(1)} collective-permute-done((f32[4,9,8,128]{3,2,1,0:T(8,128)S(1)}, f32[4,9,8,128]{3,2,1,0:T(8,128)S(1)}, u32[]{:S(2)}, u32[]{:S(2)}) %collective-permute-start.10) | collective-permute-done | bytes 147488 | tf_op jit(solution)/shard_map/ppermute | solution.py:70
  44.2 6.9 %collective-permute-done.11 = f32[4,9,8,128]{3,2,1,0:T(8,128)S(1)} collective-permute-done((f32[4,9,8,128]{3,2,1,0:T(8,128)S(1)}, f32[4,9,8,128]{3,2,1,0:T(8,128)S(1)}, u32[]{:S(2)}, u32[]{:S(2)}) %collective-permute-start.11) | collective-permute-done | bytes 147488 | tf_op jit(solution)/shard_map/ppermute | solution.py:70
  51.8 0.9 collective-permute-start.14
  52.7 2.1 %collective-permute-start.15 = (bf16[9,8,128]{2,1,0:T(8,128)(2,1)S(1)}, bf16[9,8,128]{2,1,0:T(8,128)(2,1)S(1)}, u32[]{:S(2)}, u32[]{:S(2)}) collective-permute-start(bf16[9,8,128]{2,1,0:T(8,128)(2,1)S(1)} %get-tuple-element.69), channel_id=1, source_target_pairs={{0,3},{1,2},{2,1},{3,0},{4,7},{5,6},{6,5},{7,4},{8,11},{9,10},{10,... | collective-permute-start | bytes 55304 | tf_op jit(solution)/shard_map/ppermute | solution.py:70
  55.5 1.8 collective-permute-done.15
  57.4 3.0 %collective-permute-start.16 = (bf16[4,9,8,128]{3,2,1,0:T(8,128)(2,1)S(1)}, bf16[4,9,8,128]{3,2,1,0:T(8,128)(2,1)S(1)}, u32[]{:S(2)}, u32[]{:S(2)}) collective-permute-start(bf16[4,9,8,128]{3,2,1,0:T(8,128)(2,1)S(1)} %get-tuple-element.67), channel_id=1, source_target_pairs={{0,8},{8,0},{16,24},{24,16},{1,9},{9,1},{17,25},{25,17},{2,10},{10... | collective-permute-start | bytes 221192 | tf_op jit(solution)/shard_map/ppermute | solution.py:70
  60.4 2.4 %collective-permute-start.18 = (bf16[4,9,8,128]{3,2,1,0:T(8,128)(2,1)S(1)}, bf16[4,9,8,128]{3,2,1,0:T(8,128)(2,1)S(1)}, u32[]{:S(2)}, u32[]{:S(2)}) collective-permute-start(bf16[4,9,8,128]{3,2,1,0:T(8,128)(2,1)S(1)} %get-tuple-element.67), channel_id=1, source_target_pairs={{0,24},{8,16},{16,8},{24,0},{1,25},{9,17},{17,9},{25,1},{2,26},{10... | collective-permute-start | bytes 221192 | tf_op jit(solution)/shard_map/ppermute | solution.py:70
  62.8 1.4 collective-permute-done.16
  64.1 2.5 %collective-permute-done.17 = bf16[4,9,8,128]{3,2,1,0:T(8,128)(2,1)S(1)} collective-permute-done((bf16[4,9,8,128]{3,2,1,0:T(8,128)(2,1)S(1)}, bf16[4,9,8,128]{3,2,1,0:T(8,128)(2,1)S(1)}, u32[]{:S(2)}, u32[]{:S(2)}) %collective-permute-start.17) | collective-permute-done | bytes 73760 | tf_op jit(solution)/shard_map/ppermute | solution.py:70
  66.8 4.9 %attend.1 = (bf16[16,7,8,128]{3,2,1,0:T(8,128)(2,1)S(1)}, bf16[2,3,8,512]{3,2,1,0:T(8,128)(2,1)S(1)}) custom-call(s32[284]{0:T(512)S(1)} %dynamic-slice_reduce_fusion.table, bf16[144,8,128]{2,1,0:T(8,128)(2,1)S(1)} %bitcast.163, f32[3,8,128]{2,1,0:T(8,128)S(1)} %get-tuple-element.38.cosine, f32[3,8,128]{2,1,0:T(8,128)S(1)} %get-tuple-element.39.sine, ...), custom_call_target="tpu_custom_call" | custom-call | flops 1073741824 | bytes 4194304 | tf_op jit(solution)/shard_map/attend/pallas_call | solution.py:554
  71.6 14.0 %all_to_all.5 = bf16[16,7,8,128]{3,2,1,0:T(8,128)(2,1)S(1)} all-to-all(bf16[16,7,8,128]{3,2,1,0:T(8,128)(2,1)S(1)} %get-tuple-element.45), channel_id=1, replica_groups=mesh['z'=4,'core'=2,'branch'=4] {'z','branch'}, dimensions={0} | all-to-all | bytes 458752 | tf_op jit(solution)/shard_map/all_to_all | solution.py:45
  86.5 1.3 collective-permute-start.20
  87.7 2.7 %collective-permute-start.21 = (bf16[4,6,8,128]{3,2,1,0:T(8,128)(2,1)S(1)}, bf16[4,6,8,128]{3,2,1,0:T(8,128)(2,1)S(1)}, u32[]{:S(2)}, u32[]{:S(2)}) collective-permute-start(bf16[4,6,8,128]{3,2,1,0:T(8,128)(2,1)S(1)} %join.1), channel_id=1, source_target_pairs={{0,24},{8,16},{16,8},{24,0},{1,25},{9,17},{17,9},{25,1},{2,26},{10... | collective-permute-start | bytes 147464 | tf_op jit(solution)/shard_map/ppermute | solution.py:70
  90.4 1.0 collective-permute-done.20
  91.4 2.2 %collective-permute-done.21 = bf16[4,6,8,128]{3,2,1,0:T(8,128)(2,1)S(1)} collective-permute-done((bf16[4,6,8,128]{3,2,1,0:T(8,128)(2,1)S(1)}, bf16[4,6,8,128]{3,2,1,0:T(8,128)(2,1)S(1)}, u32[]{:S(2)}, u32[]{:S(2)}) %collective-permute-start.21) | collective-permute-done | bytes 49184 | tf_op jit(solution)/shard_map/ppermute | solution.py:70
  93.7 1.4 collective-permute-done.22
  95.2 1.5 mix.1
  96.8 0.8 collective-permute-start.23
  98.3 3.4 %collective-permute-done.23 = bf16[4,3,8,512]{3,2,1,0:T(8,128)(2,1)S(1)} collective-permute-done((bf16[4,3,8,512]{3,2,1,0:T(8,128)(2,1)S(1)}, bf16[4,3,8,512]{3,2,1,0:T(8,128)(2,1)S(1)}, u32[]{:S(2)}, u32[]{:S(2)}) %collective-permute-start.23) | collective-permute-done | bytes 98336 | tf_op jit(solution)/shard_map/ppermute | solution.py:70
  101.7 1.4 collective-permute-start.24
  103.6 2.8 %collective-permute-done.24 = bf16[4,3,8,512]{3,2,1,0:T(8,128)(2,1)S(1)} collective-permute-done((bf16[4,3,8,512]{3,2,1,0:T(8,128)(2,1)S(1)}, bf16[4,3,8,512]{3,2,1,0:T(8,128)(2,1)S(1)}, u32[]{:S(2)}, u32[]{:S(2)}) %collective-permute-start.24) | collective-permute-done | bytes 98336 | tf_op jit(solution)/shard_map/ppermute | solution.py:70
  106.5 1.4 collective-permute-done.26
  108.2 1.2 collective-permute-done.27
  109.3 2.8 %collective-permute-start.29 = (f32[16,128]{1,0:T(8,128)S(1)}, f32[16,128]{1,0:T(8,128)S(1)}, u32[]{:S(2)}, u32[]{:S(2)}) collective-permute-start(f32[16,128]{1,0:T(8,128)S(1)} %pad_add_fusion.1), channel_id=1, source_target_pairs={{0,16},{8,24},{16,0},{24,8},{1,17},{9,25},{17,1},{25,9},{2,18},{10... | collective-permute-start | bytes 24584 | tf_op jit(solution)/shard_map/ppermute | solution.py:70
  112.2 1.5 collective-permute-start.30
  114.0 3.7 %collective-permute-done.30 = f32[16,128]{1,0:T(8,128)S(1)} collective-permute-done((f32[16,128]{1,0:T(8,128)S(1)}, f32[16,128]{1,0:T(8,128)S(1)}, u32[]{:S(2)}, u32[]{:S(2)}) %collective-permute-start.30) | collective-permute-done | bytes 8224 | tf_op jit(solution)/shard_map/ppermute | solution.py:70
  117.8 7.4 %gate_up.2 = bf16[2,4,2,96,512]{4,3,2,1,0:T(8,128)(2,1)S(1)} custom-call(s32[3]{0:T(128)S(1)} %copy-done.6, bf16[96,1024]{1,0:T(8,128)(2,1)S(1)} %bitcast.160, bf16[2,1024,7168]{2,1,0:T(8,128)(2,1)} %w.7), custom_call_target="tpu_custom_call" | custom-call | flops 1610612736 | bytes 16777216 | tf_op jit(solution)/shard_map/gate_up/pallas_call | solution.py:321
  125.4 2.3 %collective-permute-done.31 = bf16[4,2,96,512]{3,2,1,0:T(8,128)(2,1)} collective-permute-done((bf16[4,2,96,512]{3,2,1,0:T(8,128)(2,1)S(1)}, bf16[4,2,96,512]{3,2,1,0:T(8,128)(2,1)}, u32[]{:S(2)}, u32[]{:S(2)}) %collective-permute-start.31) | collective-permute-done | bytes 786464 | tf_op jit(solution)/shard_map/ppermute | solution.py:70
  127.7 1.3 fusion
  129.0 6.2 %gate_up.3 = bf16[2,4,2,96,384]{4,3,2,1,0:T(8,128)(2,1)S(1)} custom-call(s32[3]{0:T(128)S(1)} %copy-done.6, bf16[96,1024]{1,0:T(8,128)(2,1)S(1)} %bitcast.161, bf16[2,1024,7168]{2,1,0:T(8,128)(2,1)} %w.7), custom_call_target="tpu_custom_call" | custom-call | flops 1207959552 | bytes 12582912 | tf_op jit(solution)/shard_map/gate_up/pallas_call | solution.py:321
  135.7 11.3 %collective-permute-done.32 = bf16[2,2,96,512]{3,2,1,0:T(8,128)(2,1)S(1)} collective-permute-done((bf16[2,2,96,512]{3,2,1,0:T(8,128)(2,1)S(1)}, bf16[2,2,96,512]{3,2,1,0:T(8,128)(2,1)S(1)}, u32[]{:S(2)}, u32[]{:S(2)}) %collective-permute-start.32) | collective-permute-done | bytes 393248 | tf_op jit(solution)/shard_map/ppermute | solution.py:70
  147.8 1.8 collective-permute-start.38
  149.6 9.2 %collective-permute-done.33 = bf16[1,2,96,512]{3,2,1,0:T(8,128)(2,1)S(1)} collective-permute-done((bf16[1,2,96,512]{3,2,1,0:T(8,128)(2,1)S(1)}, bf16[1,2,96,512]{3,2,1,0:T(8,128)(2,1)S(1)}, u32[]{:S(2)}, u32[]{:S(2)}) %collective-permute-start.33) | collective-permute-done | bytes 196640 | tf_op jit(solution)/shard_map/ppermute | solution.py:70
  159.0 6.5 %collective-permute-done.34 = bf16[1,96,512]{2,1,0:T(8,128)(2,1)S(1)} collective-permute-done((bf16[1,96,512]{2,1,0:T(8,128)(2,1)S(1)}, bf16[1,96,512]{2,1,0:T(8,128)(2,1)S(1)}, u32[]{:S(2)}, u32[]{:S(2)}) %collective-permute-start.34) | collective-permute-done | bytes 98336 | tf_op jit(solution)/shard_map/ppermute | solution.py:70
  165.7 2.9 %collective-permute-start.39 = (bf16[1,2,96,384]{3,2,1,0:T(8,128)(2,1)S(1)}, bf16[1,2,96,384]{3,2,1,0:T(8,128)(2,1)S(1)}, u32[]{:S(2)}, u32[]{:S(2)}) collective-permute-start(bf16[1,2,96,384]{3,2,1,0:T(8,128)(2,1)S(1)} %slice.182), channel_id=1, source_target_pairs={{0,16},{8,24},{16,0},{24,8},{1,17},{9,25},{17,1},{25,9},{2,18},{10... | collective-permute-start | bytes 442376 | tf_op jit(solution)/shard_map/ppermute | solution.py:70
  168.6 7.0 %collective-permute-done.35 = bf16[2,96,512]{2,1,0:T(8,128)(2,1)S(1)} collective-permute-done((bf16[2,96,512]{2,1,0:T(8,128)(2,1)S(1)}, bf16[2,96,512]{2,1,0:T(8,128)(2,1)S(1)}, u32[]{:S(2)}, u32[]{:S(2)}) %collective-permute-start.35) | collective-permute-done | bytes 196640 | tf_op jit(solution)/shard_map/ppermute | solution.py:70
  175.8 1.0 collective-permute-start.40
  176.8 1.8 collective-permute-start.41
  178.7 1.6 collective-permute-start.42
  180.3 1.0 collective-permute-done.40
  181.3 4.3 %collective-permute-done.41 = bf16[96,384]{1,0:T(8,128)(2,1)S(1)} collective-permute-done((bf16[96,384]{1,0:T(8,128)(2,1)S(1)}, bf16[96,384]{1,0:T(8,128)(2,1)S(1)}, u32[]{:S(2)}, u32[]{:S(2)}) %collective-permute-start.41) | collective-permute-done | bytes 73760 | tf_op jit(solution)/shard_map/ppermute | solution.py:70
  185.8 4.6 %down.2.refs_0_ = f32[96,1024]{1,0:T(8,128)S(1)} custom-call(s32[8]{0:T(128)S(1)} %add_add_fusion.table, bf16[8,96,512]{2,1,0:T(8,128)(2,1)S(1)} %bitcast.158, bf16[7168,1024]{1,0:T(8,128)(2,1)} %refs_2_.1), custom_call_target="tpu_custom_call" | custom-call | flops 805306368 | bytes 8388608 | tf_op jit(solution)/shard_map/down/pallas_call | solution.py:391
  190.5 4.1 %down.3 = bf16[4,3,8,1024]{3,2,1,0:T(8,128)(2,1)S(1)} custom-call(s32[8]{0:T(128)S(1)} %fusion.40.table, f32[96,1024]{1,0:T(8,128)S(1)} %down.2.refs_0_, bf16[8,96,384]{2,1,0:T(8,128)(2,1)S(1)} %bitcast.159, bf16[7168,1024]{1,0:T(8,128)(2,1)} %refs_2_.1), custom_call_target="tpu_custom_call" | custom-call | flops 603979776 | bytes 6291456 | tf_op jit(solution)/shard_map/down/pallas_call | solution.py:391
  194.8 1.2 collective-permute-start.45
  196.0 2.2 %collective-permute-start.46 = (bf16[3,8,1024]{2,1,0:T(8,128)(2,1)S(1)}, bf16[3,8,1024]{2,1,0:T(8,128)(2,1)S(1)}, u32[]{:S(2)}, u32[]{:S(2)}) collective-permute-start(bf16[3,8,1024]{2,1,0:T(8,128)(2,1)S(1)} %get-tuple-element.62), channel_id=1, source_target_pairs={{0,3},{1,2},{2,1},{3,0},{4,7},{5,6},{6,5},{7,4},{8,11},{9,10},{10,... | collective-permute-start | bytes 147464 | tf_op jit(solution)/shard_map/ppermute | solution.py:70
  198.9 2.1 %collective-permute-done.46 = bf16[3,8,1024]{2,1,0:T(8,128)(2,1)S(1)} collective-permute-done((bf16[3,8,1024]{2,1,0:T(8,128)(2,1)S(1)}, bf16[3,8,1024]{2,1,0:T(8,128)(2,1)S(1)}, u32[]{:S(2)}, u32[]{:S(2)}) %collective-permute-start.46) | collective-permute-done | bytes 49184 | tf_op jit(solution)/shard_map/ppermute | solution.py:70
  201.0 1.5 fusion.29
  (135 shorter events, 12.7 us)
Async XLA Ops:
  0.6 7.7 %collective-permute-start = (bf16[3,8,1024]{2,1,0:T(8,128)(2,1)}, bf16[3,8,1024]{2,1,0:T(8,128)(2,1)S(1)}, u32[]{:S(2)}, u32[]{:S(2)}) collective-permute-start(bf16[3,8,1024]{2,1,0:T(8,128)(2,1)} %param.14), channel_id=1, source_target_pairs={{0,1},{1,0},{2,3},{3,2},{4,5},{5,4},{6,7},{7,6},{8,9},{9,8},{10,11... | collective-permute-start | bytes 147464 | tf_op jit(solution)/shard_map/ppermute | solution.py:70
  3.6 4.7 %collective-permute-start.1 = (bf16[3,8,1024]{2,1,0:T(8,128)(2,1)}, bf16[3,8,1024]{2,1,0:T(8,128)(2,1)S(1)}, u32[]{:S(2)}, u32[]{:S(2)}) collective-permute-start(bf16[3,8,1024]{2,1,0:T(8,128)(2,1)} %param.14), channel_id=1, source_target_pairs={{0,2},{1,3},{2,0},{3,1},{4,6},{5,7},{6,4},{7,5},{8,10},{9,11},{10,... | collective-permute-start | bytes 147464 | tf_op jit(solution)/shard_map/ppermute | solution.py:70
  5.2 5.2 %collective-permute-start.2 = (bf16[3,8,1024]{2,1,0:T(8,128)(2,1)}, bf16[3,8,1024]{2,1,0:T(8,128)(2,1)S(1)}, u32[]{:S(2)}, u32[]{:S(2)}) collective-permute-start(bf16[3,8,1024]{2,1,0:T(8,128)(2,1)} %param.14), channel_id=1, source_target_pairs={{0,3},{1,2},{2,1},{3,0},{4,7},{5,6},{6,5},{7,4},{8,11},{9,10},{10,... | collective-permute-start | bytes 147464 | tf_op jit(solution)/shard_map/ppermute | solution.py:70
  11.2 1.6 copy-start.2
  12.8 1.6 copy-start.3
  14.4 0.6 copy-start.5
  15.0 15.4 %copy-start.8 = (f32[1024]{0:T(1024)S(1)}, f32[1024]{0:T(1024)}, u32[]{:S(2)}) copy-start(f32[1024]{0:T(1024)} %param.15) | copy-start | bytes 12292
  15.0 15.6 %copy-start.6 = (s32[3]{0:T(128)S(1)}, s32[3]{0:T(128)}, u32[]{:S(2)}) copy-start(s32[3]{0:T(128)} %pad_add_fusion.ids) | copy-start | bytes 40
  17.3 13.2 %collective-permute-start.7 = (bf16[1,2,512,512]{3,2,1,0:T(8,128)(2,1)}, bf16[1,2,512,512]{3,2,1,0:T(8,128)(2,1)S(1)}, u32[]{:S(2)}, u32[]{:S(2)}) collective-permute-start(bf16[1,2,512,512]{3,2,1,0:T(8,128)(2,1)} %get-tuple-element.31), channel_id=1, source_target_pairs={{0,4},{4,0},{1,5},{5,1},{2,6},{6,2},{3,7},{7,3},{8,12},{12,8},{9,1... | collective-permute-start | bytes 3145736 | tf_op jit(solution)/shard_map/ppermute | solution.py:70
  17.4 13.2 %collective-permute-start.8 = (bf16[8,2,64,512]{3,2,1,0:T(8,128)(2,1)}, bf16[8,2,64,512]{3,2,1,0:T(8,128)(2,1)}, u32[]{:S(2)}, u32[]{:S(2)}) collective-permute-start(bf16[8,2,64,512]{3,2,1,0:T(8,128)(2,1)} %get-tuple-element.33), channel_id=1, source_target_pairs={{0,4},{4,0},{1,5},{5,1},{2,6},{6,2},{3,7},{7,3},{8,12},{12,8},{9,1... | collective-permute-start | bytes 3145736 | tf_op jit(solution)/shard_map/ppermute | solution.py:70
  18.0 2.7 %collective-permute-start.3 = (f32[16,128]{1,0:T(8,128)S(1)}, f32[16,128]{1,0:T(8,128)S(1)}, u32[]{:S(2)}, u32[]{:S(2)}) collective-permute-start(f32[16,128]{1,0:T(8,128)S(1)} %pad.7), channel_id=1, source_target_pairs={{0,4},{4,0},{1,5},{5,1},{2,6},{6,2},{3,7},{7,3},{8,12},{12,8},{9,1... | collective-permute-start | bytes 24584 | tf_op jit(solution)/shard_map/ppermute | solution.py:70
  20.8 5.2 %collective-permute-start.4 = (f32[16,128]{1,0:T(8,128)S(1)}, f32[16,128]{1,0:T(8,128)S(1)}, u32[]{:S(2)}, u32[]{:S(2)}) collective-permute-start(f32[16,128]{1,0:T(8,128)S(1)} %pad_add_fusion.2), channel_id=1, source_target_pairs={{0,8},{8,0},{16,24},{24,16},{1,9},{9,1},{17,25},{25,17},{2,10},{10... | collective-permute-start | bytes 24584 | tf_op jit(solution)/shard_map/ppermute | solution.py:70
  22.3 4.5 %collective-permute-start.5 = (f32[16,128]{1,0:T(8,128)S(1)}, f32[16,128]{1,0:T(8,128)S(1)}, u32[]{:S(2)}, u32[]{:S(2)}) collective-permute-start(f32[16,128]{1,0:T(8,128)S(1)} %pad_add_fusion.2), channel_id=1, source_target_pairs={{0,16},{8,24},{16,0},{24,8},{1,17},{9,25},{17,1},{25,9},{2,18},{10... | collective-permute-start | bytes 24584 | tf_op jit(solution)/shard_map/ppermute | solution.py:70
  24.9 5.4 %collective-permute-start.6 = (f32[16,128]{1,0:T(8,128)S(1)}, f32[16,128]{1,0:T(8,128)S(1)}, u32[]{:S(2)}, u32[]{:S(2)}) collective-permute-start(f32[16,128]{1,0:T(8,128)S(1)} %pad_add_fusion.2), channel_id=1, source_target_pairs={{0,24},{8,16},{16,8},{24,0},{1,25},{9,17},{17,9},{25,1},{2,26},{10... | collective-permute-start | bytes 24584 | tf_op jit(solution)/shard_map/ppermute | solution.py:70
  30.6 2.5 %copy-start = (bf16[1024,2560]{1,0:T(8,128)(2,1)S(1)}, bf16[1024,2560]{1,0:T(8,128)(2,1)}, u32[]{:S(2)}) copy-start(bf16[1024,2560]{1,0:T(8,128)(2,1)} %w.4) | copy-start | bytes 15728644
  34.8 2.1 %collective-permute-start.9 = (f32[4,4,9,8,128]{4,3,2,1,0:T(8,128)S(1)}, f32[4,4,9,8,128]{4,3,2,1,0:T(8,128)S(1)}, u32[]{:S(2)}, u32[]{:S(2)}) collective-permute-start(f32[4,4,9,8,128]{4,3,2,1,0:T(8,128)S(1)} %slice_bitcast_fusion.4), channel_id=1, source_target_pairs={{0,4},{4,0},{1,5},{5,1},{2,6},{6,2},{3,7},{7,3},{8,12},{12,8},{9,1... | collective-permute-start | bytes 1769480 | tf_op jit(solution)/shard_map/ppermute | solution.py:70
  37.0 29.8 %copy-start.4 = (f32[24,2176]{1,0:T(8,128)S(1)}, f32[24,2176]{1,0:T(8,128)}, u32[]{:S(2)}) copy-start(f32[24,2176]{1,0:T(8,128)} %get-tuple-element.40.bias) | copy-start | bytes 626692
  37.0 7.2 %collective-permute-start.10 = (f32[4,9,8,128]{3,2,1,0:T(8,128)S(1)}, f32[4,9,8,128]{3,2,1,0:T(8,128)S(1)}, u32[]{:S(2)}, u32[]{:S(2)}) collective-permute-start(f32[4,9,8,128]{3,2,1,0:T(8,128)S(1)} %get-tuple-element.58), channel_id=1, source_target_pairs={{0,8},{8,0},{16,24},{24,16},{1,9},{9,1},{17,25},{25,17},{2,10},{10... | collective-permute-start | bytes 442376 | tf_op jit(solution)/shard_map/ppermute | solution.py:70
  37.1 14.0 %collective-permute-start.11 = (f32[4,9,8,128]{3,2,1,0:T(8,128)S(1)}, f32[4,9,8,128]{3,2,1,0:T(8,128)S(1)}, u32[]{:S(2)}, u32[]{:S(2)}) collective-permute-start(f32[4,9,8,128]{3,2,1,0:T(8,128)S(1)} %get-tuple-element.60), channel_id=1, source_target_pairs={{0,16},{8,24},{16,0},{24,8},{1,17},{9,25},{17,1},{25,9},{2,18},{10... | collective-permute-start | bytes 442376 | tf_op jit(solution)/shard_map/ppermute | solution.py:70
  37.9 13.2 %collective-permute-start.12 = (f32[4,9,8,128]{3,2,1,0:T(8,128)S(1)}, f32[4,9,8,128]{3,2,1,0:T(8,128)S(1)}, u32[]{:S(2)}, u32[]{:S(2)}) collective-permute-start(f32[4,9,8,128]{3,2,1,0:T(8,128)S(1)} %get-tuple-element.59), channel_id=1, source_target_pairs={{0,24},{8,16},{16,8},{24,0},{1,25},{9,17},{17,9},{25,1},{2,26},{10... | collective-permute-start | bytes 442376 | tf_op jit(solution)/shard_map/ppermute | solution.py:70
  51.2 3.8 %collective-permute-start.13 = (bf16[9,8,128]{2,1,0:T(8,128)(2,1)S(1)}, bf16[9,8,128]{2,1,0:T(8,128)(2,1)S(1)}, u32[]{:S(2)}, u32[]{:S(2)}) collective-permute-start(bf16[9,8,128]{2,1,0:T(8,128)(2,1)S(1)} %get-tuple-element.71), channel_id=1, source_target_pairs={{0,1},{1,0},{2,3},{3,2},{4,5},{5,4},{6,7},{7,6},{8,9},{9,8},{10,11... | collective-permute-start | bytes 55304 | tf_op jit(solution)/shard_map/ppermute | solution.py:70
  51.8 3.8 %collective-permute-start.14 = (bf16[9,8,128]{2,1,0:T(8,128)(2,1)S(1)}, bf16[9,8,128]{2,1,0:T(8,128)(2,1)S(1)}, u32[]{:S(2)}, u32[]{:S(2)}) collective-permute-start(bf16[9,8,128]{2,1,0:T(8,128)(2,1)S(1)} %get-tuple-element.70), channel_id=1, source_target_pairs={{0,2},{1,3},{2,0},{3,1},{4,6},{5,7},{6,4},{7,5},{8,10},{9,11},{10,... | collective-permute-start | bytes 55304 | tf_op jit(solution)/shard_map/ppermute | solution.py:70
  52.7 4.7 %collective-permute-start.15 = (bf16[9,8,128]{2,1,0:T(8,128)(2,1)S(1)}, bf16[9,8,128]{2,1,0:T(8,128)(2,1)S(1)}, u32[]{:S(2)}, u32[]{:S(2)}) collective-permute-start(bf16[9,8,128]{2,1,0:T(8,128)(2,1)S(1)} %get-tuple-element.69), channel_id=1, source_target_pairs={{0,3},{1,2},{2,1},{3,0},{4,7},{5,6},{6,5},{7,4},{8,11},{9,10},{10,... | collective-permute-start | bytes 55304 | tf_op jit(solution)/shard_map/ppermute | solution.py:70
  57.4 6.8 %collective-permute-start.16 = (bf16[4,9,8,128]{3,2,1,0:T(8,128)(2,1)S(1)}, bf16[4,9,8,128]{3,2,1,0:T(8,128)(2,1)S(1)}, u32[]{:S(2)}, u32[]{:S(2)}) collective-permute-start(bf16[4,9,8,128]{3,2,1,0:T(8,128)(2,1)S(1)} %get-tuple-element.67), channel_id=1, source_target_pairs={{0,8},{8,0},{16,24},{24,16},{1,9},{9,1},{17,25},{25,17},{2,10},{10... | collective-permute-start | bytes 221192 | tf_op jit(solution)/shard_map/ppermute | solution.py:70
  60.4 6.3 %collective-permute-start.17 = (bf16[4,9,8,128]{3,2,1,0:T(8,128)(2,1)S(1)}, bf16[4,9,8,128]{3,2,1,0:T(8,128)(2,1)S(1)}, u32[]{:S(2)}, u32[]{:S(2)}) collective-permute-start(bf16[4,9,8,128]{3,2,1,0:T(8,128)(2,1)S(1)} %get-tuple-element.67), channel_id=1, source_target_pairs={{0,16},{8,24},{16,0},{24,8},{1,17},{9,25},{17,1},{25,9},{2,18},{10... | collective-permute-start | bytes 221192 | tf_op jit(solution)/shard_map/ppermute | solution.py:70
  60.4 6.3 %collective-permute-start.18 = (bf16[4,9,8,128]{3,2,1,0:T(8,128)(2,1)S(1)}, bf16[4,9,8,128]{3,2,1,0:T(8,128)(2,1)S(1)}, u32[]{:S(2)}, u32[]{:S(2)}) collective-permute-start(bf16[4,9,8,128]{3,2,1,0:T(8,128)(2,1)S(1)} %get-tuple-element.67), channel_id=1, source_target_pairs={{0,24},{8,16},{16,8},{24,0},{1,25},{9,17},{17,9},{25,1},{2,26},{10... | collective-permute-start | bytes 221192 | tf_op jit(solution)/shard_map/ppermute | solution.py:70
  66.8 28.5 %copy-start.1 = (bf16[2048,1024]{1,0:T(8,128)(2,1)S(1)}, bf16[2048,1024]{1,0:T(8,128)(2,1)}, u32[]{:S(2)}) copy-start(bf16[2048,1024]{1,0:T(8,128)(2,1)} %w.5) | copy-start | bytes 12582916
  86.0 4.5 %collective-permute-start.19 = (bf16[4,6,8,128]{3,2,1,0:T(8,128)(2,1)S(1)}, bf16[4,6,8,128]{3,2,1,0:T(8,128)(2,1)S(1)}, u32[]{:S(2)}, u32[]{:S(2)}) collective-permute-start(bf16[4,6,8,128]{3,2,1,0:T(8,128)(2,1)S(1)} %join.1), channel_id=1, source_target_pairs={{0,8},{8,0},{16,24},{24,16},{1,9},{9,1},{17,25},{25,17},{2,10},{10... | collective-permute-start | bytes 147464 | tf_op jit(solution)/shard_map/ppermute | solution.py:70
  86.5 5.0 %collective-permute-start.20 = (bf16[4,6,8,128]{3,2,1,0:T(8,128)(2,1)S(1)}, bf16[4,6,8,128]{3,2,1,0:T(8,128)(2,1)S(1)}, u32[]{:S(2)}, u32[]{:S(2)}) collective-permute-start(bf16[4,6,8,128]{3,2,1,0:T(8,128)(2,1)S(1)} %join.1), channel_id=1, source_target_pairs={{0,16},{8,24},{16,0},{24,8},{1,17},{9,25},{17,1},{25,9},{2,18},{10... | collective-permute-start | bytes 147464 | tf_op jit(solution)/shard_map/ppermute | solution.py:70
  87.7 5.9 %collective-permute-start.21 = (bf16[4,6,8,128]{3,2,1,0:T(8,128)(2,1)S(1)}, bf16[4,6,8,128]{3,2,1,0:T(8,128)(2,1)S(1)}, u32[]{:S(2)}, u32[]{:S(2)}) collective-permute-start(bf16[4,6,8,128]{3,2,1,0:T(8,128)(2,1)S(1)} %join.1), channel_id=1, source_target_pairs={{0,24},{8,16},{16,8},{24,0},{1,25},{9,17},{17,9},{25,1},{2,26},{10... | collective-permute-start | bytes 147464 | tf_op jit(solution)/shard_map/ppermute | solution.py:70
  93.7 1.5 collective-permute-start.22
  96.8 4.9 %collective-permute-start.23 = (bf16[4,3,8,512]{3,2,1,0:T(8,128)(2,1)S(1)}, bf16[4,3,8,512]{3,2,1,0:T(8,128)(2,1)S(1)}, u32[]{:S(2)}, u32[]{:S(2)}) collective-permute-start(bf16[4,3,8,512]{3,2,1,0:T(8,128)(2,1)S(1)} %get-tuple-element.46), channel_id=1, source_target_pairs={{0,1},{1,0},{2,3},{3,2},{4,5},{5,4},{6,7},{7,6},{8,9},{9,8},{10,11... | collective-permute-start | bytes 294920 | tf_op jit(solution)/shard_map/ppermute | solution.py:70
  97.6 5.5 %collective-permute-start.25 = (bf16[4,3,8,512]{3,2,1,0:T(8,128)(2,1)S(1)}, bf16[4,3,8,512]{3,2,1,0:T(8,128)(2,1)S(1)}, u32[]{:S(2)}, u32[]{:S(2)}) collective-permute-start(bf16[4,3,8,512]{3,2,1,0:T(8,128)(2,1)S(1)} %get-tuple-element.47), channel_id=1, source_target_pairs={{0,2},{1,3},{2,0},{3,1},{4,6},{5,7},{6,4},{7,5},{8,10},{9,11},{10,... | collective-permute-start | bytes 294920 | tf_op jit(solution)/shard_map/ppermute | solution.py:70
  101.7 4.7 %collective-permute-start.24 = (bf16[4,3,8,512]{3,2,1,0:T(8,128)(2,1)S(1)}, bf16[4,3,8,512]{3,2,1,0:T(8,128)(2,1)S(1)}, u32[]{:S(2)}, u32[]{:S(2)}) collective-permute-start(bf16[4,3,8,512]{3,2,1,0:T(8,128)(2,1)S(1)} %fusion.13), channel_id=1, source_target_pairs={{0,2},{1,3},{2,0},{3,1},{4,6},{5,7},{6,4},{7,5},{8,10},{9,11},{10,... | collective-permute-start | bytes 294920 | tf_op jit(solution)/shard_map/ppermute | solution.py:70
  103.1 14.5 %copy-start.9 = (f32[1024]{0:T(1024)S(1)}, f32[1024]{0:T(1024)}, u32[]{:S(2)}) copy-start(f32[1024]{0:T(1024)} %param.16) | copy-start | bytes 12292
  103.2 4.7 %collective-permute-start.26 = (bf16[4,3,8,512]{3,2,1,0:T(8,128)(2,1)S(1)}, bf16[4,3,8,512]{3,2,1,0:T(8,128)(2,1)S(1)}, u32[]{:S(2)}, u32[]{:S(2)}) collective-permute-start(bf16[4,3,8,512]{3,2,1,0:T(8,128)(2,1)S(1)} %fusion.12), channel_id=1, source_target_pairs={{0,1},{1,0},{2,3},{3,2},{4,5},{5,4},{6,7},{7,6},{8,9},{9,8},{10,11... | collective-permute-start | bytes 294920 | tf_op jit(solution)/shard_map/ppermute | solution.py:70
  108.1 17.1 %copy-start.7 = (bf16[4,3,8,1024]{3,2,1,0:T(8,128)(2,1)}, bf16[4,3,8,1024]{3,2,1,0:T(8,128)(2,1)S(1)}, u32[]{:S(2)}) copy-start(bf16[4,3,8,1024]{3,2,1,0:T(8,128)(2,1)S(1)} %get-tuple-element.57) | copy-start | bytes 589828
  108.1 1.2 collective-permute-start.27
  109.3 4.4 %collective-permute-start.28 = (f32[16,128]{1,0:T(8,128)S(1)}, f32[16,128]{1,0:T(8,128)S(1)}, u32[]{:S(2)}, u32[]{:S(2)}) collective-permute-start(f32[16,128]{1,0:T(8,128)S(1)} %pad_add_fusion.1), channel_id=1, source_target_pairs={{0,8},{8,0},{16,24},{24,16},{1,9},{9,1},{17,25},{25,17},{2,10},{10... | collective-permute-start | bytes 24584 | tf_op jit(solution)/shard_map/ppermute | solution.py:70
  109.3 4.6 %collective-permute-start.29 = (f32[16,128]{1,0:T(8,128)S(1)}, f32[16,128]{1,0:T(8,128)S(1)}, u32[]{:S(2)}, u32[]{:S(2)}) collective-permute-start(f32[16,128]{1,0:T(8,128)S(1)} %pad_add_fusion.1), channel_id=1, source_target_pairs={{0,16},{8,24},{16,0},{24,8},{1,17},{9,25},{17,1},{25,9},{2,18},{10... | collective-permute-start | bytes 24584 | tf_op jit(solution)/shard_map/ppermute | solution.py:70
  112.2 5.4 %collective-permute-start.30 = (f32[16,128]{1,0:T(8,128)S(1)}, f32[16,128]{1,0:T(8,128)S(1)}, u32[]{:S(2)}, u32[]{:S(2)}) collective-permute-start(f32[16,128]{1,0:T(8,128)S(1)} %pad_add_fusion.1), channel_id=1, source_target_pairs={{0,24},{8,16},{16,8},{24,0},{1,25},{9,17},{17,9},{25,1},{2,26},{10... | collective-permute-start | bytes 24584 | tf_op jit(solution)/shard_map/ppermute | solution.py:70
  113.7 11.6 %collective-permute-start.47 = (bf16[2,3,8,512]{3,2,1,0:T(8,128)(2,1)S(1)}, bf16[2,3,8,512]{3,2,1,0:T(8,128)(2,1)S(1)}, u32[]{:S(2)}, u32[]{:S(2)}) collective-permute-start(bf16[2,3,8,512]{3,2,1,0:T(8,128)(2,1)S(1)} %get-tuple-element.51), channel_id=1, source_target_pairs={{0,4},{4,0},{1,5},{5,1},{2,6},{6,2},{3,7},{7,3},{8,12},{12,8},{9,1... | collective-permute-start | bytes 147464 | tf_op jit(solution)/shard_map/ppermute | solution.py:70
  125.2 2.5 %collective-permute-start.31 = (bf16[4,2,96,512]{3,2,1,0:T(8,128)(2,1)S(1)}, bf16[4,2,96,512]{3,2,1,0:T(8,128)(2,1)}, u32[]{:S(2)}, u32[]{:S(2)}) collective-permute-start(bf16[4,2,96,512]{3,2,1,0:T(8,128)(2,1)S(1)} %slice_bitcast_fusion), channel_id=1, source_target_pairs={{0,4},{4,0},{1,5},{5,1},{2,6},{6,2},{3,7},{7,3},{8,12},{12,8},{9,1... | collective-permute-start | bytes 2359304 | tf_op jit(solution)/shard_map/ppermute | solution.py:70
  135.3 12.3 %collective-permute-start.37 = (bf16[4,2,96,384]{3,2,1,0:T(8,128)(2,1)S(1)}, bf16[4,2,96,384]{3,2,1,0:T(8,128)(2,1)S(1)}, u32[]{:S(2)}, u32[]{:S(2)}) collective-permute-start(bf16[4,2,96,384]{3,2,1,0:T(8,128)(2,1)S(1)} %slice_bitcast_fusion.2), channel_id=1, source_target_pairs={{0,4},{4,0},{1,5},{5,1},{2,6},{6,2},{3,7},{7,3},{8,12},{12,8},{9,1... | collective-permute-start | bytes 1769480 | tf_op jit(solution)/shard_map/ppermute | solution.py:70
  135.6 11.5 %collective-permute-start.32 = (bf16[2,2,96,512]{3,2,1,0:T(8,128)(2,1)S(1)}, bf16[2,2,96,512]{3,2,1,0:T(8,128)(2,1)S(1)}, u32[]{:S(2)}, u32[]{:S(2)}) collective-permute-start(bf16[2,2,96,512]{3,2,1,0:T(8,128)(2,1)S(1)} %slice.135), channel_id=1, source_target_pairs={{0,8},{8,0},{16,24},{24,16},{1,9},{9,1},{17,25},{25,17},{2,10},{10... | collective-permute-start | bytes 1179656 | tf_op jit(solution)/shard_map/ppermute | solution.py:70
  147.1 11.6 %collective-permute-start.33 = (bf16[1,2,96,512]{3,2,1,0:T(8,128)(2,1)S(1)}, bf16[1,2,96,512]{3,2,1,0:T(8,128)(2,1)S(1)}, u32[]{:S(2)}, u32[]{:S(2)}) collective-permute-start(bf16[1,2,96,512]{3,2,1,0:T(8,128)(2,1)S(1)} %slice.178), channel_id=1, source_target_pairs={{0,16},{8,24},{16,0},{24,8},{1,17},{9,25},{17,1},{25,9},{2,18},{10... | collective-permute-start | bytes 589832 | tf_op jit(solution)/shard_map/ppermute | solution.py:70
  147.8 17.8 %collective-permute-start.38 = (bf16[2,2,96,384]{3,2,1,0:T(8,128)(2,1)S(1)}, bf16[2,2,96,384]{3,2,1,0:T(8,128)(2,1)S(1)}, u32[]{:S(2)}, u32[]{:S(2)}) collective-permute-start(bf16[2,2,96,384]{3,2,1,0:T(8,128)(2,1)S(1)} %slice.141), channel_id=1, source_target_pairs={{0,8},{8,0},{16,24},{24,16},{1,9},{9,1},{17,25},{25,17},{2,10},{10... | collective-permute-start | bytes 884744 | tf_op jit(solution)/shard_map/ppermute | solution.py:70
  158.9 6.6 %collective-permute-start.34 = (bf16[1,96,512]{2,1,0:T(8,128)(2,1)S(1)}, bf16[1,96,512]{2,1,0:T(8,128)(2,1)S(1)}, u32[]{:S(2)}, u32[]{:S(2)}) collective-permute-start(bf16[1,96,512]{2,1,0:T(8,128)(2,1)S(1)} %fusion.11), channel_id=1, source_target_pairs={{0,16},{8,24},{16,0},{24,8},{1,17},{9,25},{17,1},{25,9},{2,18},{10... | collective-permute-start | bytes 294920 | tf_op jit(solution)/shard_map/ppermute | solution.py:70
  165.5 10.0 %collective-permute-start.35 = (bf16[2,96,512]{2,1,0:T(8,128)(2,1)S(1)}, bf16[2,96,512]{2,1,0:T(8,128)(2,1)S(1)}, u32[]{:S(2)}, u32[]{:S(2)}) collective-permute-start(bf16[2,96,512]{2,1,0:T(8,128)(2,1)S(1)} %pad_maximum_fusion.5), channel_id=1, source_target_pairs={{0,8},{8,0},{16,24},{24,16},{1,9},{9,1},{17,25},{25,17},{2,10},{10... | collective-permute-start | bytes 589832 | tf_op jit(solution)/shard_map/ppermute | solution.py:70
  165.7 10.0 %collective-permute-start.39 = (bf16[1,2,96,384]{3,2,1,0:T(8,128)(2,1)S(1)}, bf16[1,2,96,384]{3,2,1,0:T(8,128)(2,1)S(1)}, u32[]{:S(2)}, u32[]{:S(2)}) collective-permute-start(bf16[1,2,96,384]{3,2,1,0:T(8,128)(2,1)S(1)} %slice.182), channel_id=1, source_target_pairs={{0,16},{8,24},{16,0},{24,8},{1,17},{9,25},{17,1},{25,9},{2,18},{10... | collective-permute-start | bytes 442376 | tf_op jit(solution)/shard_map/ppermute | solution.py:70
  175.6 10.1 %collective-permute-start.36 = (bf16[1,4,96,512]{3,2,1,0:T(8,128)(2,1)S(1)}, bf16[1,4,96,512]{3,2,1,0:T(8,128)(2,1)S(1)}, u32[]{:S(2)}, u32[]{:S(2)}) collective-permute-start(bf16[1,4,96,512]{3,2,1,0:T(8,128)(2,1)S(1)} %maximum_bitcast_fusion), channel_id=1, source_target_pairs={{0,4},{4,0},{1,5},{5,1},{2,6},{6,2},{3,7},{7,3},{8,12},{12,8},{9,1... | collective-permute-start | bytes 1179656 | tf_op jit(solution)/shard_map/ppermute | solution.py:70
  175.8 5.5 %collective-permute-start.40 = (bf16[96,384]{1,0:T(8,128)(2,1)S(1)}, bf16[96,384]{1,0:T(8,128)(2,1)S(1)}, u32[]{:S(2)}, u32[]{:S(2)}) collective-permute-start(bf16[96,384]{1,0:T(8,128)(2,1)S(1)} %fusion.18), channel_id=1, source_target_pairs={{0,8},{8,0},{16,24},{24,16},{1,9},{9,1},{17,25},{25,17},{2,10},{10... | collective-permute-start | bytes 221192 | tf_op jit(solution)/shard_map/ppermute | solution.py:70
  176.8 8.7 %collective-permute-start.41 = (bf16[96,384]{1,0:T(8,128)(2,1)S(1)}, bf16[96,384]{1,0:T(8,128)(2,1)S(1)}, u32[]{:S(2)}, u32[]{:S(2)}) collective-permute-start(bf16[96,384]{1,0:T(8,128)(2,1)S(1)} %fusion.18), channel_id=1, source_target_pairs={{0,16},{8,24},{16,0},{24,8},{1,17},{9,25},{17,1},{25,9},{2,18},{10... | collective-permute-start | bytes 221192 | tf_op jit(solution)/shard_map/ppermute | solution.py:70
  178.7 6.9 %collective-permute-start.42 = (bf16[96,384]{1,0:T(8,128)(2,1)S(1)}, bf16[96,384]{1,0:T(8,128)(2,1)S(1)}, u32[]{:S(2)}, u32[]{:S(2)}) collective-permute-start(bf16[96,384]{1,0:T(8,128)(2,1)S(1)} %fusion.18), channel_id=1, source_target_pairs={{0,24},{8,16},{16,8},{24,0},{1,25},{9,17},{17,9},{25,1},{2,26},{10... | collective-permute-start | bytes 221192 | tf_op jit(solution)/shard_map/ppermute | solution.py:70
  185.6 4.8 %collective-permute-start.43 = (bf16[1,4,96,384]{3,2,1,0:T(8,128)(2,1)S(1)}, bf16[1,4,96,384]{3,2,1,0:T(8,128)(2,1)S(1)}, u32[]{:S(2)}, u32[]{:S(2)}) collective-permute-start(bf16[1,4,96,384]{3,2,1,0:T(8,128)(2,1)S(1)} %maximum_bitcast_fusion.1), channel_id=1, source_target_pairs={{0,4},{4,0},{1,5},{5,1},{2,6},{6,2},{3,7},{7,3},{8,12},{12,8},{9,1... | collective-permute-start | bytes 884744 | tf_op jit(solution)/shard_map/ppermute | solution.py:70
  194.6 4.3 %collective-permute-start.44 = (bf16[3,8,1024]{2,1,0:T(8,128)(2,1)S(1)}, bf16[3,8,1024]{2,1,0:T(8,128)(2,1)S(1)}, u32[]{:S(2)}, u32[]{:S(2)}) collective-permute-start(bf16[3,8,1024]{2,1,0:T(8,128)(2,1)S(1)} %get-tuple-element.61), channel_id=1, source_target_pairs={{0,1},{1,0},{2,3},{3,2},{4,5},{5,4},{6,7},{7,6},{8,9},{9,8},{10,11... | collective-permute-start | bytes 147464 | tf_op jit(solution)/shard_map/ppermute | solution.py:70
  194.8 4.1 %collective-permute-start.45 = (bf16[3,8,1024]{2,1,0:T(8,128)(2,1)S(1)}, bf16[3,8,1024]{2,1,0:T(8,128)(2,1)S(1)}, u32[]{:S(2)}, u32[]{:S(2)}) collective-permute-start(bf16[3,8,1024]{2,1,0:T(8,128)(2,1)S(1)} %get-tuple-element.63), channel_id=1, source_target_pairs={{0,2},{1,3},{2,0},{3,1},{4,6},{5,7},{6,4},{7,5},{8,10},{9,11},{10,... | collective-permute-start | bytes 147464 | tf_op jit(solution)/shard_map/ppermute | solution.py:70
  196.0 5.0 %collective-permute-start.46 = (bf16[3,8,1024]{2,1,0:T(8,128)(2,1)S(1)}, bf16[3,8,1024]{2,1,0:T(8,128)(2,1)S(1)}, u32[]{:S(2)}, u32[]{:S(2)}) collective-permute-start(bf16[3,8,1024]{2,1,0:T(8,128)(2,1)S(1)} %get-tuple-element.62), channel_id=1, source_target_pairs={{0,3},{1,2},{2,1},{3,0},{4,7},{5,6},{6,5},{7,4},{8,11},{9,10},{10,... | collective-permute-start | bytes 147464 | tf_op jit(solution)/shard_map/ppermute | solution.py:70
